TPU v7x, 512 devices: a whole 4x4x16 slice. The times are simulated.
512 devices in a mesh: mem: 32 (over y_hi, z), dp: 16 (over x, y_lo, core).
Axes of the slice: x: 4, y: 4 (y_hi: 2, y_lo: 2; y = y_hi * 2 + y_lo), z: 16, core: 2. Of those that a mesh axis runs over, the one named last changes fastest.
Arguments:
- query_vectors: bfloat16 [65536, 256], P(('mem', 'dp')), may hold values from -2 to 2
- item_vectors: bfloat16 [65536, 256], P(('mem', 'dp')), may hold values from -1.5 to 1.5
- negative_vectors: bfloat16 [32768, 256], P(('mem', 'dp')), may hold values from -1.5 to 1.5
- item_ids: int32 [65536], P(('mem', 'dp')), may hold values from 0 to 65535, as said below
- negative_ids: int32 [32768], P(('mem', 'dp')), may hold values from 0 to 65535, as said below
- negative_counts: int32 [32768], P(('mem', 'dp')), may hold values from 1 to 4
- memory: bfloat16 [16, 32768, 256], P('dp', 'mem'), may hold values from -2 to 2
- owners: int32 [65536, 1], P(('mem', 'dp')), may hold values from 0 to 31, as said below
- memory_slots: int32 [65536], P(('mem', 'dp')), may hold values from 0 to 1023
Outputs:
- query_loss: float32 [65536], P(('mem', 'dp'))
- query_grad: float32 [65536, 256], P(('mem', 'dp'))
- item_grad: float32 [65536, 256], P(('mem', 'dp'))
- negative_grad: float32 [32768, 256], P(('mem', 'dp'))
- new_memory: bfloat16 [16, 32768, 256], P('dp', 'mem')
Inputs may be any that keep to these rules, and one draw needn't show every extreme that they name: `item_ids`: catalogue ids; every binary octave of ids is about equally likely. `negative_ids`: catalogue ids; every binary octave of ids is about equally likely. `owners`: among the 128 items of one device no owner is named more than 8 times; for every dp index one owner is named exactly 8 times by each device with that dp index.
All inputs are finite; a program needn't handle non-finite values.
Results may differ from a plain program's by a relative error of at most 0.003.
Values may be sent and summed in bfloat16 or wider, within the bound.
No kernel may reach another device: no remote copies, remote signals or barrier semaphores. Data moves between devices by JAX's collectives and lax.ppermute only.
A program may use at most 64 MiB of HBM per device.

v0:
```python
import math

import jax
import jax.numpy as jnp
from jax import lax
from jax.sharding import PartitionSpec as P

ITEMS = 65536


def shifted(block, axis, distance):
    devices = range(lax.axis_size(axis))
    route = [((i - distance) % len(devices), i) for i in devices]
    return lax.ppermute(block, axis, route)


def sample_chance(identities):
    return jnp.log1p(1.0 / (identities.astype(jnp.float32) + 1.0)) / math.log(ITEMS + 1)


def inner_products(left, right):
    return lax.dot_general(
        left, right, (((1,), (1,)), ((), ())), preferred_element_type=jnp.float32
    )


def column_sums(weights, vectors):
    return lax.dot_general(
        weights, vectors, (((0,), (0,)), ((), ())), preferred_element_type=jnp.float32
    )


def merge_stats(running, exp_total, logits):
    newest = jnp.maximum(running, jnp.max(logits, axis=1))
    exp_total = exp_total * jnp.exp(running - newest) + jnp.sum(
        jnp.exp(logits - newest[:, None]), axis=1
    )
    return (newest, exp_total)


def place_items(memory_rows, candidates, target_rows, arrival):
    row_count = memory_rows.shape[0]
    entry_count = target_rows.shape[0]
    latest = jnp.full((row_count,), -1, jnp.int32).at[target_rows].max(arrival)
    winners = (arrival >= 0) & (arrival == latest[target_rows])
    positions = jnp.where(winners, jnp.arange(entry_count, dtype=jnp.int32), 0)
    chosen = jnp.zeros((row_count,), jnp.int32).at[target_rows].max(positions)
    fresh_rows = jnp.take(candidates, chosen, axis=0)
    return jnp.where((latest >= 0)[:, None], fresh_rows, memory_rows)


def local(
    query_vectors,
    item_vectors,
    negative_vectors,
    item_ids,
    negative_ids,
    negative_counts,
    memory,
    owners,
    memory_slots,
):
    query_count = query_vectors.shape[0]
    negative_count = negative_vectors.shape[0]
    cycle_size = lax.axis_size("mem")
    group_size = lax.axis_size("dp")
    here_dp = lax.axis_index("dp")
    memory_rows = memory[0]
    group_items, group_negatives, group_item_ids, group_negative_ids, group_counts = (
        lax.all_gather(item_vectors, "dp", axis=0, tiled=True),
        lax.all_gather(negative_vectors, "dp", axis=0, tiled=True),
        lax.all_gather(item_ids, "dp", axis=0, tiled=True),
        lax.all_gather(negative_ids, "dp", axis=0, tiled=True),
        lax.all_gather(negative_counts, "dp", axis=0, tiled=True),
    )
    batch_shift = -jnp.log(query_count * group_size * sample_chance(group_item_ids))
    negative_shift = jnp.log(group_counts.astype(jnp.float32)) - jnp.log(
        negative_count * group_size * sample_chance(group_negative_ids)
    )
    batch_logits = inner_products(query_vectors, group_items) + batch_shift[None, :]
    negative_logits = inner_products(query_vectors, group_negatives) + negative_shift[None, :]
    running = jnp.maximum(jnp.max(batch_logits, axis=1), jnp.max(negative_logits, axis=1))
    exp_total = jnp.sum(jnp.exp(batch_logits - running[:, None]), axis=1) + jnp.sum(
        jnp.exp(negative_logits - running[:, None]), axis=1
    )
    visited = jnp.zeros((1, 1), jnp.bfloat16)

    def stats_turn(cycle_state):
        query_block, running, exp_total, visited = cycle_state
        running, exp_total = merge_stats(
            running, exp_total, inner_products(query_block, memory_rows)
        )
        query_block, running, exp_total = (
            shifted(query_block.astype(jnp.float32), "mem", 1).astype(query_block.dtype),
            shifted(running, "mem", 1),
            shifted(exp_total, "mem", 1),
        )
        return (query_block, running, exp_total, visited)

    def stats_pair(cycle_turn, cycle_state):
        return stats_turn(stats_turn(cycle_state))

    stats_state = lax.fori_loop(
        0, cycle_size // 2, stats_pair, (query_vectors, running, exp_total, visited)
    )
    log_total = stats_state[1] + jnp.log(stats_state[2])
    visited = stats_state[3]
    zero_sums = jnp.zeros(query_vectors.shape, jnp.float32)

    def grad_turn(cycle_state):
        query_block, log_rows, summed = cycle_state
        weights = jnp.exp(inner_products(query_block, memory_rows) - log_rows[:, None]).astype(
            jnp.bfloat16
        )
        summed = summed + jnp.dot(weights, memory_rows, preferred_element_type=jnp.float32)
        return (
            shifted(query_block.astype(jnp.float32), "mem", 1).astype(query_block.dtype),
            shifted(log_rows, "mem", 1),
            shifted(summed, "mem", 1),
        )

    start_state = (query_vectors, log_total, zero_sums)

    def grad_pair(cycle_turn, cycle_state):
        return grad_turn(grad_turn(cycle_state))

    final_state = lax.fori_loop(0, cycle_size // 2, grad_pair, start_state)
    memory_part = final_state[-1]
    batch_weights = jnp.exp(batch_logits - log_total[:, None]).astype(jnp.bfloat16)
    negative_weights = jnp.exp(negative_logits - log_total[:, None]).astype(jnp.bfloat16)
    query_grad = (
        memory_part
        + jnp.dot(batch_weights, group_items, preferred_element_type=jnp.float32)
        + jnp.dot(negative_weights, group_negatives, preferred_element_type=jnp.float32)
        - item_vectors.astype(jnp.float32)
    )
    own_logits = jnp.diagonal(
        lax.dynamic_slice_in_dim(batch_logits, here_dp * query_count, query_count, 1)
    )
    query_loss = log_total - own_logits
    span = query_count + negative_count
    blocks = span * lax.axis_size("dp") // span
    batch_term = column_sums(batch_weights, query_vectors).reshape(blocks, query_count, -1)
    negative_term = column_sums(negative_weights, query_vectors).reshape(blocks, negative_count, -1)
    key_sums = lax.psum_scatter(
        jnp.concatenate([batch_term, negative_term], axis=1).reshape(
            span * lax.axis_size("dp"), -1
        ),
        "dp",
        scatter_dimension=0,
        tiled=True,
    )
    item_grad = key_sums[:query_count] - query_vectors.astype(jnp.float32)
    negative_grad = key_sums[query_count:]
    owner_list = owners[:, 0]
    capacity = max(2, 2 * query_count // cycle_size)
    matches = owner_list[:, None] == jnp.arange(cycle_size, dtype=jnp.int32)[None, :]
    ranks = jnp.cumsum(matches.astype(jnp.int32), axis=0) - 1
    own_rank = jnp.sum(jnp.where(matches, ranks, 0), axis=1)
    target_place = owner_list * capacity + own_rank
    selection = target_place[None, :] == jnp.arange(cycle_size * capacity, dtype=jnp.int32)[:, None]
    filled = jnp.any(selection, axis=1)
    outgoing = jnp.dot(
        selection.astype(jnp.bfloat16), item_vectors, preferred_element_type=jnp.float32
    ).astype(jnp.bfloat16)
    out_slot = jnp.sum(jnp.where(selection, memory_slots[None, :], 0), axis=1)
    row_order = jnp.arange(query_count, dtype=jnp.int32)
    out_row = jnp.where(filled, jnp.sum(jnp.where(selection, row_order[None, :], 0), axis=1), -1)
    details = jnp.stack([out_slot, out_row], axis=1)
    arrived, arrived_details = (
        lax.all_to_all(
            outgoing.reshape(cycle_size, capacity, -1),
            "mem",
            split_axis=0,
            concat_axis=0,
            tiled=True,
        ),
        lax.all_to_all(
            details.reshape(cycle_size, capacity, 2), "mem", split_axis=0, concat_axis=0, tiled=True
        ),
    )
    anchor = jnp.arange(cycle_size, dtype=jnp.int32)[:, None] * query_count
    arrival = jnp.where(
        arrived_details[:, :, 1] >= 0, anchor + arrived_details[:, :, 1], -1
    ).reshape(-1)
    updated = place_items(
        memory_rows,
        arrived.reshape(cycle_size * capacity, -1),
        arrived_details[:, :, 0].reshape(-1),
        arrival,
    )
    return (query_loss, query_grad, item_grad, negative_grad, updated[None])


def solution(mesh):
    placed = (
        P(("mem", "dp"), None),
        P(("mem", "dp"), None),
        P(("mem", "dp"), None),
        P(("mem", "dp")),
        P(("mem", "dp")),
        P(("mem", "dp")),
        P("dp", "mem", None),
        P(("mem", "dp"), None),
        P(("mem", "dp")),
    )
    return jax.shard_map(
        local,
        mesh=mesh,
        in_specs=placed,
        out_specs=(
            P(("mem", "dp")),
            P(("mem", "dp"), None),
            P(("mem", "dp"), None),
            P(("mem", "dp"), None),
            P("dp", "mem", None),
        ),
        check_vma=False,
    )
```

profile of v0, /device:TPU:6, one launch (start us, length us, event | category | flops | bytes accessed | tf_op | source)
XLA Modules:
  0.0 964.8 jit_solution(11051648405174071873)
XLA Ops:
  12.1 18.1 %all-to-all-start = ((s32[32,8,2]{1,2,0:T(2,128)}), s32[32,8,2]{1,2,0:T(2,128)S(1)}, u32[]{:S(2)}, u32[]{:S(2)}) async-start(s32[32,8,2]{1,2,0:T(2,128)} %copy.19), calls=%async_computation.1 | async-start | bytes 65536 | tf_op jit(solution)/shard_map/all_to_all | solution.py:178
  31.9 15.4 %all-gather = s32[16,1,128]{2,1,0:T(1,128)S(1)} all-gather(s32[1,1,128]{2,1,0:T(1,128)} %bitcast.75), channel_id=1, replica_groups=mesh['mem'=32,'dp'=16] {'dp'}, dimensions={0}, use_global_device_ids=true | all-gather | bytes 8704 | tf_op jit(solution)/shard_map/all_gather | solution.py:72
  47.3 18.0 %all_gather.17 = bf16[1024,256]{1,0:T(8,128)(2,1)S(1)} all-gather(bf16[64,256]{1,0:T(8,128)(2,1)} %param.15), channel_id=1, replica_groups=mesh['mem'=32,'dp'=16] {'dp'}, dimensions={0}, use_global_device_ids=true | all-gather | bytes 557056 | tf_op jit(solution)/shard_map/all_gather | solution.py:71
  69.0 13.7 %all-reduce.2 = (s32[1024]{0:T(1024)S(1)}, s32[1024]{0:T(1024)S(1)}) all-reduce(s32[1024]{0:T(1024)S(1)} %dynamic-update-slice.1, s32[1024]{0:T(1024)S(1)} %dynamic-update-slice), channel_id=1, replica_groups=mesh['mem'=32,'dp'=16] {'dp'}, use_global_device_ids=true, to_apply=%add.1 | all-reduce | flops 2048 | bytes 16384
  84.2 15.3 %all-to-all-start.1 = ((bf16[32,8,256]{2,1,0:T(8,128)(2,1)}), bf16[32,8,256]{2,1,0:T(8,128)(2,1)S(1)}, u32[]{:S(2)}, u32[]{:S(2)}) async-start(bf16[32,8,256]{2,1,0:T(8,128)(2,1)} %fusion.15), calls=%async_computation.2 | async-start | bytes 262144 | tf_op jit(solution)/shard_map/all_to_all | solution.py:171
  105.9 10.6 %all-to-all-done.1 = bf16[32,8,256]{2,1,0:T(8,128)(2,1)S(1)} async-done(((bf16[32,8,256]{2,1,0:T(8,128)(2,1)}), bf16[32,8,256]{2,1,0:T(8,128)(2,1)S(1)}, u32[]{:S(2)}, u32[]{:S(2)}) %all-to-all-start.1) | async-done | bytes 131104 | tf_op jit(solution)/shard_map/all_to_all | solution.py:171
  116.5 3.9 gather_fusion.2
  125.2 393.2 %while.28 = (s32[]{:T(128)}, bf16[128,256]{1,0:T(8,128)(2,1)S(1)}, f32[128]{0:T(128)S(1)}, f32[128]{0:T(128)S(1)}, bf16[1024,256]{1,0:T(8,128)(2,1)S(1)}, /*index=5*/s32[]{:T(128)}) while((s32[]{:T(128)}, bf16[128,256]{1,0:T(8,128)(2,1)S(1)}, f32[128]{0:T(128)S(1)}, f32[128]{0:T(128)S(1)}, bf16[1024,256]{1,0:T(8,128)(2,1)S(1)}, ...), condition=%wide.region_9.0_spmd, body=%wide.region_4.0_spmd.sunk | while | flops 135004672 | bytes 3820853 | solution.py:103
  146.4 4.1 collective-permute-done.5
  157.0 3.3 collective-permute-done
  170.9 4.1 collective-permute-done.5
  181.5 3.4 collective-permute-done
  195.5 4.1 collective-permute-done.5
  206.0 3.6 collective-permute-done
  220.0 4.1 collective-permute-done.5
  230.5 3.3 collective-permute-done
  244.5 4.1 collective-permute-done.5
  269.0 4.1 collective-permute-done.5
  293.6 4.1 collective-permute-done.5
  318.1 4.1 collective-permute-done.5
  342.6 4.1 collective-permute-done.5
  367.1 4.1 collective-permute-done.5
  391.7 4.1 collective-permute-done.5
  416.2 4.1 collective-permute-done.5
  426.7 3.3 collective-permute-done
  440.7 4.1 collective-permute-done.5
  451.2 4.0 collective-permute-done
  465.2 4.1 collective-permute-done.5
  489.7 4.1 collective-permute-done.5
  500.3 3.9 collective-permute-done
  514.3 4.1 collective-permute-done.5
  522.7 429.6 %while.29 = (s32[]{:T(128)}, bf16[128,256]{1,0:T(8,128)(2,1)S(1)}, f32[128]{0:T(128)S(1)}, f32[128,256]{1,0:T(8,128)S(1)}, bf16[1024,256]{1,0:T(8,128)(2,1)S(1)}, /*index=5*/s32[]{:T(128)}) while((s32[]{:T(128)}, bf16[128,256]{1,0:T(8,128)(2,1)S(1)}, f32[128]{0:T(128)S(1)}, f32[128,256]{1,0:T(8,128)S(1)}, bf16[1024,256]{1,0:T(8,128)(2,1)S(1)}, ...), condition=%wide.region_11.0_spmd, body=%wide.region_10.0_spmd.sunk | while | flops 269025280 | bytes 3282229 | solution.py:127
  529.0 7.1 collective-permute-done.8
  542.4 7.1 collective-permute-done.9
  555.8 7.1 collective-permute-done.8
  569.2 7.1 collective-permute-done.9
  582.7 7.2 collective-permute-done.8
  596.1 7.2 collective-permute-done.9
  609.6 7.2 collective-permute-done.8
  623.1 7.1 collective-permute-done.9
  636.5 7.1 collective-permute-done.8
  649.9 7.1 collective-permute-done.9
  663.3 7.1 collective-permute-done.8
  676.8 7.1 collective-permute-done.9
  690.2 7.1 collective-permute-done.8
  703.6 7.1 collective-permute-done.9
  717.0 7.1 collective-permute-done.8
  730.4 7.1 collective-permute-done.9
  743.8 7.1 collective-permute-done.8
  757.3 7.2 collective-permute-done.9
  770.7 7.2 collective-permute-done.8
  784.2 7.1 collective-permute-done.9
  797.6 7.1 collective-permute-done.8
  811.1 7.1 collective-permute-done.9
  824.5 7.1 collective-permute-done.8
  837.9 7.1 collective-permute-done.9
  851.3 7.1 collective-permute-done.8
  864.7 7.1 collective-permute-done.9
  878.1 7.1 collective-permute-done.8
  891.5 7.1 collective-permute-done.9
  905.0 7.1 collective-permute-done.8
  918.4 7.1 collective-permute-done.9
  931.8 7.1 collective-permute-done.8
  945.2 7.1 collective-permute-done.9
  (563 shorter events, 533.6 us)
Async XLA Ops:
  7.2 114.4 %all-gather.3.cloned.1.call-start = ((), (), s32[]{:S(2)}) async-start(), calls=%async_computation.3 | async-start | bytes 1114112 | tf_op jit(solution)/shard_map/all_gather | solution.py:70
  12.1 72.1 %all-to-all-start = ((s32[32,8,2]{1,2,0:T(2,128)}), s32[32,8,2]{1,2,0:T(2,128)S(1)}, u32[]{:S(2)}, u32[]{:S(2)}) async-start(s32[32,8,2]{1,2,0:T(2,128)} %copy.19), calls=%async_computation.1 | async-start | bytes 65536 | tf_op jit(solution)/shard_map/all_to_all | solution.py:178
  84.2 32.3 %all-to-all-start.1 = ((bf16[32,8,256]{2,1,0:T(8,128)(2,1)}), bf16[32,8,256]{2,1,0:T(8,128)(2,1)S(1)}, u32[]{:S(2)}, u32[]{:S(2)}) async-start(bf16[32,8,256]{2,1,0:T(8,128)(2,1)} %fusion.15), calls=%async_computation.2 | async-start | bytes 262144 | tf_op jit(solution)/shard_map/all_to_all | solution.py:171
  99.4 855.5 %reduce-scatter.2.cloned.1.call-start = ((), (), s32[]{:S(2)}) async-start(), calls=%async_computation.4 | async-start | bytes 3342336 | tf_op jit(solution)/shard_map/reduce_scatter | solution.py:145
  139.5 11.0 %collective-permute-start.1 = (bf16[128,256]{1,0:T(8,128)(2,1)S(1)}, bf16[128,256]{1,0:T(8,128)(2,1)S(1)}, u32[]{:S(2)}, u32[]{:S(2)}) collective-permute-start(bf16[128,256]{1,0:T(8,128)(2,1)S(1)} %collective-permute-done), channel_id=1, source_target_pairs={{496,0},{0,16},{16,32},{32,48},{48,64},{64,80},{80,96},{96,112},{1... | collective-permute-start | bytes 196616 | tf_op jit(solution)/shard_map/while/body/eval_jaxpr/ppermute | solution.py:14
  164.1 11.0 %collective-permute-start.1 = (bf16[128,256]{1,0:T(8,128)(2,1)S(1)}, bf16[128,256]{1,0:T(8,128)(2,1)S(1)}, u32[]{:S(2)}, u32[]{:S(2)}) collective-permute-start(bf16[128,256]{1,0:T(8,128)(2,1)S(1)} %collective-permute-done), channel_id=1, source_target_pairs={{496,0},{0,16},{16,32},{32,48},{48,64},{64,80},{80,96},{96,112},{1... | collective-permute-start | bytes 196616 | tf_op jit(solution)/shard_map/while/body/eval_jaxpr/ppermute | solution.py:14
  188.6 11.0 %collective-permute-start.1 = (bf16[128,256]{1,0:T(8,128)(2,1)S(1)}, bf16[128,256]{1,0:T(8,128)(2,1)S(1)}, u32[]{:S(2)}, u32[]{:S(2)}) collective-permute-start(bf16[128,256]{1,0:T(8,128)(2,1)S(1)} %collective-permute-done), channel_id=1, source_target_pairs={{496,0},{0,16},{16,32},{32,48},{48,64},{64,80},{80,96},{96,112},{1... | collective-permute-start | bytes 196616 | tf_op jit(solution)/shard_map/while/body/eval_jaxpr/ppermute | solution.py:14
  213.1 11.0 %collective-permute-start.1 = (bf16[128,256]{1,0:T(8,128)(2,1)S(1)}, bf16[128,256]{1,0:T(8,128)(2,1)S(1)}, u32[]{:S(2)}, u32[]{:S(2)}) collective-permute-start(bf16[128,256]{1,0:T(8,128)(2,1)S(1)} %collective-permute-done), channel_id=1, source_target_pairs={{496,0},{0,16},{16,32},{32,48},{48,64},{64,80},{80,96},{96,112},{1... | collective-permute-start | bytes 196616 | tf_op jit(solution)/shard_map/while/body/eval_jaxpr/ppermute | solution.py:14
  237.6 11.0 %collective-permute-start.1 = (bf16[128,256]{1,0:T(8,128)(2,1)S(1)}, bf16[128,256]{1,0:T(8,128)(2,1)S(1)}, u32[]{:S(2)}, u32[]{:S(2)}) collective-permute-start(bf16[128,256]{1,0:T(8,128)(2,1)S(1)} %collective-permute-done), channel_id=1, source_target_pairs={{496,0},{0,16},{16,32},{32,48},{48,64},{64,80},{80,96},{96,112},{1... | collective-permute-start | bytes 196616 | tf_op jit(solution)/shard_map/while/body/eval_jaxpr/ppermute | solution.py:14
  262.2 11.0 %collective-permute-start.1 = (bf16[128,256]{1,0:T(8,128)(2,1)S(1)}, bf16[128,256]{1,0:T(8,128)(2,1)S(1)}, u32[]{:S(2)}, u32[]{:S(2)}) collective-permute-start(bf16[128,256]{1,0:T(8,128)(2,1)S(1)} %collective-permute-done), channel_id=1, source_target_pairs={{496,0},{0,16},{16,32},{32,48},{48,64},{64,80},{80,96},{96,112},{1... | collective-permute-start | bytes 196616 | tf_op jit(solution)/shard_map/while/body/eval_jaxpr/ppermute | solution.py:14
  286.7 11.0 %collective-permute-start.1 = (bf16[128,256]{1,0:T(8,128)(2,1)S(1)}, bf16[128,256]{1,0:T(8,128)(2,1)S(1)}, u32[]{:S(2)}, u32[]{:S(2)}) collective-permute-start(bf16[128,256]{1,0:T(8,128)(2,1)S(1)} %collective-permute-done), channel_id=1, source_target_pairs={{496,0},{0,16},{16,32},{32,48},{48,64},{64,80},{80,96},{96,112},{1... | collective-permute-start | bytes 196616 | tf_op jit(solution)/shard_map/while/body/eval_jaxpr/ppermute | solution.py:14
  311.2 11.0 %collective-permute-start.1 = (bf16[128,256]{1,0:T(8,128)(2,1)S(1)}, bf16[128,256]{1,0:T(8,128)(2,1)S(1)}, u32[]{:S(2)}, u32[]{:S(2)}) collective-permute-start(bf16[128,256]{1,0:T(8,128)(2,1)S(1)} %collective-permute-done), channel_id=1, source_target_pairs={{496,0},{0,16},{16,32},{32,48},{48,64},{64,80},{80,96},{96,112},{1... | collective-permute-start | bytes 196616 | tf_op jit(solution)/shard_map/while/body/eval_jaxpr/ppermute | solution.py:14
  335.7 11.0 %collective-permute-start.1 = (bf16[128,256]{1,0:T(8,128)(2,1)S(1)}, bf16[128,256]{1,0:T(8,128)(2,1)S(1)}, u32[]{:S(2)}, u32[]{:S(2)}) collective-permute-start(bf16[128,256]{1,0:T(8,128)(2,1)S(1)} %collective-permute-done), channel_id=1, source_target_pairs={{496,0},{0,16},{16,32},{32,48},{48,64},{64,80},{80,96},{96,112},{1... | collective-permute-start | bytes 196616 | tf_op jit(solution)/shard_map/while/body/eval_jaxpr/ppermute | solution.py:14
  360.2 11.0 %collective-permute-start.1 = (bf16[128,256]{1,0:T(8,128)(2,1)S(1)}, bf16[128,256]{1,0:T(8,128)(2,1)S(1)}, u32[]{:S(2)}, u32[]{:S(2)}) collective-permute-start(bf16[128,256]{1,0:T(8,128)(2,1)S(1)} %collective-permute-done), channel_id=1, source_target_pairs={{496,0},{0,16},{16,32},{32,48},{48,64},{64,80},{80,96},{96,112},{1... | collective-permute-start | bytes 196616 | tf_op jit(solution)/shard_map/while/body/eval_jaxpr/ppermute | solution.py:14
  384.8 11.0 %collective-permute-start.1 = (bf16[128,256]{1,0:T(8,128)(2,1)S(1)}, bf16[128,256]{1,0:T(8,128)(2,1)S(1)}, u32[]{:S(2)}, u32[]{:S(2)}) collective-permute-start(bf16[128,256]{1,0:T(8,128)(2,1)S(1)} %collective-permute-done), channel_id=1, source_target_pairs={{496,0},{0,16},{16,32},{32,48},{48,64},{64,80},{80,96},{96,112},{1... | collective-permute-start | bytes 196616 | tf_op jit(solution)/shard_map/while/body/eval_jaxpr/ppermute | solution.py:14
  409.3 11.0 %collective-permute-start.1 = (bf16[128,256]{1,0:T(8,128)(2,1)S(1)}, bf16[128,256]{1,0:T(8,128)(2,1)S(1)}, u32[]{:S(2)}, u32[]{:S(2)}) collective-permute-start(bf16[128,256]{1,0:T(8,128)(2,1)S(1)} %collective-permute-done), channel_id=1, source_target_pairs={{496,0},{0,16},{16,32},{32,48},{48,64},{64,80},{80,96},{96,112},{1... | collective-permute-start | bytes 196616 | tf_op jit(solution)/shard_map/while/body/eval_jaxpr/ppermute | solution.py:14
  433.8 11.0 %collective-permute-start.1 = (bf16[128,256]{1,0:T(8,128)(2,1)S(1)}, bf16[128,256]{1,0:T(8,128)(2,1)S(1)}, u32[]{:S(2)}, u32[]{:S(2)}) collective-permute-start(bf16[128,256]{1,0:T(8,128)(2,1)S(1)} %collective-permute-done), channel_id=1, source_target_pairs={{496,0},{0,16},{16,32},{32,48},{48,64},{64,80},{80,96},{96,112},{1... | collective-permute-start | bytes 196616 | tf_op jit(solution)/shard_map/while/body/eval_jaxpr/ppermute | solution.py:14
  458.3 11.0 %collective-permute-start.1 = (bf16[128,256]{1,0:T(8,128)(2,1)S(1)}, bf16[128,256]{1,0:T(8,128)(2,1)S(1)}, u32[]{:S(2)}, u32[]{:S(2)}) collective-permute-start(bf16[128,256]{1,0:T(8,128)(2,1)S(1)} %collective-permute-done), channel_id=1, source_target_pairs={{496,0},{0,16},{16,32},{32,48},{48,64},{64,80},{80,96},{96,112},{1... | collective-permute-start | bytes 196616 | tf_op jit(solution)/shard_map/while/body/eval_jaxpr/ppermute | solution.py:14
  482.9 11.0 %collective-permute-start.1 = (bf16[128,256]{1,0:T(8,128)(2,1)S(1)}, bf16[128,256]{1,0:T(8,128)(2,1)S(1)}, u32[]{:S(2)}, u32[]{:S(2)}) collective-permute-start(bf16[128,256]{1,0:T(8,128)(2,1)S(1)} %collective-permute-done), channel_id=1, source_target_pairs={{496,0},{0,16},{16,32},{32,48},{48,64},{64,80},{80,96},{96,112},{1... | collective-permute-start | bytes 196616 | tf_op jit(solution)/shard_map/while/body/eval_jaxpr/ppermute | solution.py:14
  507.4 11.0 %collective-permute-start.1 = (bf16[128,256]{1,0:T(8,128)(2,1)S(1)}, bf16[128,256]{1,0:T(8,128)(2,1)S(1)}, u32[]{:S(2)}, u32[]{:S(2)}) collective-permute-start(bf16[128,256]{1,0:T(8,128)(2,1)S(1)} %collective-permute-done), channel_id=1, source_target_pairs={{496,0},{0,16},{16,32},{32,48},{48,64},{64,80},{80,96},{96,112},{1... | collective-permute-start | bytes 196616 | tf_op jit(solution)/shard_map/while/body/eval_jaxpr/ppermute | solution.py:14
  523.2 12.9 %collective-permute-start.10 = (f32[128,256]{1,0:T(8,128)S(1)}, f32[128,256]{1,0:T(8,128)S(1)}, u32[]{:S(2)}, u32[]{:S(2)}) collective-permute-start(f32[128,256]{1,0:T(8,128)S(1)} %fusion.79), channel_id=1, source_target_pairs={{496,0},{0,16},{16,32},{32,48},{48,64},{64,80},{80,96},{96,112},{1... | collective-permute-start | bytes 393224 | tf_op jit(solution)/shard_map/while/body/eval_jaxpr/ppermute | solution.py:14
  525.1 11.0 %collective-permute-start.6 = (bf16[128,256]{1,0:T(8,128)(2,1)S(1)}, bf16[128,256]{1,0:T(8,128)(2,1)S(1)}, u32[]{:S(2)}, u32[]{:S(2)}) collective-permute-start(bf16[128,256]{1,0:T(8,128)(2,1)S(1)} %get-tuple-element.194), channel_id=1, source_target_pairs={{496,0},{0,16},{16,32},{32,48},{48,64},{64,80},{80,96},{96,112},{1... | collective-permute-start | bytes 196616 | tf_op jit(solution)/shard_map/while/body/eval_jaxpr/ppermute | solution.py:14
  536.6 12.9 %collective-permute-start.11 = (f32[128,256]{1,0:T(8,128)S(1)}, f32[128,256]{1,0:T(8,128)S(1)}, u32[]{:S(2)}, u32[]{:S(2)}) collective-permute-start(f32[128,256]{1,0:T(8,128)S(1)} %fusion.80), channel_id=1, source_target_pairs={{496,0},{0,16},{16,32},{32,48},{48,64},{64,80},{80,96},{96,112},{1... | collective-permute-start | bytes 393224 | tf_op jit(solution)/shard_map/while/body/eval_jaxpr/ppermute | solution.py:14
  538.5 11.0 %collective-permute-start.7 = (bf16[128,256]{1,0:T(8,128)(2,1)S(1)}, bf16[128,256]{1,0:T(8,128)(2,1)S(1)}, u32[]{:S(2)}, u32[]{:S(2)}) collective-permute-start(bf16[128,256]{1,0:T(8,128)(2,1)S(1)} %collective-permute-done.6), channel_id=1, source_target_pairs={{496,0},{0,16},{16,32},{32,48},{48,64},{64,80},{80,96},{96,112},{1... | collective-permute-start | bytes 196616 | tf_op jit(solution)/shard_map/while/body/eval_jaxpr/ppermute | solution.py:14
  550.0 12.9 %collective-permute-start.10 = (f32[128,256]{1,0:T(8,128)S(1)}, f32[128,256]{1,0:T(8,128)S(1)}, u32[]{:S(2)}, u32[]{:S(2)}) collective-permute-start(f32[128,256]{1,0:T(8,128)S(1)} %fusion.79), channel_id=1, source_target_pairs={{496,0},{0,16},{16,32},{32,48},{48,64},{64,80},{80,96},{96,112},{1... | collective-permute-start | bytes 393224 | tf_op jit(solution)/shard_map/while/body/eval_jaxpr/ppermute | solution.py:14
  552.0 11.0 %collective-permute-start.6 = (bf16[128,256]{1,0:T(8,128)(2,1)S(1)}, bf16[128,256]{1,0:T(8,128)(2,1)S(1)}, u32[]{:S(2)}, u32[]{:S(2)}) collective-permute-start(bf16[128,256]{1,0:T(8,128)(2,1)S(1)} %get-tuple-element.194), channel_id=1, source_target_pairs={{496,0},{0,16},{16,32},{32,48},{48,64},{64,80},{80,96},{96,112},{1... | collective-permute-start | bytes 196616 | tf_op jit(solution)/shard_map/while/body/eval_jaxpr/ppermute | solution.py:14
  563.5 12.9 %collective-permute-start.11 = (f32[128,256]{1,0:T(8,128)S(1)}, f32[128,256]{1,0:T(8,128)S(1)}, u32[]{:S(2)}, u32[]{:S(2)}) collective-permute-start(f32[128,256]{1,0:T(8,128)S(1)} %fusion.80), channel_id=1, source_target_pairs={{496,0},{0,16},{16,32},{32,48},{48,64},{64,80},{80,96},{96,112},{1... | collective-permute-start | bytes 393224 | tf_op jit(solution)/shard_map/while/body/eval_jaxpr/ppermute | solution.py:14
  565.4 11.0 %collective-permute-start.7 = (bf16[128,256]{1,0:T(8,128)(2,1)S(1)}, bf16[128,256]{1,0:T(8,128)(2,1)S(1)}, u32[]{:S(2)}, u32[]{:S(2)}) collective-permute-start(bf16[128,256]{1,0:T(8,128)(2,1)S(1)} %collective-permute-done.6), channel_id=1, source_target_pairs={{496,0},{0,16},{16,32},{32,48},{48,64},{64,80},{80,96},{96,112},{1... | collective-permute-start | bytes 196616 | tf_op jit(solution)/shard_map/while/body/eval_jaxpr/ppermute | solution.py:14
  576.9 13.0 %collective-permute-start.10 = (f32[128,256]{1,0:T(8,128)S(1)}, f32[128,256]{1,0:T(8,128)S(1)}, u32[]{:S(2)}, u32[]{:S(2)}) collective-permute-start(f32[128,256]{1,0:T(8,128)S(1)} %fusion.79), channel_id=1, source_target_pairs={{496,0},{0,16},{16,32},{32,48},{48,64},{64,80},{80,96},{96,112},{1... | collective-permute-start | bytes 393224 | tf_op jit(solution)/shard_map/while/body/eval_jaxpr/ppermute | solution.py:14
  578.8 11.0 %collective-permute-start.6 = (bf16[128,256]{1,0:T(8,128)(2,1)S(1)}, bf16[128,256]{1,0:T(8,128)(2,1)S(1)}, u32[]{:S(2)}, u32[]{:S(2)}) collective-permute-start(bf16[128,256]{1,0:T(8,128)(2,1)S(1)} %get-tuple-element.194), channel_id=1, source_target_pairs={{496,0},{0,16},{16,32},{32,48},{48,64},{64,80},{80,96},{96,112},{1... | collective-permute-start | bytes 196616 | tf_op jit(solution)/shard_map/while/body/eval_jaxpr/ppermute | solution.py:14
  590.3 13.0 %collective-permute-start.11 = (f32[128,256]{1,0:T(8,128)S(1)}, f32[128,256]{1,0:T(8,128)S(1)}, u32[]{:S(2)}, u32[]{:S(2)}) collective-permute-start(f32[128,256]{1,0:T(8,128)S(1)} %fusion.80), channel_id=1, source_target_pairs={{496,0},{0,16},{16,32},{32,48},{48,64},{64,80},{80,96},{96,112},{1... | collective-permute-start | bytes 393224 | tf_op jit(solution)/shard_map/while/body/eval_jaxpr/ppermute | solution.py:14
  592.3 11.0 %collective-permute-start.7 = (bf16[128,256]{1,0:T(8,128)(2,1)S(1)}, bf16[128,256]{1,0:T(8,128)(2,1)S(1)}, u32[]{:S(2)}, u32[]{:S(2)}) collective-permute-start(bf16[128,256]{1,0:T(8,128)(2,1)S(1)} %collective-permute-done.6), channel_id=1, source_target_pairs={{496,0},{0,16},{16,32},{32,48},{48,64},{64,80},{80,96},{96,112},{1... | collective-permute-start | bytes 196616 | tf_op jit(solution)/shard_map/while/body/eval_jaxpr/ppermute | solution.py:14
  603.8 13.0 %collective-permute-start.10 = (f32[128,256]{1,0:T(8,128)S(1)}, f32[128,256]{1,0:T(8,128)S(1)}, u32[]{:S(2)}, u32[]{:S(2)}) collective-permute-start(f32[128,256]{1,0:T(8,128)S(1)} %fusion.79), channel_id=1, source_target_pairs={{496,0},{0,16},{16,32},{32,48},{48,64},{64,80},{80,96},{96,112},{1... | collective-permute-start | bytes 393224 | tf_op jit(solution)/shard_map/while/body/eval_jaxpr/ppermute | solution.py:14
  605.8 11.1 %collective-permute-start.6 = (bf16[128,256]{1,0:T(8,128)(2,1)S(1)}, bf16[128,256]{1,0:T(8,128)(2,1)S(1)}, u32[]{:S(2)}, u32[]{:S(2)}) collective-permute-start(bf16[128,256]{1,0:T(8,128)(2,1)S(1)} %get-tuple-element.194), channel_id=1, source_target_pairs={{496,0},{0,16},{16,32},{32,48},{48,64},{64,80},{80,96},{96,112},{1... | collective-permute-start | bytes 196616 | tf_op jit(solution)/shard_map/while/body/eval_jaxpr/ppermute | solution.py:14
  617.3 12.9 %collective-permute-start.11 = (f32[128,256]{1,0:T(8,128)S(1)}, f32[128,256]{1,0:T(8,128)S(1)}, u32[]{:S(2)}, u32[]{:S(2)}) collective-permute-start(f32[128,256]{1,0:T(8,128)S(1)} %fusion.80), channel_id=1, source_target_pairs={{496,0},{0,16},{16,32},{32,48},{48,64},{64,80},{80,96},{96,112},{1... | collective-permute-start | bytes 393224 | tf_op jit(solution)/shard_map/while/body/eval_jaxpr/ppermute | solution.py:14
  630.7 12.9 %collective-permute-start.10 = (f32[128,256]{1,0:T(8,128)S(1)}, f32[128,256]{1,0:T(8,128)S(1)}, u32[]{:S(2)}, u32[]{:S(2)}) collective-permute-start(f32[128,256]{1,0:T(8,128)S(1)} %fusion.79), channel_id=1, source_target_pairs={{496,0},{0,16},{16,32},{32,48},{48,64},{64,80},{80,96},{96,112},{1... | collective-permute-start | bytes 393224 | tf_op jit(solution)/shard_map/while/body/eval_jaxpr/ppermute | solution.py:14
  632.7 11.0 %collective-permute-start.6 = (bf16[128,256]{1,0:T(8,128)(2,1)S(1)}, bf16[128,256]{1,0:T(8,128)(2,1)S(1)}, u32[]{:S(2)}, u32[]{:S(2)}) collective-permute-start(bf16[128,256]{1,0:T(8,128)(2,1)S(1)} %get-tuple-element.194), channel_id=1, source_target_pairs={{496,0},{0,16},{16,32},{32,48},{48,64},{64,80},{80,96},{96,112},{1... | collective-permute-start | bytes 196616 | tf_op jit(solution)/shard_map/while/body/eval_jaxpr/ppermute | solution.py:14
  644.1 12.9 %collective-permute-start.11 = (f32[128,256]{1,0:T(8,128)S(1)}, f32[128,256]{1,0:T(8,128)S(1)}, u32[]{:S(2)}, u32[]{:S(2)}) collective-permute-start(f32[128,256]{1,0:T(8,128)S(1)} %fusion.80), channel_id=1, source_target_pairs={{496,0},{0,16},{16,32},{32,48},{48,64},{64,80},{80,96},{96,112},{1... | collective-permute-start | bytes 393224 | tf_op jit(solution)/shard_map/while/body/eval_jaxpr/ppermute | solution.py:14
  657.6 12.9 %collective-permute-start.10 = (f32[128,256]{1,0:T(8,128)S(1)}, f32[128,256]{1,0:T(8,128)S(1)}, u32[]{:S(2)}, u32[]{:S(2)}) collective-permute-start(f32[128,256]{1,0:T(8,128)S(1)} %fusion.79), channel_id=1, source_target_pairs={{496,0},{0,16},{16,32},{32,48},{48,64},{64,80},{80,96},{96,112},{1... | collective-permute-start | bytes 393224 | tf_op jit(solution)/shard_map/while/body/eval_jaxpr/ppermute | solution.py:14
  659.5 11.0 %collective-permute-start.6 = (bf16[128,256]{1,0:T(8,128)(2,1)S(1)}, bf16[128,256]{1,0:T(8,128)(2,1)S(1)}, u32[]{:S(2)}, u32[]{:S(2)}) collective-permute-start(bf16[128,256]{1,0:T(8,128)(2,1)S(1)} %get-tuple-element.194), channel_id=1, source_target_pairs={{496,0},{0,16},{16,32},{32,48},{48,64},{64,80},{80,96},{96,112},{1... | collective-permute-start | bytes 196616 | tf_op jit(solution)/shard_map/while/body/eval_jaxpr/ppermute | solution.py:14
  671.0 12.9 %collective-permute-start.11 = (f32[128,256]{1,0:T(8,128)S(1)}, f32[128,256]{1,0:T(8,128)S(1)}, u32[]{:S(2)}, u32[]{:S(2)}) collective-permute-start(f32[128,256]{1,0:T(8,128)S(1)} %fusion.80), channel_id=1, source_target_pairs={{496,0},{0,16},{16,32},{32,48},{48,64},{64,80},{80,96},{96,112},{1... | collective-permute-start | bytes 393224 | tf_op jit(solution)/shard_map/while/body/eval_jaxpr/ppermute | solution.py:14
  684.4 12.9 %collective-permute-start.10 = (f32[128,256]{1,0:T(8,128)S(1)}, f32[128,256]{1,0:T(8,128)S(1)}, u32[]{:S(2)}, u32[]{:S(2)}) collective-permute-start(f32[128,256]{1,0:T(8,128)S(1)} %fusion.79), channel_id=1, source_target_pairs={{496,0},{0,16},{16,32},{32,48},{48,64},{64,80},{80,96},{96,112},{1... | collective-permute-start | bytes 393224 | tf_op jit(solution)/shard_map/while/body/eval_jaxpr/ppermute | solution.py:14
  697.8 12.9 %collective-permute-start.11 = (f32[128,256]{1,0:T(8,128)S(1)}, f32[128,256]{1,0:T(8,128)S(1)}, u32[]{:S(2)}, u32[]{:S(2)}) collective-permute-start(f32[128,256]{1,0:T(8,128)S(1)} %fusion.80), channel_id=1, source_target_pairs={{496,0},{0,16},{16,32},{32,48},{48,64},{64,80},{80,96},{96,112},{1... | collective-permute-start | bytes 393224 | tf_op jit(solution)/shard_map/while/body/eval_jaxpr/ppermute | solution.py:14
  711.2 12.9 %collective-permute-start.10 = (f32[128,256]{1,0:T(8,128)S(1)}, f32[128,256]{1,0:T(8,128)S(1)}, u32[]{:S(2)}, u32[]{:S(2)}) collective-permute-start(f32[128,256]{1,0:T(8,128)S(1)} %fusion.79), channel_id=1, source_target_pairs={{496,0},{0,16},{16,32},{32,48},{48,64},{64,80},{80,96},{96,112},{1... | collective-permute-start | bytes 393224 | tf_op jit(solution)/shard_map/while/body/eval_jaxpr/ppermute | solution.py:14
  724.6 12.9 %collective-permute-start.11 = (f32[128,256]{1,0:T(8,128)S(1)}, f32[128,256]{1,0:T(8,128)S(1)}, u32[]{:S(2)}, u32[]{:S(2)}) collective-permute-start(f32[128,256]{1,0:T(8,128)S(1)} %fusion.80), channel_id=1, source_target_pairs={{496,0},{0,16},{16,32},{32,48},{48,64},{64,80},{80,96},{96,112},{1... | collective-permute-start | bytes 393224 | tf_op jit(solution)/shard_map/while/body/eval_jaxpr/ppermute | solution.py:14
  738.0 12.9 %collective-permute-start.10 = (f32[128,256]{1,0:T(8,128)S(1)}, f32[128,256]{1,0:T(8,128)S(1)}, u32[]{:S(2)}, u32[]{:S(2)}) collective-permute-start(f32[128,256]{1,0:T(8,128)S(1)} %fusion.79), channel_id=1, source_target_pairs={{496,0},{0,16},{16,32},{32,48},{48,64},{64,80},{80,96},{96,112},{1... | collective-permute-start | bytes 393224 | tf_op jit(solution)/shard_map/while/body/eval_jaxpr/ppermute | solution.py:14
  740.0 11.0 %collective-permute-start.6 = (bf16[128,256]{1,0:T(8,128)(2,1)S(1)}, bf16[128,256]{1,0:T(8,128)(2,1)S(1)}, u32[]{:S(2)}, u32[]{:S(2)}) collective-permute-start(bf16[128,256]{1,0:T(8,128)(2,1)S(1)} %get-tuple-element.194), channel_id=1, source_target_pairs={{496,0},{0,16},{16,32},{32,48},{48,64},{64,80},{80,96},{96,112},{1... | collective-permute-start | bytes 196616 | tf_op jit(solution)/shard_map/while/body/eval_jaxpr/ppermute | solution.py:14
  751.5 13.0 %collective-permute-start.11 = (f32[128,256]{1,0:T(8,128)S(1)}, f32[128,256]{1,0:T(8,128)S(1)}, u32[]{:S(2)}, u32[]{:S(2)}) collective-permute-start(f32[128,256]{1,0:T(8,128)S(1)} %fusion.80), channel_id=1, source_target_pairs={{496,0},{0,16},{16,32},{32,48},{48,64},{64,80},{80,96},{96,112},{1... | collective-permute-start | bytes 393224 | tf_op jit(solution)/shard_map/while/body/eval_jaxpr/ppermute | solution.py:14
  753.4 11.0 %collective-permute-start.7 = (bf16[128,256]{1,0:T(8,128)(2,1)S(1)}, bf16[128,256]{1,0:T(8,128)(2,1)S(1)}, u32[]{:S(2)}, u32[]{:S(2)}) collective-permute-start(bf16[128,256]{1,0:T(8,128)(2,1)S(1)} %collective-permute-done.6), channel_id=1, source_target_pairs={{496,0},{0,16},{16,32},{32,48},{48,64},{64,80},{80,96},{96,112},{1... | collective-permute-start | bytes 196616 | tf_op jit(solution)/shard_map/while/body/eval_jaxpr/ppermute | solution.py:14
  764.9 13.0 %collective-permute-start.10 = (f32[128,256]{1,0:T(8,128)S(1)}, f32[128,256]{1,0:T(8,128)S(1)}, u32[]{:S(2)}, u32[]{:S(2)}) collective-permute-start(f32[128,256]{1,0:T(8,128)S(1)} %fusion.79), channel_id=1, source_target_pairs={{496,0},{0,16},{16,32},{32,48},{48,64},{64,80},{80,96},{96,112},{1... | collective-permute-start | bytes 393224 | tf_op jit(solution)/shard_map/while/body/eval_jaxpr/ppermute | solution.py:14
  766.9 11.1 %collective-permute-start.6 = (bf16[128,256]{1,0:T(8,128)(2,1)S(1)}, bf16[128,256]{1,0:T(8,128)(2,1)S(1)}, u32[]{:S(2)}, u32[]{:S(2)}) collective-permute-start(bf16[128,256]{1,0:T(8,128)(2,1)S(1)} %get-tuple-element.194), channel_id=1, source_target_pairs={{496,0},{0,16},{16,32},{32,48},{48,64},{64,80},{80,96},{96,112},{1... | collective-permute-start | bytes 196616 | tf_op jit(solution)/shard_map/while/body/eval_jaxpr/ppermute | solution.py:14
  778.4 12.9 %collective-permute-start.11 = (f32[128,256]{1,0:T(8,128)S(1)}, f32[128,256]{1,0:T(8,128)S(1)}, u32[]{:S(2)}, u32[]{:S(2)}) collective-permute-start(f32[128,256]{1,0:T(8,128)S(1)} %fusion.80), channel_id=1, source_target_pairs={{496,0},{0,16},{16,32},{32,48},{48,64},{64,80},{80,96},{96,112},{1... | collective-permute-start | bytes 393224 | tf_op jit(solution)/shard_map/while/body/eval_jaxpr/ppermute | solution.py:14
  791.9 12.9 %collective-permute-start.10 = (f32[128,256]{1,0:T(8,128)S(1)}, f32[128,256]{1,0:T(8,128)S(1)}, u32[]{:S(2)}, u32[]{:S(2)}) collective-permute-start(f32[128,256]{1,0:T(8,128)S(1)} %fusion.79), channel_id=1, source_target_pairs={{496,0},{0,16},{16,32},{32,48},{48,64},{64,80},{80,96},{96,112},{1... | collective-permute-start | bytes 393224 | tf_op jit(solution)/shard_map/while/body/eval_jaxpr/ppermute | solution.py:14
  805.3 12.9 %collective-permute-start.11 = (f32[128,256]{1,0:T(8,128)S(1)}, f32[128,256]{1,0:T(8,128)S(1)}, u32[]{:S(2)}, u32[]{:S(2)}) collective-permute-start(f32[128,256]{1,0:T(8,128)S(1)} %fusion.80), channel_id=1, source_target_pairs={{496,0},{0,16},{16,32},{32,48},{48,64},{64,80},{80,96},{96,112},{1... | collective-permute-start | bytes 393224 | tf_op jit(solution)/shard_map/while/body/eval_jaxpr/ppermute | solution.py:14
  818.7 12.9 %collective-permute-start.10 = (f32[128,256]{1,0:T(8,128)S(1)}, f32[128,256]{1,0:T(8,128)S(1)}, u32[]{:S(2)}, u32[]{:S(2)}) collective-permute-start(f32[128,256]{1,0:T(8,128)S(1)} %fusion.79), channel_id=1, source_target_pairs={{496,0},{0,16},{16,32},{32,48},{48,64},{64,80},{80,96},{96,112},{1... | collective-permute-start | bytes 393224 | tf_op jit(solution)/shard_map/while/body/eval_jaxpr/ppermute | solution.py:14
  832.1 12.9 %collective-permute-start.11 = (f32[128,256]{1,0:T(8,128)S(1)}, f32[128,256]{1,0:T(8,128)S(1)}, u32[]{:S(2)}, u32[]{:S(2)}) collective-permute-start(f32[128,256]{1,0:T(8,128)S(1)} %fusion.80), channel_id=1, source_target_pairs={{496,0},{0,16},{16,32},{32,48},{48,64},{64,80},{80,96},{96,112},{1... | collective-permute-start | bytes 393224 | tf_op jit(solution)/shard_map/while/body/eval_jaxpr/ppermute | solution.py:14
  845.5 12.9 %collective-permute-start.10 = (f32[128,256]{1,0:T(8,128)S(1)}, f32[128,256]{1,0:T(8,128)S(1)}, u32[]{:S(2)}, u32[]{:S(2)}) collective-permute-start(f32[128,256]{1,0:T(8,128)S(1)} %fusion.79), channel_id=1, source_target_pairs={{496,0},{0,16},{16,32},{32,48},{48,64},{64,80},{80,96},{96,112},{1... | collective-permute-start | bytes 393224 | tf_op jit(solution)/shard_map/while/body/eval_jaxpr/ppermute | solution.py:14
  858.9 12.9 %collective-permute-start.11 = (f32[128,256]{1,0:T(8,128)S(1)}, f32[128,256]{1,0:T(8,128)S(1)}, u32[]{:S(2)}, u32[]{:S(2)}) collective-permute-start(f32[128,256]{1,0:T(8,128)S(1)} %fusion.80), channel_id=1, source_target_pairs={{496,0},{0,16},{16,32},{32,48},{48,64},{64,80},{80,96},{96,112},{1... | collective-permute-start | bytes 393224 | tf_op jit(solution)/shard_map/while/body/eval_jaxpr/ppermute | solution.py:14
  872.3 12.9 %collective-permute-start.10 = (f32[128,256]{1,0:T(8,128)S(1)}, f32[128,256]{1,0:T(8,128)S(1)}, u32[]{:S(2)}, u32[]{:S(2)}) collective-permute-start(f32[128,256]{1,0:T(8,128)S(1)} %fusion.79), channel_id=1, source_target_pairs={{496,0},{0,16},{16,32},{32,48},{48,64},{64,80},{80,96},{96,112},{1... | collective-permute-start | bytes 393224 | tf_op jit(solution)/shard_map/while/body/eval_jaxpr/ppermute | solution.py:14
  885.8 12.9 %collective-permute-start.11 = (f32[128,256]{1,0:T(8,128)S(1)}, f32[128,256]{1,0:T(8,128)S(1)}, u32[]{:S(2)}, u32[]{:S(2)}) collective-permute-start(f32[128,256]{1,0:T(8,128)S(1)} %fusion.80), channel_id=1, source_target_pairs={{496,0},{0,16},{16,32},{32,48},{48,64},{64,80},{80,96},{96,112},{1... | collective-permute-start | bytes 393224 | tf_op jit(solution)/shard_map/while/body/eval_jaxpr/ppermute | solution.py:14
  899.2 12.9 %collective-permute-start.10 = (f32[128,256]{1,0:T(8,128)S(1)}, f32[128,256]{1,0:T(8,128)S(1)}, u32[]{:S(2)}, u32[]{:S(2)}) collective-permute-start(f32[128,256]{1,0:T(8,128)S(1)} %fusion.79), channel_id=1, source_target_pairs={{496,0},{0,16},{16,32},{32,48},{48,64},{64,80},{80,96},{96,112},{1... | collective-permute-start | bytes 393224 | tf_op jit(solution)/shard_map/while/body/eval_jaxpr/ppermute | solution.py:14
  912.6 12.9 %collective-permute-start.11 = (f32[128,256]{1,0:T(8,128)S(1)}, f32[128,256]{1,0:T(8,128)S(1)}, u32[]{:S(2)}, u32[]{:S(2)}) collective-permute-start(f32[128,256]{1,0:T(8,128)S(1)} %fusion.80), channel_id=1, source_target_pairs={{496,0},{0,16},{16,32},{32,48},{48,64},{64,80},{80,96},{96,112},{1... | collective-permute-start | bytes 393224 | tf_op jit(solution)/shard_map/while/body/eval_jaxpr/ppermute | solution.py:14
  926.0 12.9 %collective-permute-start.10 = (f32[128,256]{1,0:T(8,128)S(1)}, f32[128,256]{1,0:T(8,128)S(1)}, u32[]{:S(2)}, u32[]{:S(2)}) collective-permute-start(f32[128,256]{1,0:T(8,128)S(1)} %fusion.79), channel_id=1, source_target_pairs={{496,0},{0,16},{16,32},{32,48},{48,64},{64,80},{80,96},{96,112},{1... | collective-permute-start | bytes 393224 | tf_op jit(solution)/shard_map/while/body/eval_jaxpr/ppermute | solution.py:14
  939.4 12.9 %collective-permute-start.11 = (f32[128,256]{1,0:T(8,128)S(1)}, f32[128,256]{1,0:T(8,128)S(1)}, u32[]{:S(2)}, u32[]{:S(2)}) collective-permute-start(f32[128,256]{1,0:T(8,128)S(1)} %fusion.80), channel_id=1, source_target_pairs={{496,0},{0,16},{16,32},{32,48},{48,64},{64,80},{80,96},{96,112},{1... | collective-permute-start | bytes 393224 | tf_op jit(solution)/shard_map/while/body/eval_jaxpr/ppermute | solution.py:14
  (138 other events, 1757.5 us)
Sparse Core Ops, SparseCore 0:
  10.1 43.5 all-gather.2
  522.0 72.0 reduce-scatter.1
where the time goes:
time: 974 us; the launch traced here: 965 us
  waiting for transfers between devices  425 us (44%)
  starting transfers between devices  404 us (41%)
  blocking collectives  47.2 us (5%)
  matrix products  36.5 us (4%)
  other arithmetic  21.5 us (2%)
  between operations  15 us (2%)
  local copies, waits for them, and re-layouts  13.1 us (1%)
    ppermute x192, waiting for transfers between devices, shifted(): return lax.ppermute(block, axis, route)  414 us
    ppermute x192, starting transfers between devices, shifted(): return lax.ppermute(block, axis, route)  370 us
  transfers between devices with their start and end apart: 196, of which 97 were waited for; matrix products, arithmetic and copies ran while one was open for 6% of the time, Pallas kernels for 0%

commit v1 on v0

v1 whole, which is shorter than its diff:
```python
import math

import jax
import jax.numpy as jnp
from jax import lax
from jax.experimental import pallas as pl
from jax.experimental.pallas import tpu as pltpu
from jax.sharding import Mesh, PartitionSpec as P

ITEMS = 65536
BF16 = jnp.bfloat16
F32 = jnp.float32
VMEM_LIMIT = 56 * 1024 * 1024


def sample_chance(identities):
    return jnp.log1p(1.0 / (identities.astype(F32) + 1.0)) / math.log(ITEMS + 1)


def dot_rows(left, right):
    return lax.dot_general(left, right, (((1,), (1,)), ((), ())), preferred_element_type=F32)


def dot_plain(left, right):
    return jnp.dot(left, right, preferred_element_type=F32)


def eye(size):
    return lax.broadcasted_iota(jnp.int32, (size, size), 0) == lax.broadcasted_iota(
        jnp.int32, (size, size), 1
    )


def to_row(column):
    return jnp.sum(jnp.where(eye(column.shape[0]), column, 0), axis=0, keepdims=True)


def to_column(row):
    return jnp.sum(jnp.where(eye(row.shape[1]), row, 0), axis=1, keepdims=True)


def call(kernel, out_shape, name, **more):
    return pl.pallas_call(
        kernel,
        out_shape=out_shape,
        name=name,
        compiler_params=pltpu.CompilerParams(vmem_limit_bytes=VMEM_LIMIT),
        **more,
    )


def prepare_kernel(
    capacity, q_ref, it_ref, ng_ref, sh_ref, own_col_ref, own_row_ref, slot_ref, block_ref, out_ref
):
    rows, keys = q_ref.shape[0], it_ref.shape[0] + ng_ref.shape[0]
    block_ref[0:rows, :] = q_ref[...]
    block_ref[rows : 2 * rows, :] = it_ref[...]
    block_ref[2 * rows : rows + keys, :] = ng_ref[...]
    shift = sh_ref[...]
    high = shift.astype(BF16)
    rest = shift - high.astype(F32)
    middle = rest.astype(BF16)
    low = (rest - middle.astype(F32)).astype(BF16)
    extra = block_ref.shape[0] - rows - keys
    place = lax.broadcasted_iota(jnp.int32, (extra, keys), 0)
    stacked = jnp.where(
        place == 0,
        high.astype(F32),
        jnp.where(place == 1, middle.astype(F32), jnp.where(place == 2, low.astype(F32), 0.0)),
    )
    block_ref[rows + keys :, :] = jnp.zeros((extra, block_ref.shape[1]), BF16)
    block_ref[rows + keys :, 0:keys] = stacked.astype(BF16)

    count = it_ref.shape[0]
    own_col, own_row = own_col_ref[...], own_row_ref[...]
    earlier = lax.broadcasted_iota(jnp.int32, (count, count), 0) < lax.broadcasted_iota(
        jnp.int32, (count, count), 1
    )
    rank = jnp.sum(
        jnp.where(jnp.logical_and(own_col == own_row, earlier), 1.0, 0.0), axis=0, keepdims=True
    )
    target = own_row * capacity + rank.astype(jnp.int32)
    places = out_ref.shape[0]
    chosen = jnp.where(
        lax.broadcasted_iota(jnp.int32, (places, count), 0) == target, 1.0, 0.0
    ).astype(BF16)
    slot = slot_ref[...]
    lane = lax.broadcasted_iota(jnp.int32, (count, 128), 1)
    details = jnp.where(
        lane == 0, slot >> 5, jnp.where(lane == 1, slot & 31, jnp.where(lane == 2, 1, 0))
    )
    width = it_ref.shape[1]
    out_ref[:, 0:width] = dot_plain(chosen, it_ref[...]).astype(BF16)
    out_ref[:, width:] = dot_plain(chosen, details.astype(F32).astype(BF16)).astype(BF16)


def update_kernel(got_ref, mem_ref, new_ref):
    places, width = got_ref.shape[0], mem_ref.shape[1]
    rows = mem_ref.shape[0]
    details = jnp.transpose(got_ref[:, width:].astype(F32))
    slot = details[0:1, :] * 32.0 + details[1:2, :]
    slot = jnp.where(details[2:3, :] > 0.5, slot, -1.0).astype(jnp.int32)
    entry = lax.broadcasted_iota(jnp.int32, (1, places), 1).astype(F32)
    step = 256
    for start in range(0, rows, step):
        row = lax.broadcasted_iota(jnp.int32, (step, places), 0) + start
        latest = jnp.max(jnp.where(row == slot, entry, -1.0), axis=1, keepdims=True)
        chosen = jnp.where(entry == latest, 1.0, 0.0).astype(BF16)
        fresh = dot_plain(chosen, got_ref[:, 0:width])
        old = mem_ref[start : start + step, :].astype(F32)
        new_ref[start : start + step, :] = jnp.where(latest >= 0.0, fresh, old).astype(BF16)


def memory_kernel(*refs):
    q_ref, *mem_refs, out_ref, lse_ref, s_ref = refs
    step = 512
    pieces = [(ref, at) for ref in mem_refs for at in range(0, ref.shape[0], step)]
    q = q_ref[...]
    highest = None
    for n, (ref, at) in enumerate(pieces):
        s = dot_rows(q, ref[at : at + step, :])
        s_ref[:, n * step : (n + 1) * step] = s
        for lane in range(0, step, 128):
            part = s[:, lane : lane + 128]
            highest = part if highest is None else jnp.maximum(highest, part)
    top = jnp.max(highest, axis=1, keepdims=True)
    total = jnp.zeros((q.shape[0], 128), F32)
    acc = jnp.zeros(q.shape, F32)
    for n, (ref, at) in enumerate(pieces):
        p = jnp.exp(s_ref[:, n * step : (n + 1) * step] - top)
        for lane in range(0, step, 128):
            total = total + p[:, lane : lane + 128]
        acc = acc + dot_plain(p.astype(BF16), ref[at : at + step, :])
    total = jnp.sum(total, axis=1, keepdims=True)
    out_ref[...] = (acc / total).astype(BF16)
    lse = top + jnp.log(total)
    for n in range(q.shape[0] // 128):
        lse_ref[0, n : n + 1, :] = to_row(lse[n * 128 : (n + 1) * 128, :])


def batch_kernel(g_ref, q_ref, it_ref, sh_ref, out_ref, stat_ref, s_ref):
    peers = g_ref.shape[0]
    rows = q_ref.shape[0]
    keys = sh_ref.shape[1]
    q = q_ref[...]
    highest = None
    for k in range(peers):
        parts = g_ref[k, rows + keys :, 0:keys].astype(F32)
        shift = parts[0:1, :] + (parts[1:2, :] + parts[2:3, :])
        s = dot_rows(q, g_ref[k, rows : rows + keys, :]) + shift
        s_ref[k] = s
        highest = s if highest is None else jnp.maximum(highest, s)
    top = jnp.max(highest, axis=1, keepdims=True)
    total = jnp.zeros((rows, keys), F32)
    acc = jnp.zeros(q.shape, F32)
    for k in range(peers):
        p = jnp.exp(s_ref[k] - top)
        total = total + p
        acc = acc + dot_plain(p.astype(BF16), g_ref[k, rows : rows + keys, :])
    total = jnp.sum(total, axis=1, keepdims=True)
    out_ref[...] = acc / total
    stat_ref[0:1, :] = to_row(top + jnp.log(total))
    own = dot_rows(q, it_ref[...]) + sh_ref[:, 0:rows]
    stat_ref[1:2, :] = jnp.sum(jnp.where(eye(rows), own, 0.0), axis=0, keepdims=True)


def total_kernel(lse_ref, stat_ref, total_ref, loss_ref):
    lse = lse_ref[...]
    batch = stat_ref[0:1, :]
    top = jnp.maximum(jnp.max(lse, axis=0, keepdims=True), batch)
    summed = jnp.sum(jnp.exp(lse - top), axis=0, keepdims=True) + jnp.exp(batch - top)
    log_total = top + jnp.log(summed)
    total_ref[...] = log_total
    loss_ref[...] = log_total - stat_ref[1:2, :]


def item_kernel(g_ref, lt_ref, q_ref, it_ref, ng_ref, sh_ref, item_ref, neg_ref):
    peers = g_ref.shape[0]
    rows = q_ref.shape[0]
    items, negs = it_ref[...], ng_ref[...]
    shift_items = to_column(sh_ref[:, 0:rows])
    shift_negs = to_column(sh_ref[:, rows:])
    item_acc = jnp.zeros(items.shape, F32)
    neg_acc = jnp.zeros(negs.shape, F32)
    for k in range(peers):
        queries = g_ref[k, 0:rows, :]
        log_total = lt_ref[k : k + 1, :]
        w = jnp.exp(dot_rows(items, queries) + shift_items - log_total).astype(BF16)
        item_acc = item_acc + dot_plain(w, queries)
        w = jnp.exp(dot_rows(negs, queries) + shift_negs - log_total).astype(BF16)
        neg_acc = neg_acc + dot_plain(w, queries)
    item_ref[...] = item_acc - q_ref[...].astype(F32)
    neg_ref[...] = neg_acc


def query_kernel(parts_ref, lse_ref, lt_ref, batch_ref, stat_ref, it_ref, out_ref):
    log_total = lt_ref[...]
    out = batch_ref[...] * to_column(jnp.exp(stat_ref[0:1, :] - log_total))
    for k in range(parts_ref.shape[0]):
        share = to_column(jnp.exp(lse_ref[k : k + 1, :] - log_total))
        out = out + parts_ref[k].astype(F32) * share
    out_ref[...] = out - it_ref[...].astype(F32)


def local(
    query_vectors,
    item_vectors,
    negative_vectors,
    item_ids,
    negative_ids,
    negative_counts,
    memory,
    owners,
    memory_slots,
):
    rows, width = query_vectors.shape
    negatives = negative_vectors.shape[0]
    keys = rows + negatives
    mem = memory[0]
    half = mem.shape[0] // 2
    group = lax.axis_size("dp")
    shards = lax.axis_size("zh")
    depth = shards * lax.axis_size("zl")
    cycle = depth * lax.axis_size("yh")
    column = ("yh", "zh", "zl")

    def moved(block, over, by):
        route = [
            (y * depth + z, ((y + over) % 2) * depth + (z + by) % depth)
            for y in range(cycle // depth)
            for z in range(depth)
        ]
        return lax.ppermute(block, column, route)

    first, second = mem[:half], mem[half:]
    memory_blocks = [
        mem,
        moved(mem, 1, 0),
        moved(first, 0, -1),
        moved(second, 0, 1),
        moved(first, 1, -1),
        moved(second, 1, 1),
    ]
    column_queries = lax.all_gather(query_vectors, "zh", axis=0, tiled=True)

    batch_shift = -jnp.log(rows * group * sample_chance(item_ids))
    negative_shift = jnp.log(negative_counts.astype(F32)) - jnp.log(
        negatives * group * sample_chance(negative_ids)
    )
    shift = jnp.concatenate([batch_shift, negative_shift])[None, :]
    capacity = max(2, 2 * rows // cycle)
    block, outgoing = call(
        lambda *refs: prepare_kernel(capacity, *refs),
        (
            jax.ShapeDtypeStruct((rows + keys + 16, width), BF16),
            jax.ShapeDtypeStruct((cycle * capacity, width + 128), BF16),
        ),
        "prepare",
    )(
        query_vectors,
        item_vectors,
        negative_vectors,
        shift,
        owners,
        owners.reshape(1, rows),
        memory_slots.reshape(rows, 1),
    )
    gathered = lax.all_gather(block, "dp", axis=0, tiled=False)

    tile = 256
    count = column_queries.shape[0]
    total_rows = sum(b.shape[0] for b in memory_blocks)
    parts, lse = call(
        memory_kernel,
        (
            jax.ShapeDtypeStruct((count, width), BF16),
            jax.ShapeDtypeStruct((count // tile, tile // 128, 128), F32),
        ),
        "memory",
        grid=(count // tile,),
        in_specs=[pl.BlockSpec((tile, width), lambda i: (i, 0))]
        + [pl.BlockSpec(b.shape, lambda i: (0, 0)) for b in memory_blocks],
        out_specs=(
            pl.BlockSpec((tile, width), lambda i: (i, 0)),
            pl.BlockSpec((1, tile // 128, 128), lambda i: (i, 0, 0)),
        ),
        scratch_shapes=[pltpu.VMEM((tile, total_rows), F32)],
    )(column_queries, *memory_blocks)
    lse_back = lax.all_to_all(lse.reshape(shards, rows), "zh", 0, 0, tiled=True)
    parts, lse_back = lax.optimization_barrier((parts, lse_back))
    parts_back = lax.all_to_all(parts.reshape(shards, rows, width), "zh", 0, 0, tiled=True)

    batch_part, batch_stat = call(
        batch_kernel,
        (
            jax.ShapeDtypeStruct((rows, width), F32),
            jax.ShapeDtypeStruct((2, rows), F32),
        ),
        "batch",
        scratch_shapes=[pltpu.VMEM((group, rows, keys), F32)],
    )(gathered, query_vectors, item_vectors, shift)
    log_total, loss = call(
        total_kernel,
        (jax.ShapeDtypeStruct((1, rows), F32), jax.ShapeDtypeStruct((1, rows), F32)),
        "total",
    )(lse_back, batch_stat)
    group_totals = lax.all_gather(log_total, "dp", axis=0, tiled=True)
    item_grad, negative_grad = call(
        item_kernel,
        (
            jax.ShapeDtypeStruct((rows, width), F32),
            jax.ShapeDtypeStruct((negatives, width), F32),
        ),
        "items",
    )(gathered, group_totals, query_vectors, item_vectors, negative_vectors, shift)
    query_grad = call(query_kernel, jax.ShapeDtypeStruct((rows, width), F32), "queries")(
        parts_back, lse_back, log_total, batch_part, batch_stat, item_vectors
    )

    arrived = lax.all_to_all(outgoing, column, 0, 0, tiled=True)
    updated = call(update_kernel, jax.ShapeDtypeStruct(mem.shape, BF16), "update")(arrived, mem)
    return (loss[0], query_grad, item_grad, negative_grad, updated[None])


def solution(mesh):
    cycle, group = mesh.shape["mem"], mesh.shape["dp"]
    cut = Mesh(
        mesh.devices.reshape(2, cycle // 4, 2, group), ("yh", "zh", "zl", "dp")
    )
    spread = ("yh", "zh", "zl", "dp")
    column = ("yh", "zh", "zl")
    return jax.shard_map(
        local,
        mesh=cut,
        in_specs=(
            P(spread, None),
            P(spread, None),
            P(spread, None),
            P(spread),
            P(spread),
            P(spread),
            P("dp", column, None),
            P(spread, None),
            P(spread),
        ),
        out_specs=(
            P(spread),
            P(spread, None),
            P(spread, None),
            P(spread, None),
            P("dp", column, None),
        ),
        check_vma=False,
    )
```

time: 974 us -> 184 us (0.19)
  the two profiles are of different devices: /device:TPU:6 before, /device:TPU:1 now
where the time goes in v1:
time: 184 us; the launch traced here: 183 us
  blocking collectives  78.2 us (42%)
  starting transfers between devices  34.4 us (19%)
  Pallas kernels  31.1 us (17%)
  waiting for transfers between devices  17.3 us (9%)
  between operations  14.2 us (8%)
  local copies, waits for them, and re-layouts  6.36 us (3%)
  other arithmetic  1.94 us (1%)
    all_gather x1, blocking collectives, local(): column_queries = lax.all_gather(query_vectors, 'zh', axis=0, tiled=True)  30.5 us
    all_gather x1, blocking collectives, local(): group_totals = lax.all_gather(log_total, 'dp', axis=0, tiled=True)  29.7 us
    ppermute x5, starting transfers between devices, moved(): return lax.ppermute(block, column, route)  26.4 us
    all_to_all x1, blocking collectives, local(): lse_back = lax.all_to_all(lse.reshape(shards, rows), 'zh', 0, 0, tiled=True)  18 us
    all_to_all x1, waiting for transfers between devices, local(): arrived = lax.all_to_all(outgoing, column, 0, 0, tiled=True)  17.2 us
    pallas_call x1, Pallas kernels, local(): call(memory_kernel, (jax.ShapeDtypeStruct((count, width), BF16), jax.Shap...  14 us
    pallas_call x1, Pallas kernels, local(): call(item_kernel, (jax.ShapeDtypeStruct((rows, width), F32), jax.ShapeDty...  5.27 us
    all_to_all x1, starting transfers between devices, local(): arrived = lax.all_to_all(outgoing, column, 0, 0, tiled=True)  4.5 us
  transfers between devices with their start and end apart: 8, of which 1 were waited for; matrix products, arithmetic and copies ran while one was open for 1% of the time, Pallas kernels for 15%

profile of v1, /device:TPU:1, one launch (start us, length us, event | category | flops | bytes accessed | tf_op | source)
XLA Modules:
  0.0 183.5 jit_solution(15484159230959015318)
XLA Ops:
  7.2 0.0 all-gather.4.cloned.1.call-start
  7.2 0.7 log_negate_fusion
  7.9 1.4 copy.18.refs_4_
  9.3 1.4 copy.19.refs_6_
  10.7 0.7 log_subtract_fusion
  11.4 0.6 pad_maximum_fusion
  11.9 1.9 %prepare.1 = (bf16[336,256]{1,0:T(8,128)(2,1)}, bf16[256,384]{1,0:T(8,128)(2,1)}) custom-call(bf16[128,256]{1,0:T(8,128)(2,1)} %q_ref.3, bf16[128,256]{1,0:T(8,128)(2,1)} %it_ref.5, bf16[64,256]{1,0:T(8,128)(2,1)} %ng_ref.1, f32[1,192]{1,0:T(1,128)} %bitcast.31, s32[128,1]{1,0:T(8,128)} %copy.18.refs_4_, s32[1,128]{1,0:T(1,128)} %bitcast.35, ...), custom_call_target="tpu_custom_call" | custom-call | tf_op jit(solution)/shard_map/prepare/pallas_call | solution.py:252
  13.9 0.0 all-gather.4.cloned.1.call-update
  13.9 5.7 %collective-permute-start = (bf16[1024,256]{1,0:T(8,128)(2,1)}, bf16[1024,256]{1,0:T(8,128)(2,1)S(1)}, u32[]{:S(2)}, u32[]{:S(2)}) collective-permute-start(bf16[1024,256]{1,0:T(8,128)(2,1)} %bitcast.22), channel_id=1, source_target_pairs={{0,256},{16,272},{32,288},{48,304},{64,320},{80,336},{96,352},{112... | collective-permute-start | bytes 1572872 | tf_op jit(solution)/shard_map/ppermute | solution.py:233
  19.6 1.1 slice_bitcast_fusion
  20.6 11.1 %collective-permute-start.1 = (bf16[512,256]{1,0:T(8,128)(2,1)S(1)}, bf16[512,256]{1,0:T(8,128)(2,1)S(1)}, u32[]{:S(2)}, u32[]{:S(2)}) collective-permute-start(bf16[512,256]{1,0:T(8,128)(2,1)S(1)} %get-tuple-element.30), channel_id=1, source_target_pairs={{0,240},{16,0},{32,16},{48,32},{64,48},{80,64},{96,80},{112,96},{1... | collective-permute-start | bytes 786440 | tf_op jit(solution)/shard_map/ppermute | solution.py:233
  31.8 1.9 %collective-permute-start.2 = (bf16[512,256]{1,0:T(8,128)(2,1)S(1)}, bf16[512,256]{1,0:T(8,128)(2,1)S(1)}, u32[]{:S(2)}, u32[]{:S(2)}) collective-permute-start(bf16[512,256]{1,0:T(8,128)(2,1)S(1)} %get-tuple-element.29), channel_id=1, source_target_pairs={{0,16},{16,32},{32,48},{48,64},{64,80},{80,96},{96,112},{112,128},... | collective-permute-start | bytes 786440 | tf_op jit(solution)/shard_map/ppermute | solution.py:233
  33.7 4.3 %collective-permute-start.3 = (bf16[512,256]{1,0:T(8,128)(2,1)S(1)}, bf16[512,256]{1,0:T(8,128)(2,1)S(1)}, u32[]{:S(2)}, u32[]{:S(2)}) collective-permute-start(bf16[512,256]{1,0:T(8,128)(2,1)S(1)} %get-tuple-element.30), channel_id=1, source_target_pairs={{0,496},{16,256},{32,272},{48,288},{64,304},{80,320},{96,336},{112... | collective-permute-start | bytes 786440 | tf_op jit(solution)/shard_map/ppermute | solution.py:233
  38.0 3.3 %collective-permute-start.4 = (bf16[512,256]{1,0:T(8,128)(2,1)S(1)}, bf16[512,256]{1,0:T(8,128)(2,1)S(1)}, u32[]{:S(2)}, u32[]{:S(2)}) collective-permute-start(bf16[512,256]{1,0:T(8,128)(2,1)S(1)} %get-tuple-element.29), channel_id=1, source_target_pairs={{0,272},{16,288},{32,304},{48,320},{64,336},{80,352},{96,368},{112... | collective-permute-start | bytes 786440 | tf_op jit(solution)/shard_map/ppermute | solution.py:233
  41.4 30.5 %all_gather.12.refs_0_ = bf16[1024,256]{1,0:T(8,128)(2,1)} all-gather(bf16[128,256]{1,0:T(8,128)(2,1)} %q_ref.3), channel_id=1, replica_groups=mesh['yh'=2,'zh'=8,'zl'=2,'dp'=16] {'zh'}, dimensions={0}, use_global_device_ids=true | all-gather | bytes 589824 | tf_op jit(solution)/shard_map/all_gather | solution.py:244
  71.9 0.0 collective-permute-done.1.refs_3_
  71.9 0.0 copy-start.3
  71.9 0.0 collective-permute-done.2.refs_4_
  71.9 0.0 copy-start.4
  72.0 0.0 collective-permute-done.3.refs_5_
  72.0 0.0 copy-start.5
  72.0 0.0 collective-permute-done.4.refs_6_
  72.0 0.0 copy-start.6
  72.0 0.0 collective-permute-done.refs_2_
  72.0 0.6 copy-done.3
  72.6 0.1 copy-done.4
  72.7 0.1 copy-done.5
  72.8 0.1 copy-done.6
  72.9 0.0 copy-start.2
  72.9 0.8 copy-done.2
  73.7 14.0 %memory.1 = (bf16[1024,256]{1,0:T(8,128)(2,1)}, f32[4,2,128]{2,1,0:T(2,128)}) custom-call(bf16[1024,256]{1,0:T(8,128)(2,1)} %all_gather.12.refs_0_, bf16[1024,256]{1,0:T(8,128)(2,1)} %bitcast.23, bf16[1024,256]{1,0:T(8,128)(2,1)} %copy-done.2, bf16[512,256]{1,0:T(8,128)(2,1)} %copy-done.3, bf16[512,256]{1,0:T(8,128)(2,1)} %copy-done.4, ...), custom_call_target="tpu_custom_call" | custom-call | tf_op jit(solution)/shard_map/memory/pallas_call | solution.py:273
  87.7 18.0 %all_to_all.28 = f32[8,1,128]{2,1,0:T(1,128)} all-to-all(f32[8,1,128]{2,1,0:T(1,128)} %bitcast.34), channel_id=1, replica_groups=mesh['yh'=2,'zh'=8,'zl'=2,'dp'=16] {'zh'}, dimensions={0} | all-to-all | bytes 8192 | tf_op jit(solution)/shard_map/all_to_all | solution.py:289
  105.7 4.5 %all-to-all-start.2 = ((bf16[32,8,384]{2,1,0:T(8,128)(2,1)}), bf16[32,8,384]{2,1,0:T(8,128)(2,1)S(1)}, u32[]{:S(2)}, u32[]{:S(2)}) async-start(bf16[32,8,384]{2,1,0:T(8,128)(2,1)} %bitcast.14), calls=%async_computation.2 | async-start | bytes 393216 | tf_op jit(solution)/shard_map/all_to_all | solution.py:320
  110.2 17.2 %all-to-all-done.2 = bf16[32,8,384]{2,1,0:T(8,128)(2,1)S(1)} async-done(((bf16[32,8,384]{2,1,0:T(8,128)(2,1)}), bf16[32,8,384]{2,1,0:T(8,128)(2,1)S(1)}, u32[]{:S(2)}, u32[]{:S(2)}) %all-to-all-start.2) | async-done | bytes 196640 | tf_op jit(solution)/shard_map/all_to_all | solution.py:320
  127.4 0.0 copy-start.1
  127.4 3.5 %all-to-all-start.1 = ((bf16[8,128,256]{2,1,0:T(8,128)(2,1)}), bf16[8,128,256]{2,1,0:T(8,128)(2,1)S(1)}, u32[]{:S(2)}, u32[]{:S(2)}) async-start(bf16[8,128,256]{2,1,0:T(8,128)(2,1)} %bitcast.26), calls=%async_computation.1 | async-start | bytes 1048576 | tf_op jit(solution)/shard_map/all_to_all | solution.py:291
  130.9 0.0 copy-done.1
  130.9 2.4 %update.1 = bf16[1024,256]{1,0:T(8,128)(2,1)} custom-call(bf16[256,384]{1,0:T(8,128)(2,1)} %bitcast.25, bf16[1024,256]{1,0:T(8,128)(2,1)} %bitcast.24), custom_call_target="tpu_custom_call" | custom-call | tf_op jit(solution)/shard_map/update/pallas_call | solution.py:321
  133.3 0.0 all-gather.4.cloned.1.call-done
  133.3 4.3 %batch.1 = (f32[128,256]{1,0:T(8,128)}, f32[2,128]{1,0:T(2,128)}) custom-call(bf16[16,336,256]{2,1,0:T(8,128)(2,1)} %bitcast.20, bf16[128,256]{1,0:T(8,128)(2,1)} %q_ref.3, bf16[128,256]{1,0:T(8,128)(2,1)} %it_ref.5, f32[1,192]{1,0:T(1,128)} %bitcast.32), custom_call_target="tpu_custom_call" | custom-call | tf_op jit(solution)/shard_map/batch/pallas_call | solution.py:293
  137.6 1.2 total.1
  138.8 29.7 %all-gather.1 = f32[16,1,128]{2,1,0:T(1,128)} all-gather(f32[1,1,128]{2,1,0:T(1,128)} %bitcast.36), channel_id=1, replica_groups=mesh['yh'=2,'zh'=8,'zl'=2,'dp'=16] {'dp'}, dimensions={0}, use_global_device_ids=true | all-gather | bytes 8704 | tf_op jit(solution)/shard_map/all_gather | solution.py:307
  168.5 5.3 %items.1 = (f32[128,256]{1,0:T(8,128)}, f32[64,256]{1,0:T(8,128)}) custom-call(bf16[16,336,256]{2,1,0:T(8,128)(2,1)} %bitcast.21, f32[16,128]{1,0:T(8,128)} %bitcast.30, bf16[128,256]{1,0:T(8,128)(2,1)} %q_ref.3, bf16[128,256]{1,0:T(8,128)(2,1)} %it_ref.5, bf16[64,256]{1,0:T(8,128)(2,1)} %ng_ref.1, f32[1,192]{1,0:T(1,128)} %bitcast.33), custom_call_target="tpu_custom_call" | custom-call | tf_op jit(solution)/shard_map/items/pallas_call | solution.py:308
  173.8 0.0 all-to-all-done.1.parts_ref
  173.8 0.0 copy-start
  173.8 0.8 copy-done
  174.6 2.0 %queries.1 = f32[128,256]{1,0:T(8,128)} custom-call(bf16[8,128,256]{2,1,0:T(8,128)(2,1)} %copy-done, f32[8,128]{1,0:T(8,128)} %bitcast.29, f32[1,128]{1,0:T(1,128)} %get-tuple-element.24.lt_ref, f32[128,256]{1,0:T(8,128)} %get-tuple-element.25.batch_ref, f32[2,128]{1,0:T(2,128)} %get-tuple-element.21.stat_ref, bf16[128,256]{1,0:T(8,128)(2,1)} %it_ref.5), custom_call_target="tpu_custom_call" | custom-call | tf_op jit(solution)/shard_map/queries/pallas_call | solution.py:316
Async XLA Ops:
  7.2 126.2 %all-gather.4.cloned.1.call-start = ((), (), s32[]{:S(2)}) async-start(), calls=%async_computation.3 | async-start | bytes 2924544 | tf_op jit(solution)/shard_map/all_gather | solution.py:268
  13.9 58.1 %collective-permute-start = (bf16[1024,256]{1,0:T(8,128)(2,1)}, bf16[1024,256]{1,0:T(8,128)(2,1)S(1)}, u32[]{:S(2)}, u32[]{:S(2)}) collective-permute-start(bf16[1024,256]{1,0:T(8,128)(2,1)} %bitcast.22), channel_id=1, source_target_pairs={{0,256},{16,272},{32,288},{48,304},{64,320},{80,336},{96,352},{112... | collective-permute-start | bytes 1572872 | tf_op jit(solution)/shard_map/ppermute | solution.py:233
  20.6 51.3 %collective-permute-start.1 = (bf16[512,256]{1,0:T(8,128)(2,1)S(1)}, bf16[512,256]{1,0:T(8,128)(2,1)S(1)}, u32[]{:S(2)}, u32[]{:S(2)}) collective-permute-start(bf16[512,256]{1,0:T(8,128)(2,1)S(1)} %get-tuple-element.30), channel_id=1, source_target_pairs={{0,240},{16,0},{32,16},{48,32},{64,48},{80,64},{96,80},{112,96},{1... | collective-permute-start | bytes 786440 | tf_op jit(solution)/shard_map/ppermute | solution.py:233
  31.8 40.2 %collective-permute-start.2 = (bf16[512,256]{1,0:T(8,128)(2,1)S(1)}, bf16[512,256]{1,0:T(8,128)(2,1)S(1)}, u32[]{:S(2)}, u32[]{:S(2)}) collective-permute-start(bf16[512,256]{1,0:T(8,128)(2,1)S(1)} %get-tuple-element.29), channel_id=1, source_target_pairs={{0,16},{16,32},{32,48},{48,64},{64,80},{80,96},{96,112},{112,128},... | collective-permute-start | bytes 786440 | tf_op jit(solution)/shard_map/ppermute | solution.py:233
  33.7 38.3 %collective-permute-start.3 = (bf16[512,256]{1,0:T(8,128)(2,1)S(1)}, bf16[512,256]{1,0:T(8,128)(2,1)S(1)}, u32[]{:S(2)}, u32[]{:S(2)}) collective-permute-start(bf16[512,256]{1,0:T(8,128)(2,1)S(1)} %get-tuple-element.30), channel_id=1, source_target_pairs={{0,496},{16,256},{32,272},{48,288},{64,304},{80,320},{96,336},{112... | collective-permute-start | bytes 786440 | tf_op jit(solution)/shard_map/ppermute | solution.py:233
  38.0 33.9 %collective-permute-start.4 = (bf16[512,256]{1,0:T(8,128)(2,1)S(1)}, bf16[512,256]{1,0:T(8,128)(2,1)S(1)}, u32[]{:S(2)}, u32[]{:S(2)}) collective-permute-start(bf16[512,256]{1,0:T(8,128)(2,1)S(1)} %get-tuple-element.29), channel_id=1, source_target_pairs={{0,272},{16,288},{32,304},{48,320},{64,336},{80,352},{96,368},{112... | collective-permute-start | bytes 786440 | tf_op jit(solution)/shard_map/ppermute | solution.py:233
  71.9 0.7 copy-start.3
  71.9 0.8 copy-start.4
  72.0 0.9 copy-start.5
  72.0 0.9 copy-start.6
  72.9 0.8 copy-start.2
  105.7 21.7 %all-to-all-start.2 = ((bf16[32,8,384]{2,1,0:T(8,128)(2,1)}), bf16[32,8,384]{2,1,0:T(8,128)(2,1)S(1)}, u32[]{:S(2)}, u32[]{:S(2)}) async-start(bf16[32,8,384]{2,1,0:T(8,128)(2,1)} %bitcast.14), calls=%async_computation.2 | async-start | bytes 393216 | tf_op jit(solution)/shard_map/all_to_all | solution.py:320
  127.4 3.5 %copy-start.1 = (bf16[32,8,384]{2,1,0:T(8,128)(2,1)}, bf16[32,8,384]{2,1,0:T(8,128)(2,1)S(1)}, u32[]{:S(2)}) copy-start(bf16[32,8,384]{2,1,0:T(8,128)(2,1)S(1)} %all-to-all-done.2) | copy-start | bytes 589828
  127.4 46.4 %all-to-all-start.1 = ((bf16[8,128,256]{2,1,0:T(8,128)(2,1)}), bf16[8,128,256]{2,1,0:T(8,128)(2,1)S(1)}, u32[]{:S(2)}, u32[]{:S(2)}) async-start(bf16[8,128,256]{2,1,0:T(8,128)(2,1)} %bitcast.26), calls=%async_computation.1 | async-start | bytes 1048576 | tf_op jit(solution)/shard_map/all_to_all | solution.py:291
  173.8 0.8 copy-start
Sparse Core Ops, SparseCore 0:
  14.0 58.2 all-gather.3

commit v2 on v1

v2 whole, which is shorter than its diff:
```python
import math

import jax
import jax.numpy as jnp
from jax import lax
from jax.experimental import pallas as pl
from jax.experimental.pallas import tpu as pltpu
from jax.sharding import Mesh, PartitionSpec as P

ITEMS = 65536
BF16 = jnp.bfloat16
F32 = jnp.float32
VMEM_LIMIT = 56 * 1024 * 1024


def sample_chance(identities):
    return jnp.log1p(1.0 / (identities.astype(F32) + 1.0)) / math.log(ITEMS + 1)


def dot_rows(left, right):
    return lax.dot_general(left, right, (((1,), (1,)), ((), ())), preferred_element_type=F32)


def dot_plain(left, right):
    return jnp.dot(left, right, preferred_element_type=F32)


def eye(size):
    return lax.broadcasted_iota(jnp.int32, (size, size), 0) == lax.broadcasted_iota(
        jnp.int32, (size, size), 1
    )


def to_row(column):
    return jnp.sum(jnp.where(eye(column.shape[0]), column, 0), axis=0, keepdims=True)


def to_column(row):
    return jnp.sum(jnp.where(eye(row.shape[1]), row, 0), axis=1, keepdims=True)


def split_rows(row, count):
    high = row.astype(BF16).astype(F32)
    middle = (row - high).astype(BF16).astype(F32)
    low = row - high - middle
    place = lax.broadcasted_iota(jnp.int32, (count, row.shape[1]), 0)
    return jnp.where(
        place == 0, high, jnp.where(place == 1, middle, jnp.where(place == 2, low, 0.0))
    )


def joined(three):
    three = three.astype(F32)
    return three[0:1, :] + (three[1:2, :] + three[2:3, :])


def call(kernel, operands, out_shape, name, scratch=()):
    here = pl.BlockSpec(memory_space=pltpu.VMEM)
    return pl.pallas_call(
        kernel,
        out_shape=out_shape,
        in_specs=[here] * len(operands),
        out_specs=(here,) * len(out_shape),
        scratch_shapes=list(scratch),
        name=name,
        compiler_params=pltpu.CompilerParams(vmem_limit_bytes=VMEM_LIMIT),
    )(*operands)


def prepare_kernel(
    capacity,
    group,
    q_ref,
    it_ref,
    ng_ref,
    id_ref,
    ng_id_ref,
    ng_count_ref,
    owner_ref,
    slot_ref,
    block_ref,
    out_ref,
    sh_ref,
):
    rows, negs = q_ref.shape[0], ng_ref.shape[0]
    keys = rows + negs
    extra = block_ref.shape[0] - rows - keys
    sh_ref[:, 0:rows] = -jnp.log(rows * group * sample_chance(id_ref[...]))
    sh_ref[:, rows:] = jnp.log(ng_count_ref[...].astype(F32)) - jnp.log(
        negs * group * sample_chance(ng_id_ref[...])
    )
    block_ref[0:rows, :] = q_ref[...]
    block_ref[rows : 2 * rows, :] = it_ref[...]
    block_ref[2 * rows : rows + keys, :] = ng_ref[...]
    block_ref[rows + keys :, :] = jnp.zeros((extra, block_ref.shape[1]), BF16)
    block_ref[rows + keys :, 0:keys] = split_rows(sh_ref[...], extra).astype(BF16)

    count = it_ref.shape[0]
    own_row = owner_ref[...].astype(F32)
    own_col = to_column(own_row)
    earlier = lax.broadcasted_iota(jnp.int32, (count, count), 0) < lax.broadcasted_iota(
        jnp.int32, (count, count), 1
    )
    rank = jnp.sum(
        jnp.where(jnp.logical_and(own_col == own_row, earlier), 1.0, 0.0), axis=0, keepdims=True
    )
    target = (own_row * capacity + rank).astype(jnp.int32)
    places = out_ref.shape[0]
    chosen = jnp.where(
        lax.broadcasted_iota(jnp.int32, (places, count), 0) == target, 1.0, 0.0
    ).astype(BF16)
    slot = slot_ref[...]
    high = to_column((slot >> 5).astype(F32))
    low = to_column((slot & 31).astype(F32))
    lane = lax.broadcasted_iota(jnp.int32, (count, 128), 1)
    details = jnp.where(
        lane == 0, high, jnp.where(lane == 1, low, jnp.where(lane == 2, 1.0, 0.0))
    )
    width = it_ref.shape[1]
    out_ref[:, 0:width] = dot_plain(chosen, it_ref[...]).astype(BF16)
    out_ref[:, width:] = dot_plain(chosen, details.astype(BF16)).astype(BF16)


def update_kernel(got_ref, mem_ref, new_ref):
    places, width = got_ref.shape[0], mem_ref.shape[1]
    rows = mem_ref.shape[0]
    details = jnp.transpose(got_ref[:, width:].astype(F32))
    slot = details[0:1, :] * 32.0 + details[1:2, :]
    slot = jnp.where(details[2:3, :] > 0.5, slot, -1.0).astype(jnp.int32)
    entry = lax.broadcasted_iota(jnp.int32, (1, places), 1).astype(F32)
    step = 256
    for start in range(0, rows, step):
        row = lax.broadcasted_iota(jnp.int32, (step, places), 0) + start
        latest = jnp.max(jnp.where(row == slot, entry, -1.0), axis=1, keepdims=True)
        chosen = jnp.where(entry == latest, 1.0, 0.0).astype(BF16)
        fresh = dot_plain(chosen, got_ref[:, 0:width])
        old = mem_ref[start : start + step, :].astype(F32)
        new_ref[start : start + step, :] = jnp.where(latest >= 0.0, fresh, old).astype(BF16)


def memory_kernel(tile, *refs):
    q_ref, *mem_refs, out_ref = refs
    block = 128
    extra = out_ref.shape[1] - block
    step = 1024
    pieces, open_piece = [], []
    for ref in mem_refs:
        for at in range(0, ref.shape[0], step):
            open_piece.append(ref[at : at + step, :])
            if sum(p.shape[0] for p in open_piece) >= step:
                pieces.append(jnp.concatenate(open_piece, axis=0))
                open_piece = []

    def one_tile(n, carry):
        q = q_ref[pl.ds(pl.multiple_of(n * tile, tile), tile), :]
        top = jnp.full((tile, 1), -jnp.inf, F32)
        total = jnp.zeros((tile, 1), F32)
        acc = jnp.zeros(q.shape, F32)
        following = dot_rows(q, pieces[0])
        for k, rows in enumerate(pieces):
            s = following
            if k + 1 < len(pieces):
                following = dot_rows(q, pieces[k + 1])
            newest = jnp.maximum(top, jnp.max(s, axis=1, keepdims=True))
            p = jnp.exp(s - newest)
            scale = jnp.exp(top - newest)
            total = total * scale + jnp.sum(p, axis=1, keepdims=True)
            acc = acc * scale + dot_plain(p.astype(BF16), rows)
            top = newest
        average = (acc / total).astype(BF16)
        lse = top + jnp.log(total)
        for h in range(tile // block):
            at = n * (tile // block) + h
            out_ref[at, 0:block, :] = average[h * block : (h + 1) * block, :]
            lse_row = to_row(lse[h * block : (h + 1) * block, :])
            out_ref[at, block:, 0:block] = split_rows(lse_row, extra).astype(BF16)
            out_ref[at, block:, block:] = jnp.zeros((extra, q.shape[1] - block), BF16)
        return carry

    lax.fori_loop(0, q_ref.shape[0] // tile, one_tile, 0)


def batch_kernel(g_ref, q_ref, it_ref, sh_ref, out_ref, stat_ref, s_ref):
    peers = g_ref.shape[0]
    rows = q_ref.shape[0]
    keys = sh_ref.shape[1]
    q = q_ref[...]
    highest = None
    for k in range(peers):
        shift = joined(g_ref[k, rows + keys :, 0:keys])
        s = dot_rows(q, g_ref[k, rows : rows + keys, :]) + shift
        s_ref[k] = s
        highest = s if highest is None else jnp.maximum(highest, s)
    top = jnp.max(highest, axis=1, keepdims=True)
    total = jnp.zeros((rows, keys), F32)
    acc = jnp.zeros(q.shape, F32)
    for k in range(peers):
        p = jnp.exp(s_ref[k] - top)
        total = total + p
        acc = acc + dot_plain(p.astype(BF16), g_ref[k, rows : rows + keys, :])
    total = jnp.sum(total, axis=1, keepdims=True)
    out_ref[...] = acc / total
    stat_ref[0:1, :] = to_row(top + jnp.log(total))
    own = dot_rows(q, it_ref[...]) + sh_ref[:, 0:rows]
    stat_ref[1:2, :] = jnp.sum(jnp.where(eye(rows), own, 0.0), axis=0, keepdims=True)


def total_kernel(parts_ref, stat_ref, total_ref, loss_ref):
    rows = total_ref.shape[1]
    shards = parts_ref.shape[0]
    batch = stat_ref[0:1, :]
    lse = [joined(parts_ref[k, rows:, 0:rows]) for k in range(shards)]
    top = batch
    for row in lse:
        top = jnp.maximum(top, row)
    summed = jnp.exp(batch - top)
    for row in lse:
        summed = summed + jnp.exp(row - top)
    log_total = top + jnp.log(summed)
    total_ref[...] = log_total
    loss_ref[...] = log_total - stat_ref[1:2, :]


def item_kernel(g_ref, lt_ref, q_ref, it_ref, ng_ref, sh_ref, item_ref, neg_ref):
    peers = g_ref.shape[0]
    rows = q_ref.shape[0]
    items, negs = it_ref[...], ng_ref[...]
    shift_items = to_column(sh_ref[:, 0:rows])
    shift_negs = to_column(sh_ref[:, rows:])
    item_acc = jnp.zeros(items.shape, F32)
    neg_acc = jnp.zeros(negs.shape, F32)
    for k in range(peers):
        queries = g_ref[k, 0:rows, :]
        log_total = lt_ref[k : k + 1, :]
        w = jnp.exp(dot_rows(items, queries) + shift_items - log_total).astype(BF16)
        item_acc = item_acc + dot_plain(w, queries)
        w = jnp.exp(dot_rows(negs, queries) + shift_negs - log_total).astype(BF16)
        neg_acc = neg_acc + dot_plain(w, queries)
    item_ref[...] = item_acc - q_ref[...].astype(F32)
    neg_ref[...] = neg_acc


def query_kernel(parts_ref, lt_ref, batch_ref, stat_ref, it_ref, out_ref):
    log_total = lt_ref[...]
    rows = log_total.shape[1]
    out = batch_ref[...] * to_column(jnp.exp(stat_ref[0:1, :] - log_total))
    for k in range(parts_ref.shape[0]):
        share = to_column(jnp.exp(joined(parts_ref[k, rows:, 0:rows]) - log_total))
        out = out + parts_ref[k, 0:rows, :].astype(F32) * share
    out_ref[...] = out - it_ref[...].astype(F32)


def local(
    query_vectors,
    item_vectors,
    negative_vectors,
    item_ids,
    negative_ids,
    negative_counts,
    memory,
    owners,
    memory_slots,
):
    rows, width = query_vectors.shape
    negatives = negative_vectors.shape[0]
    keys = rows + negatives
    mem = memory[0]
    half = mem.shape[0] // 2
    group = lax.axis_size("dp")
    shards = lax.axis_size("zh")
    depth = shards * lax.axis_size("zl")
    cycle = depth * lax.axis_size("yh")
    column = ("yh", "zh", "zl")

    def moved(block, over, by):
        route = [
            (y * depth + z, ((y + over) % 2) * depth + (z + by) % depth)
            for y in range(cycle // depth)
            for z in range(depth)
        ]
        return lax.ppermute(block, column, route)

    def collected(block, axis):
        count = lax.axis_size(axis)
        return lax.all_to_all(
            jnp.broadcast_to(block[None], (count,) + block.shape), axis, 0, 0, tiled=True
        )

    column_queries = collected(query_vectors, "zh").reshape(-1, width)
    first, second = mem[:half], mem[half:]
    memory_blocks = [
        mem,
        moved(mem, 1, 0),
        moved(first, 0, -1),
        moved(second, 0, 1),
        moved(first, 1, -1),
        moved(second, 1, 1),
    ]

    capacity = max(2, 2 * rows // cycle)
    block, outgoing, shift = call(
        lambda *refs: prepare_kernel(capacity, group, *refs),
        (
            query_vectors,
            item_vectors,
            negative_vectors,
            item_ids[None, :],
            negative_ids[None, :],
            negative_counts[None, :],
            owners.reshape(1, rows),
            memory_slots[None, :],
        ),
        (
            jax.ShapeDtypeStruct((rows + keys + 16, width), BF16),
            jax.ShapeDtypeStruct((cycle * capacity, width + 128), BF16),
            jax.ShapeDtypeStruct((1, keys), F32),
        ),
        "prepare",
    )
    gathered = lax.all_gather(block, "dp", axis=0, tiled=False)

    column_queries, outgoing, *memory_blocks = lax.optimization_barrier(
        (column_queries, outgoing, *memory_blocks)
    )
    arrived = lax.all_to_all(
        outgoing.reshape(cycle, capacity, width + 128), column, 0, 0, tiled=True
    )
    (parts,) = call(
        lambda *refs: memory_kernel(512, *refs),
        (column_queries, *memory_blocks),
        (jax.ShapeDtypeStruct((shards, rows + 16, width), BF16),),
        "memory",
    )
    parts, arrived = lax.optimization_barrier((parts, arrived))
    parts_back = lax.all_to_all(parts, "zh", 0, 0, tiled=True)

    batch_part, batch_stat = call(
        batch_kernel,
        (gathered, query_vectors, item_vectors, shift),
        (
            jax.ShapeDtypeStruct((rows, width), F32),
            jax.ShapeDtypeStruct((2, rows), F32),
        ),
        "batch",
        [pltpu.VMEM((group, rows, keys), F32)],
    )
    (updated,) = call(
        update_kernel,
        (arrived.reshape(cycle * capacity, width + 128), mem),
        (jax.ShapeDtypeStruct(mem.shape, BF16),),
        "update",
    )
    parts_back, updated, batch_part, batch_stat = lax.optimization_barrier(
        (parts_back, updated, batch_part, batch_stat)
    )
    log_total, loss = call(
        total_kernel,
        (parts_back, batch_stat),
        (jax.ShapeDtypeStruct((1, rows), F32), jax.ShapeDtypeStruct((1, rows), F32)),
        "total",
    )
    group_totals = collected(log_total, "dp").reshape(group, rows)
    (query_grad,) = call(
        query_kernel,
        (parts_back, log_total, batch_part, batch_stat, item_vectors),
        (jax.ShapeDtypeStruct((rows, width), F32),),
        "queries",
    )
    group_totals, query_grad = lax.optimization_barrier((group_totals, query_grad))
    item_grad, negative_grad = call(
        item_kernel,
        (gathered, group_totals, query_vectors, item_vectors, negative_vectors, shift),
        (
            jax.ShapeDtypeStruct((rows, width), F32),
            jax.ShapeDtypeStruct((negatives, width), F32),
        ),
        "items",
    )
    return (loss[0], query_grad, item_grad, negative_grad, updated[None])


def solution(mesh):
    cycle, group = mesh.shape["mem"], mesh.shape["dp"]
    cut = Mesh(
        mesh.devices.reshape(2, cycle // 4, 2, group), ("yh", "zh", "zl", "dp")
    )
    spread = ("yh", "zh", "zl", "dp")
    column = ("yh", "zh", "zl")
    return jax.shard_map(
        local,
        mesh=cut,
        in_specs=(
            P(spread, None),
            P(spread, None),
            P(spread, None),
            P(spread),
            P(spread),
            P(spread),
            P("dp", column, None),
            P(spread, None),
            P(spread),
        ),
        out_specs=(
            P(spread),
            P(spread, None),
            P(spread, None),
            P(spread, None),
            P("dp", column, None),
        ),
        check_vma=False,
    )
```

time: 184 us -> 164 us (0.89)
  the two profiles are of different devices: /device:TPU:1 before, /device:TPU:33 now
where the time goes in v2:
time: 164 us; the launch traced here: 163 us
  waiting for transfers between devices  62.5 us (38%)
  starting transfers between devices  54.3 us (33%)
  Pallas kernels  26.4 us (16%)
  between operations  14.2 us (9%)
  local copies, waits for them, and re-layouts  5.38 us (3%)
    pallas_call x7, Pallas kernels, call(): pl.pallas_call(kernel, out_shape=out_shape, in_specs=[here] * len(operand...  26.4 us
    all_to_all x1, waiting for transfers between devices, local(): parts_back = lax.all_to_all(parts, 'zh', 0, 0, tiled=True)  25.6 us
    ppermute x5, waiting for transfers between devices, moved(): return lax.ppermute(block, column, route)  23.5 us
    all_to_all x2, starting transfers between devices, collected(): lax.all_to_all(jnp.broadcast_to(block[None], (count,) + block.shape), axi...  20.6 us
    ppermute x5, starting transfers between devices, moved(): return lax.ppermute(block, column, route)  18.2 us
    all_to_all x1, starting transfers between devices, local(): lax.all_to_all(outgoing.reshape(cycle, capacity, width + 128), column, 0,...  11.9 us
    all_to_all x1, waiting for transfers between devices, local(): lax.all_to_all(outgoing.reshape(cycle, capacity, width + 128), column, 0,...  9.96 us
    all_to_all x1, starting transfers between devices, local(): parts_back = lax.all_to_all(parts, 'zh', 0, 0, tiled=True)  3.54 us
  transfers between devices with their start and end apart: 10, of which 5 were waited for; matrix products, arithmetic and copies ran while one was open for 2% of the time, Pallas kernels for 11%

profile of v2, /device:TPU:33, one launch (start us, length us, event | category | flops | bytes accessed | tf_op | source)
XLA Modules:
  0.0 162.7 jit_solution(12125829426861863086)
XLA Ops:
  7.2 0.0 all-gather.3.cloned.1.call-start
  7.2 1.9 %prepare.1 = (bf16[336,256]{1,0:T(8,128)(2,1)}, bf16[256,384]{1,0:T(8,128)(2,1)}, f32[1,192]{1,0:T(1,128)}) custom-call(bf16[128,256]{1,0:T(8,128)(2,1)} %q_ref.3, bf16[128,256]{1,0:T(8,128)(2,1)} %it_ref.5, bf16[64,256]{1,0:T(8,128)(2,1)} %ng_ref.1, s32[1,128]{1,0:T(1,128)} %bitcast.28, s32[1,64]{1,0:T(1,128)} %bitcast.29, s32[1,64]{1,0:T(1,128)} %bitcast.30, ...), custom_call_target="tpu_custom_call" | custom-call | tf_op jit(solution)/shard_map/prepare/pallas_call | solution.py:59
  9.1 0.0 all-gather.3.cloned.1.call-update
  9.1 1.7 %broadcast_in_dim.29 = bf16[8,128,256]{2,1,0:T(8,128)(2,1)} broadcast(bf16[128,256]{1,0:T(8,128)(2,1)} %q_ref.3), dimensions={1,2} | broadcast | bytes 589824 | tf_op jit(solution)/shard_map/broadcast_in_dim | solution.py:286
  10.8 13.9 %all-to-all-start = ((bf16[8,128,256]{2,1,0:T(8,128)(2,1)}), bf16[8,128,256]{2,1,0:T(8,128)(2,1)S(1)}, u32[]{:S(2)}, u32[]{:S(2)}) async-start(bf16[8,128,256]{2,1,0:T(8,128)(2,1)} %broadcast_in_dim.29), calls=%async_computation | async-start | bytes 1048576 | tf_op jit(solution)/shard_map/all_to_all | solution.py:285
  24.7 4.8 %collective-permute-start = (bf16[1024,256]{1,0:T(8,128)(2,1)}, bf16[1024,256]{1,0:T(8,128)(2,1)S(1)}, u32[]{:S(2)}, u32[]{:S(2)}) collective-permute-start(bf16[1024,256]{1,0:T(8,128)(2,1)} %bitcast.20), channel_id=1, source_target_pairs={{0,256},{16,272},{32,288},{48,304},{64,320},{80,336},{96,352},{112... | collective-permute-start | bytes 1572872 | tf_op jit(solution)/shard_map/ppermute | solution.py:281
  29.5 1.1 slice_bitcast_fusion
  30.6 2.6 %collective-permute-start.1 = (bf16[512,256]{1,0:T(8,128)(2,1)S(1)}, bf16[512,256]{1,0:T(8,128)(2,1)S(1)}, u32[]{:S(2)}, u32[]{:S(2)}) collective-permute-start(bf16[512,256]{1,0:T(8,128)(2,1)S(1)} %get-tuple-element.56), channel_id=1, source_target_pairs={{0,240},{16,0},{32,16},{48,32},{64,48},{80,64},{96,80},{112,96},{1... | collective-permute-start | bytes 786440 | tf_op jit(solution)/shard_map/ppermute | solution.py:281
  33.2 3.1 %collective-permute-start.2 = (bf16[512,256]{1,0:T(8,128)(2,1)S(1)}, bf16[512,256]{1,0:T(8,128)(2,1)S(1)}, u32[]{:S(2)}, u32[]{:S(2)}) collective-permute-start(bf16[512,256]{1,0:T(8,128)(2,1)S(1)} %get-tuple-element.55), channel_id=1, source_target_pairs={{0,16},{16,32},{32,48},{48,64},{64,80},{80,96},{96,112},{112,128},... | collective-permute-start | bytes 786440 | tf_op jit(solution)/shard_map/ppermute | solution.py:281
  36.3 3.6 %collective-permute-start.3 = (bf16[512,256]{1,0:T(8,128)(2,1)S(1)}, bf16[512,256]{1,0:T(8,128)(2,1)S(1)}, u32[]{:S(2)}, u32[]{:S(2)}) collective-permute-start(bf16[512,256]{1,0:T(8,128)(2,1)S(1)} %get-tuple-element.56), channel_id=1, source_target_pairs={{0,496},{16,256},{32,272},{48,288},{64,304},{80,320},{96,336},{112... | collective-permute-start | bytes 786440 | tf_op jit(solution)/shard_map/ppermute | solution.py:281
  40.0 4.1 %collective-permute-start.4 = (bf16[512,256]{1,0:T(8,128)(2,1)S(1)}, bf16[512,256]{1,0:T(8,128)(2,1)S(1)}, u32[]{:S(2)}, u32[]{:S(2)}) collective-permute-start(bf16[512,256]{1,0:T(8,128)(2,1)S(1)} %get-tuple-element.55), channel_id=1, source_target_pairs={{0,272},{16,288},{32,304},{48,320},{64,336},{80,352},{96,368},{112... | collective-permute-start | bytes 786440 | tf_op jit(solution)/shard_map/ppermute | solution.py:281
  44.0 11.1 %collective-permute-done.1.refs_3_ = bf16[512,256]{1,0:T(8,128)(2,1)S(1)} collective-permute-done((bf16[512,256]{1,0:T(8,128)(2,1)S(1)}, bf16[512,256]{1,0:T(8,128)(2,1)S(1)}, u32[]{:S(2)}, u32[]{:S(2)}) %collective-permute-start.1) | collective-permute-done | bytes 262176 | tf_op jit(solution)/shard_map/ppermute | solution.py:281
  55.1 0.0 copy-start.4
  55.1 0.0 collective-permute-done.2.refs_4_
  55.1 0.0 copy-start.5
  55.1 12.4 %collective-permute-done.3.refs_5_ = bf16[512,256]{1,0:T(8,128)(2,1)S(1)} collective-permute-done((bf16[512,256]{1,0:T(8,128)(2,1)S(1)}, bf16[512,256]{1,0:T(8,128)(2,1)S(1)}, u32[]{:S(2)}, u32[]{:S(2)}) %collective-permute-start.3) | collective-permute-done | bytes 262176 | tf_op jit(solution)/shard_map/ppermute | solution.py:281
  67.5 0.0 copy-start.6
  67.5 0.0 collective-permute-done.4.refs_6_
  67.5 0.0 copy-start.7
  67.5 0.0 collective-permute-done.refs_2_
  67.5 0.0 copy-start.3
  67.5 0.0 all-to-all-done
  67.6 0.0 copy-start.1
  67.6 11.9 %all-to-all-start.1 = ((bf16[32,8,384]{2,1,0:T(8,128)(2,1)}), bf16[32,8,384]{2,1,0:T(8,128)(2,1)S(1)}, u32[]{:S(2)}, u32[]{:S(2)}) async-start(bf16[32,8,384]{2,1,0:T(8,128)(2,1)} %bitcast.9), calls=%async_computation.1 | async-start | bytes 393216 | tf_op jit(solution)/shard_map/all_to_all | solution.py:325
  79.5 0.0 copy-done.4
  79.5 0.0 copy-done.5
  79.5 0.0 copy-done.6
  79.5 0.0 copy-done.7
  79.5 0.0 copy-done.3
  79.5 0.0 copy-done.1
  79.5 9.0 %memory.1 = bf16[8,144,256]{2,1,0:T(8,128)(2,1)} custom-call(bf16[1024,256]{1,0:T(8,128)(2,1)} %bitcast.23, bf16[1024,256]{1,0:T(8,128)(2,1)} %bitcast.21, bf16[1024,256]{1,0:T(8,128)(2,1)} %copy-done.3, bf16[512,256]{1,0:T(8,128)(2,1)} %copy-done.4, bf16[512,256]{1,0:T(8,128)(2,1)} %copy-done.5, bf16[512,256]{1,0:T(8,128)(2,1)} %copy-done.6, ...), custom_call_target="tpu_custom_call" | custom-call | tf_op jit(solution)/shard_map/memory/pallas_call | solution.py:59
  88.5 10.0 %all-to-all-done.1 = bf16[32,8,384]{2,1,0:T(8,128)(2,1)S(1)} async-done(((bf16[32,8,384]{2,1,0:T(8,128)(2,1)}), bf16[32,8,384]{2,1,0:T(8,128)(2,1)S(1)}, u32[]{:S(2)}, u32[]{:S(2)}) %all-to-all-start.1) | async-done | bytes 196640 | tf_op jit(solution)/shard_map/all_to_all | solution.py:325
  98.4 0.0 copy-start.2
  98.4 3.5 %all-to-all-start.2 = ((bf16[8,144,256]{2,1,0:T(8,128)(2,1)}), bf16[8,144,256]{2,1,0:T(8,128)(2,1)S(1)}, u32[]{:S(2)}, u32[]{:S(2)}) async-start(bf16[8,144,256]{2,1,0:T(8,128)(2,1)} %memory.1), calls=%async_computation.2 | async-start | bytes 1179648 | tf_op jit(solution)/shard_map/all_to_all | solution.py:335
  102.0 0.0 copy-done.2
  102.0 2.4 %update.1 = bf16[1024,256]{1,0:T(8,128)(2,1)} custom-call(bf16[256,384]{1,0:T(8,128)(2,1)} %bitcast.24, bf16[1024,256]{1,0:T(8,128)(2,1)} %bitcast.22), custom_call_target="tpu_custom_call" | custom-call | tf_op jit(solution)/shard_map/update/pallas_call | solution.py:59
  104.4 0.0 all-gather.3.cloned.1.call-done
  104.4 4.3 %batch.1 = (f32[128,256]{1,0:T(8,128)}, f32[2,128]{1,0:T(2,128)}) custom-call(bf16[16,336,256]{2,1,0:T(8,128)(2,1)} %bitcast.18, bf16[128,256]{1,0:T(8,128)(2,1)} %q_ref.3, bf16[128,256]{1,0:T(8,128)(2,1)} %it_ref.5, f32[1,192]{1,0:T(1,128)} %get-tuple-element.42.sh_ref), custom_call_target="tpu_custom_call" | custom-call | tf_op jit(solution)/shard_map/batch/pallas_call | solution.py:59
  108.6 25.6 %all-to-all-done.2.parts_ref = bf16[8,144,256]{2,1,0:T(8,128)(2,1)S(1)} async-done(((bf16[8,144,256]{2,1,0:T(8,128)(2,1)}), bf16[8,144,256]{2,1,0:T(8,128)(2,1)S(1)}, u32[]{:S(2)}, u32[]{:S(2)}) %all-to-all-start.2) | async-done | bytes 589856 | tf_op jit(solution)/shard_map/all_to_all | solution.py:335
  134.3 0.0 copy-start
  134.3 0.8 copy-done
  135.1 1.6 total.1
  136.7 1.2 broadcast_in_dim.35
  137.9 6.7 %all-to-all-start.3 = ((f32[16,1,128]{2,1,0:T(1,128)}), f32[16,1,128]{2,1,0:T(1,128)S(1)}, u32[]{:S(2)}, u32[]{:S(2)}) async-start(f32[16,1,128]{2,1,0:T(1,128)} %broadcast_in_dim.35), calls=%async_computation.3 | async-start | bytes 16384 | tf_op jit(solution)/shard_map/all_to_all | solution.py:285
  144.6 2.0 %queries.1 = f32[128,256]{1,0:T(8,128)} custom-call(bf16[8,144,256]{2,1,0:T(8,128)(2,1)} %copy-done, f32[1,128]{1,0:T(1,128)} %get-tuple-element.48.lt_ref, f32[128,256]{1,0:T(8,128)} %get-tuple-element.49.batch_ref, f32[2,128]{1,0:T(2,128)} %get-tuple-element.46.stat_ref, bf16[128,256]{1,0:T(8,128)(2,1)} %it_ref.5), custom_call_target="tpu_custom_call" | custom-call | tf_op jit(solution)/shard_map/queries/pallas_call | solution.py:59
  146.6 3.4 %all-to-all-done.3 = f32[16,1,128]{2,1,0:T(1,128)S(1)} async-done(((f32[16,1,128]{2,1,0:T(1,128)}), f32[16,1,128]{2,1,0:T(1,128)S(1)}, u32[]{:S(2)}, u32[]{:S(2)}) %all-to-all-start.3) | async-done | bytes 8224 | tf_op jit(solution)/shard_map/all_to_all | solution.py:285
  150.0 0.0 copy-start.8
  150.0 0.6 copy-done.8
  150.6 5.3 %items.1 = (f32[128,256]{1,0:T(8,128)}, f32[64,256]{1,0:T(8,128)}) custom-call(bf16[16,336,256]{2,1,0:T(8,128)(2,1)} %bitcast.19, f32[16,128]{1,0:T(8,128)} %bitcast.26, bf16[128,256]{1,0:T(8,128)(2,1)} %q_ref.3, bf16[128,256]{1,0:T(8,128)(2,1)} %it_ref.5, bf16[64,256]{1,0:T(8,128)(2,1)} %ng_ref.1, f32[1,192]{1,0:T(1,128)} %get-tuple-element.42.sh_ref), custom_call_target="tpu_custom_call" | custom-call | tf_op jit(solution)/shard_map/items/pallas_call | solution.py:59
Async XLA Ops:
  7.2 97.2 %all-gather.3.cloned.1.call-start = ((), (), s32[]{:S(2)}) async-start(), calls=%async_computation.4 | async-start | bytes 2924544 | tf_op jit(solution)/shard_map/all_gather | solution.py:320
  10.8 56.8 %all-to-all-start = ((bf16[8,128,256]{2,1,0:T(8,128)(2,1)}), bf16[8,128,256]{2,1,0:T(8,128)(2,1)S(1)}, u32[]{:S(2)}, u32[]{:S(2)}) async-start(bf16[8,128,256]{2,1,0:T(8,128)(2,1)} %broadcast_in_dim.29), calls=%async_computation | async-start | bytes 1048576 | tf_op jit(solution)/shard_map/all_to_all | solution.py:285
  24.7 42.8 %collective-permute-start = (bf16[1024,256]{1,0:T(8,128)(2,1)}, bf16[1024,256]{1,0:T(8,128)(2,1)S(1)}, u32[]{:S(2)}, u32[]{:S(2)}) collective-permute-start(bf16[1024,256]{1,0:T(8,128)(2,1)} %bitcast.20), channel_id=1, source_target_pairs={{0,256},{16,272},{32,288},{48,304},{64,320},{80,336},{96,352},{112... | collective-permute-start | bytes 1572872 | tf_op jit(solution)/shard_map/ppermute | solution.py:281
  30.6 24.5 %collective-permute-start.1 = (bf16[512,256]{1,0:T(8,128)(2,1)S(1)}, bf16[512,256]{1,0:T(8,128)(2,1)S(1)}, u32[]{:S(2)}, u32[]{:S(2)}) collective-permute-start(bf16[512,256]{1,0:T(8,128)(2,1)S(1)} %get-tuple-element.56), channel_id=1, source_target_pairs={{0,240},{16,0},{32,16},{48,32},{64,48},{80,64},{96,80},{112,96},{1... | collective-permute-start | bytes 786440 | tf_op jit(solution)/shard_map/ppermute | solution.py:281
  33.2 21.9 %collective-permute-start.2 = (bf16[512,256]{1,0:T(8,128)(2,1)S(1)}, bf16[512,256]{1,0:T(8,128)(2,1)S(1)}, u32[]{:S(2)}, u32[]{:S(2)}) collective-permute-start(bf16[512,256]{1,0:T(8,128)(2,1)S(1)} %get-tuple-element.55), channel_id=1, source_target_pairs={{0,16},{16,32},{32,48},{48,64},{64,80},{80,96},{96,112},{112,128},... | collective-permute-start | bytes 786440 | tf_op jit(solution)/shard_map/ppermute | solution.py:281
  36.3 31.2 %collective-permute-start.3 = (bf16[512,256]{1,0:T(8,128)(2,1)S(1)}, bf16[512,256]{1,0:T(8,128)(2,1)S(1)}, u32[]{:S(2)}, u32[]{:S(2)}) collective-permute-start(bf16[512,256]{1,0:T(8,128)(2,1)S(1)} %get-tuple-element.56), channel_id=1, source_target_pairs={{0,496},{16,256},{32,272},{48,288},{64,304},{80,320},{96,336},{112... | collective-permute-start | bytes 786440 | tf_op jit(solution)/shard_map/ppermute | solution.py:281
  40.0 27.5 %collective-permute-start.4 = (bf16[512,256]{1,0:T(8,128)(2,1)S(1)}, bf16[512,256]{1,0:T(8,128)(2,1)S(1)}, u32[]{:S(2)}, u32[]{:S(2)}) collective-permute-start(bf16[512,256]{1,0:T(8,128)(2,1)S(1)} %get-tuple-element.55), channel_id=1, source_target_pairs={{0,272},{16,288},{32,304},{48,320},{64,336},{80,352},{96,368},{112... | collective-permute-start | bytes 786440 | tf_op jit(solution)/shard_map/ppermute | solution.py:281
  55.1 24.4 %copy-start.4 = (bf16[512,256]{1,0:T(8,128)(2,1)}, bf16[512,256]{1,0:T(8,128)(2,1)S(1)}, u32[]{:S(2)}) copy-start(bf16[512,256]{1,0:T(8,128)(2,1)S(1)} %collective-permute-done.1.refs_3_) | copy-start | bytes 786436
  55.1 24.4 %copy-start.5 = (bf16[512,256]{1,0:T(8,128)(2,1)}, bf16[512,256]{1,0:T(8,128)(2,1)S(1)}, u32[]{:S(2)}) copy-start(bf16[512,256]{1,0:T(8,128)(2,1)S(1)} %collective-permute-done.2.refs_4_) | copy-start | bytes 786436
  67.5 12.0 %copy-start.6 = (bf16[512,256]{1,0:T(8,128)(2,1)}, bf16[512,256]{1,0:T(8,128)(2,1)S(1)}, u32[]{:S(2)}) copy-start(bf16[512,256]{1,0:T(8,128)(2,1)S(1)} %collective-permute-done.3.refs_5_) | copy-start | bytes 786436
  67.5 12.0 %copy-start.7 = (bf16[512,256]{1,0:T(8,128)(2,1)}, bf16[512,256]{1,0:T(8,128)(2,1)S(1)}, u32[]{:S(2)}) copy-start(bf16[512,256]{1,0:T(8,128)(2,1)S(1)} %collective-permute-done.4.refs_6_) | copy-start | bytes 786436
  67.5 12.0 %copy-start.3 = (bf16[1024,256]{1,0:T(8,128)(2,1)}, bf16[1024,256]{1,0:T(8,128)(2,1)S(1)}, u32[]{:S(2)}) copy-start(bf16[1024,256]{1,0:T(8,128)(2,1)S(1)} %collective-permute-done.refs_2_) | copy-start | bytes 1572868
  67.6 12.0 %copy-start.1 = (bf16[8,128,256]{2,1,0:T(8,128)(2,1)}, bf16[8,128,256]{2,1,0:T(8,128)(2,1)S(1)}, u32[]{:S(2)}) copy-start(bf16[8,128,256]{2,1,0:T(8,128)(2,1)S(1)} %all-to-all-done) | copy-start | bytes 1572868
  67.6 30.9 %all-to-all-start.1 = ((bf16[32,8,384]{2,1,0:T(8,128)(2,1)}), bf16[32,8,384]{2,1,0:T(8,128)(2,1)S(1)}, u32[]{:S(2)}, u32[]{:S(2)}) async-start(bf16[32,8,384]{2,1,0:T(8,128)(2,1)} %bitcast.9), calls=%async_computation.1 | async-start | bytes 393216 | tf_op jit(solution)/shard_map/all_to_all | solution.py:325
  98.4 3.5 %copy-start.2 = (bf16[32,8,384]{2,1,0:T(8,128)(2,1)}, bf16[32,8,384]{2,1,0:T(8,128)(2,1)S(1)}, u32[]{:S(2)}) copy-start(bf16[32,8,384]{2,1,0:T(8,128)(2,1)S(1)} %all-to-all-done.1) | copy-start | bytes 589828
  98.4 35.8 %all-to-all-start.2 = ((bf16[8,144,256]{2,1,0:T(8,128)(2,1)}), bf16[8,144,256]{2,1,0:T(8,128)(2,1)S(1)}, u32[]{:S(2)}, u32[]{:S(2)}) async-start(bf16[8,144,256]{2,1,0:T(8,128)(2,1)} %memory.1), calls=%async_computation.2 | async-start | bytes 1179648 | tf_op jit(solution)/shard_map/all_to_all | solution.py:335
  134.3 0.8 copy-start
  137.9 12.1 %all-to-all-start.3 = ((f32[16,1,128]{2,1,0:T(1,128)}), f32[16,1,128]{2,1,0:T(1,128)S(1)}, u32[]{:S(2)}, u32[]{:S(2)}) async-start(f32[16,1,128]{2,1,0:T(1,128)} %broadcast_in_dim.35), calls=%async_computation.3 | async-start | bytes 16384 | tf_op jit(solution)/shard_map/all_to_all | solution.py:285
  150.0 0.6 copy-start.8
Sparse Core Ops, SparseCore 0:
  10.1 59.1 all-gather.2

commit v3 on v2

--- a/solution.py
+++ b/solution.py
@@ -56,10 +56,11 @@
 
 def call(kernel, operands, out_shape, name, scratch=()):
     here = pl.BlockSpec(memory_space=pltpu.VMEM)
+    scalars = pl.BlockSpec(memory_space=pltpu.SMEM)
     return pl.pallas_call(
         kernel,
         out_shape=out_shape,
-        in_specs=[here] * len(operands),
+        in_specs=[scalars if operand.shape == (3,) else here for operand in operands],
         out_specs=(here,) * len(out_shape),
         scratch_shapes=list(scratch),
         name=name,
@@ -70,6 +71,7 @@
 def prepare_kernel(
     capacity,
     group,
+    place_ref,
     q_ref,
     it_ref,
     ng_ref,
@@ -95,17 +97,24 @@
     block_ref[rows + keys :, :] = jnp.zeros((extra, block_ref.shape[1]), BF16)
     block_ref[rows + keys :, 0:keys] = split_rows(sh_ref[...], extra).astype(BF16)
 
+    pairs = out_ref.shape[0]
     count = it_ref.shape[0]
-    own_row = owner_ref[...].astype(F32)
+    own_int = owner_ref[...]
+    own_row = own_int.astype(F32)
     own_col = to_column(own_row)
     earlier = lax.broadcasted_iota(jnp.int32, (count, count), 0) < lax.broadcasted_iota(
         jnp.int32, (count, count), 1
     )
     rank = jnp.sum(
         jnp.where(jnp.logical_and(own_col == own_row, earlier), 1.0, 0.0), axis=0, keepdims=True
-    )
-    target = (own_row * capacity + rank).astype(jnp.int32)
-    places = out_ref.shape[0]
+    ).astype(jnp.int32)
+    half = own_int // (2 * pairs)
+    depth = own_int - half * (2 * pairs)
+    pair = depth // 2
+    parity = depth - pair * 2
+    other = jnp.where(half == place_ref[0], 0, 2) + jnp.where(parity == place_ref[1], 0, 1)
+    target = (pair * 4 + other) * capacity + rank
+    places = pairs * 4 * capacity
     chosen = jnp.where(
         lax.broadcasted_iota(jnp.int32, (places, count), 0) == target, 1.0, 0.0
     ).astype(BF16)
@@ -116,24 +125,61 @@
     details = jnp.where(
         lane == 0, high, jnp.where(lane == 1, low, jnp.where(lane == 2, 1.0, 0.0))
     )
-    width = it_ref.shape[1]
-    out_ref[:, 0:width] = dot_plain(chosen, it_ref[...]).astype(BF16)
-    out_ref[:, width:] = dot_plain(chosen, details.astype(BF16)).astype(BF16)
-
-
-def update_kernel(got_ref, mem_ref, new_ref):
-    places, width = got_ref.shape[0], mem_ref.shape[1]
-    rows = mem_ref.shape[0]
-    details = jnp.transpose(got_ref[:, width:].astype(F32))
+    sent = dot_plain(chosen, it_ref[...]).astype(BF16)
+    sent_details = dot_plain(chosen, details.astype(BF16)).astype(BF16)
+    span = 4 * capacity
+    for k in range(pairs):
+        out_ref[k, 0:rows, :] = q_ref[...]
+        out_ref[k, rows : rows + span, :] = sent[k * span : (k + 1) * span, :]
+        middle = k * span + span // 2
+        out_ref[k, rows + span :, 0:128] = sent_details[k * span : middle, :]
+        out_ref[k, rows + span :, 128:256] = sent_details[middle : (k + 1) * span, :]
+
+
+def forward_kernel(rows, got_ref, *out_refs):
+    pairs = got_ref.shape[0]
+    span = (got_ref.shape[1] - rows) * 2 // 3
+    each = span // 4
+    width = got_ref.shape[2]
+    for k in range(0, pairs, 2):
+        items = [got_ref[k + n, rows : rows + span, :].astype(F32) for n in range(2)]
+        details = [got_ref[k + n, rows + span :, :].astype(F32) for n in range(2)]
+        for c, out_ref in enumerate(out_refs):
+            at, side = (c % 2) * each, (c // 2) * 128
+            out_ref[k * each : (k + 2) * each, 0:width] = jnp.concatenate(
+                [block[c * each : (c + 1) * each, :] for block in items], axis=0
+            ).astype(BF16)
+            out_ref[k * each : (k + 2) * each, width:] = jnp.concatenate(
+                [block[at : at + each, side : side + 128] for block in details], axis=0
+            ).astype(BF16)
+
+
+def update_kernel(pairs, place_ref, got0_ref, got1_ref, got2_ref, got3_ref, mem_ref, new_ref):
+    rows, width = mem_ref.shape
+    got = jnp.concatenate(
+        [ref[...] for ref in (got0_ref, got1_ref, got2_ref, got3_ref)], axis=0
+    )
+    places = got.shape[0]
+    each = places // (4 * pairs)
+    details = jnp.transpose(got[:, width:].astype(F32))
     slot = details[0:1, :] * 32.0 + details[1:2, :]
     slot = jnp.where(details[2:3, :] > 0.5, slot, -1.0).astype(jnp.int32)
-    entry = lax.broadcasted_iota(jnp.int32, (1, places), 1).astype(F32)
+    entry = lax.broadcasted_iota(jnp.int32, (1, places), 1)
+    other = entry // (pairs * each)
+    inside = entry - other * (pairs * each)
+    pair = inside // each
+    rank = inside - pair * each
+    flipped = other // 2
+    half = jnp.where(flipped == 1, 1 - place_ref[0], place_ref[0])
+    parity = jnp.where(other - 2 * flipped == 1, 1 - place_ref[1], place_ref[1])
+    arrival = (((half * pairs + pair) * 2 + parity) * each + rank).astype(F32)
+    items = got[:, 0:width]
     step = 256
     for start in range(0, rows, step):
         row = lax.broadcasted_iota(jnp.int32, (step, places), 0) + start
-        latest = jnp.max(jnp.where(row == slot, entry, -1.0), axis=1, keepdims=True)
-        chosen = jnp.where(entry == latest, 1.0, 0.0).astype(BF16)
-        fresh = dot_plain(chosen, got_ref[:, 0:width])
+        latest = jnp.max(jnp.where(row == slot, arrival, -1.0), axis=1, keepdims=True)
+        chosen = jnp.where(arrival == latest, 1.0, 0.0).astype(BF16)
+        fresh = dot_plain(chosen, items)
         old = mem_ref[start : start + step, :].astype(F32)
         new_ref[start : start + step, :] = jnp.where(latest >= 0.0, fresh, old).astype(BF16)
 
@@ -152,7 +198,9 @@
                 open_piece = []
 
     def one_tile(n, carry):
-        q = q_ref[pl.ds(pl.multiple_of(n * tile, tile), tile), :]
+        q = jnp.concatenate(
+            [q_ref[n * (tile // block) + h, 0:block, :] for h in range(tile // block)], axis=0
+        )
         top = jnp.full((tile, 1), -jnp.inf, F32)
         total = jnp.zeros((tile, 1), F32)
         acc = jnp.zeros(q.shape, F32)
@@ -177,27 +225,28 @@
             out_ref[at, block:, block:] = jnp.zeros((extra, q.shape[1] - block), BF16)
         return carry
 
-    lax.fori_loop(0, q_ref.shape[0] // tile, one_tile, 0)
-
-
-def batch_kernel(g_ref, q_ref, it_ref, sh_ref, out_ref, stat_ref, s_ref):
-    peers = g_ref.shape[0]
+    lax.fori_loop(0, q_ref.shape[0] * block // tile, one_tile, 0)
+
+
+def batch_kernel(*refs):
+    *g_refs, q_ref, it_ref, sh_ref, out_ref, stat_ref, s_ref = refs
     rows = q_ref.shape[0]
     keys = sh_ref.shape[1]
+    blocks = [(ref, k) for ref in g_refs for k in range(ref.shape[0])]
     q = q_ref[...]
     highest = None
-    for k in range(peers):
-        shift = joined(g_ref[k, rows + keys :, 0:keys])
-        s = dot_rows(q, g_ref[k, rows : rows + keys, :]) + shift
-        s_ref[k] = s
+    for n, (ref, k) in enumerate(blocks):
+        shift = joined(ref[k, rows + keys :, 0:keys])
+        s = dot_rows(q, ref[k, rows : rows + keys, :]) + shift
+        s_ref[n] = s
         highest = s if highest is None else jnp.maximum(highest, s)
     top = jnp.max(highest, axis=1, keepdims=True)
     total = jnp.zeros((rows, keys), F32)
     acc = jnp.zeros(q.shape, F32)
-    for k in range(peers):
-        p = jnp.exp(s_ref[k] - top)
+    for n, (ref, k) in enumerate(blocks):
+        p = jnp.exp(s_ref[n] - top)
         total = total + p
-        acc = acc + dot_plain(p.astype(BF16), g_ref[k, rows : rows + keys, :])
+        acc = acc + dot_plain(p.astype(BF16), ref[k, rows : rows + keys, :])
     total = jnp.sum(total, axis=1, keepdims=True)
     out_ref[...] = acc / total
     stat_ref[0:1, :] = to_row(top + jnp.log(total))
@@ -221,23 +270,28 @@
     loss_ref[...] = log_total - stat_ref[1:2, :]
 
 
-def item_kernel(g_ref, lt_ref, q_ref, it_ref, ng_ref, sh_ref, item_ref, neg_ref):
-    peers = g_ref.shape[0]
+def item_kernel(*refs):
+    place_ref, *g_refs, lt_ref, q_ref, it_ref, ng_ref, sh_ref, item_ref, neg_ref = refs
     rows = q_ref.shape[0]
-    items, negs = it_ref[...], ng_ref[...]
-    shift_items = to_column(sh_ref[:, 0:rows])
-    shift_negs = to_column(sh_ref[:, rows:])
-    item_acc = jnp.zeros(items.shape, F32)
-    neg_acc = jnp.zeros(negs.shape, F32)
-    for k in range(peers):
-        queries = g_ref[k, 0:rows, :]
-        log_total = lt_ref[k : k + 1, :]
-        w = jnp.exp(dot_rows(items, queries) + shift_items - log_total).astype(BF16)
-        item_acc = item_acc + dot_plain(w, queries)
-        w = jnp.exp(dot_rows(negs, queries) + shift_negs - log_total).astype(BF16)
-        neg_acc = neg_acc + dot_plain(w, queries)
-    item_ref[...] = item_acc - q_ref[...].astype(F32)
-    neg_ref[...] = neg_acc
+    here = place_ref[2]
+    near = g_refs[0].shape[0]
+    peers = sum(ref.shape[0] for ref in g_refs)
+    keys = jnp.concatenate([it_ref[...], ng_ref[...]], axis=0)
+    shift = to_column(sh_ref[...])
+    acc = jnp.zeros(keys.shape, F32)
+    low = lax.rem(here, near)
+    blocks = [(ref, k) for ref in g_refs for k in range(ref.shape[0])]
+    for at in range(0, peers, 2):
+        base = lax.rem(here - low - (at // near) * near + peers, peers)
+        pair = blocks[at : at + 2]
+        queries = jnp.concatenate([ref[k, 0:rows, :] for ref, k in pair], axis=0)
+        log_total = jnp.concatenate(
+            [lt_ref[pl.ds(base + (low ^ ((at + n) % near)), 1), :] for n in range(2)], axis=1
+        )
+        w = jnp.exp(dot_rows(keys, queries) + shift - log_total).astype(BF16)
+        acc = acc + dot_plain(w, queries)
+    item_ref[...] = acc[0:rows, :] - q_ref[...].astype(F32)
+    neg_ref[...] = acc[rows:, :]
 
 
 def query_kernel(parts_ref, lt_ref, batch_ref, stat_ref, it_ref, out_ref):
@@ -265,42 +319,27 @@
     negatives = negative_vectors.shape[0]
     keys = rows + negatives
     mem = memory[0]
-    half = mem.shape[0] // 2
     group = lax.axis_size("dp")
     shards = lax.axis_size("zh")
     depth = shards * lax.axis_size("zl")
     cycle = depth * lax.axis_size("yh")
     column = ("yh", "zh", "zl")
 
-    def moved(block, over, by):
+    def beside(block, over, by):
         route = [
-            (y * depth + z, ((y + over) % 2) * depth + (z + by) % depth)
+            (y * depth + z, ((y + over) % 2) * depth + (z ^ by))
             for y in range(cycle // depth)
             for z in range(depth)
         ]
         return lax.ppermute(block, column, route)
 
-    def collected(block, axis):
-        count = lax.axis_size(axis)
-        return lax.all_to_all(
-            jnp.broadcast_to(block[None], (count,) + block.shape), axis, 0, 0, tiled=True
-        )
-
-    column_queries = collected(query_vectors, "zh").reshape(-1, width)
-    first, second = mem[:half], mem[half:]
-    memory_blocks = [
-        mem,
-        moved(mem, 1, 0),
-        moved(first, 0, -1),
-        moved(second, 0, 1),
-        moved(first, 1, -1),
-        moved(second, 1, 1),
-    ]
-
+    place = jnp.stack([lax.axis_index("yh"), lax.axis_index("zl"), lax.axis_index("dp")])
     capacity = max(2, 2 * rows // cycle)
+    span = 4 * capacity
     block, outgoing, shift = call(
         lambda *refs: prepare_kernel(capacity, group, *refs),
         (
+            place,
             query_vectors,
             item_vectors,
             negative_vectors,
@@ -312,31 +351,56 @@
         ),
         (
             jax.ShapeDtypeStruct((rows + keys + 16, width), BF16),
-            jax.ShapeDtypeStruct((cycle * capacity, width + 128), BF16),
+            jax.ShapeDtypeStruct((shards, rows + span + span // 2, width), BF16),
             jax.ShapeDtypeStruct((1, keys), F32),
         ),
         "prepare",
     )
-    gathered = lax.all_gather(block, "dp", axis=0, tiled=False)
-
-    column_queries, outgoing, *memory_blocks = lax.optimization_barrier(
-        (column_queries, outgoing, *memory_blocks)
-    )
-    arrived = lax.all_to_all(
-        outgoing.reshape(cycle, capacity, width + 128), column, 0, 0, tiled=True
-    )
+    arrived = lax.all_to_all(outgoing, "zh", 0, 0, tiled=True)
+
+    near = 4
+    pair_blocks = jnp.stack(
+        [block] + [lax.ppermute(block, "dp", [(i, i ^ k) for i in range(group)]) for k in range(1, near)]
+    )
+    z_rows = beside(mem, 0, 1)
+    memory_blocks = [mem, z_rows, beside(mem, 1, 0), beside(z_rows, 1, 0)]
+
+    def along(blocks, by):
+        return lax.ppermute(blocks, "dp", [(i, (i + near * by) % group) for i in range(group)])
+
+    before, after = along(pair_blocks, 1), along(pair_blocks, -1)
+    arrived, before, after, *memory_blocks = lax.optimization_barrier(
+        (arrived, before, after, *memory_blocks)
+    )
+
     (parts,) = call(
         lambda *refs: memory_kernel(512, *refs),
-        (column_queries, *memory_blocks),
+        (arrived, *memory_blocks),
         (jax.ShapeDtypeStruct((shards, rows + 16, width), BF16),),
         "memory",
     )
-    parts, arrived = lax.optimization_barrier((parts, arrived))
+    parts, arrived, before, after = lax.optimization_barrier((parts, arrived, before, after))
     parts_back = lax.all_to_all(parts, "zh", 0, 0, tiled=True)
 
+    group_blocks = [
+        pair_blocks,
+        before,
+        along(before[: near // 2], 1),
+        along(after[near // 2 :], -1),
+        after,
+    ]
+    own_items, *others_items = call(
+        lambda *refs: forward_kernel(rows, *refs),
+        (arrived,),
+        (jax.ShapeDtypeStruct((shards * capacity, width + 128), BF16),) * 4,
+        "forward",
+    )
+    new_items = [own_items] + [
+        beside(items, c // 2, c % 2) for c, items in enumerate(others_items, start=1)
+    ]
     batch_part, batch_stat = call(
         batch_kernel,
-        (gathered, query_vectors, item_vectors, shift),
+        (*group_blocks, query_vectors, item_vectors, shift),
         (
             jax.ShapeDtypeStruct((rows, width), F32),
             jax.ShapeDtypeStruct((2, rows), F32),
@@ -344,14 +408,8 @@
         "batch",
         [pltpu.VMEM((group, rows, keys), F32)],
     )
-    (updated,) = call(
-        update_kernel,
-        (arrived.reshape(cycle * capacity, width + 128), mem),
-        (jax.ShapeDtypeStruct(mem.shape, BF16),),
-        "update",
-    )
-    parts_back, updated, batch_part, batch_stat = lax.optimization_barrier(
-        (parts_back, updated, batch_part, batch_stat)
+    parts_back, batch_part, batch_stat, *new_items = lax.optimization_barrier(
+        (parts_back, batch_part, batch_stat, *new_items)
     )
     log_total, loss = call(
         total_kernel,
@@ -359,17 +417,35 @@
         (jax.ShapeDtypeStruct((1, rows), F32), jax.ShapeDtypeStruct((1, rows), F32)),
         "total",
     )
-    group_totals = collected(log_total, "dp").reshape(group, rows)
+    group_totals = lax.all_to_all(
+        jnp.broadcast_to(log_total[None], (group, 1, rows)), "dp", 0, 0, tiled=True
+    ).reshape(group, rows)
     (query_grad,) = call(
         query_kernel,
         (parts_back, log_total, batch_part, batch_stat, item_vectors),
         (jax.ShapeDtypeStruct((rows, width), F32),),
         "queries",
     )
-    group_totals, query_grad = lax.optimization_barrier((group_totals, query_grad))
+    (updated,) = call(
+        lambda *refs: update_kernel(shards, *refs),
+        (place, *new_items, mem),
+        (jax.ShapeDtypeStruct(mem.shape, BF16),),
+        "update",
+    )
+    group_totals, query_grad, updated = lax.optimization_barrier(
+        (group_totals, query_grad, updated)
+    )
     item_grad, negative_grad = call(
         item_kernel,
-        (gathered, group_totals, query_vectors, item_vectors, negative_vectors, shift),
+        (
+            place,
+            *group_blocks,
+            group_totals,
+            query_vectors,
+            item_vectors,
+            negative_vectors,
+            shift,
+        ),
         (
             jax.ShapeDtypeStruct((rows, width), F32),
             jax.ShapeDtypeStruct((negatives, width), F32),

time: 164 us -> 155 us (0.945)
  the two profiles are of different devices: /device:TPU:33 before, /device:TPU:1 now
where the time goes in v3:
time: 155 us; the launch traced here: 154 us
  starting transfers between devices  82.2 us (53%)
  waiting for transfers between devices  38.7 us (25%)
  Pallas kernels  26.4 us (17%)
  local copies, waits for them, and re-layouts  5.17 us (3%)
    ppermute x6, waiting for transfers between devices, beside(): return lax.ppermute(block, column, route)  33.2 us
    pallas_call x8, Pallas kernels, call(): pl.pallas_call(kernel, out_shape=out_shape, in_specs=[scalars if operand....  26.4 us
    ppermute x6, starting transfers between devices, beside(): return lax.ppermute(block, column, route)  24.1 us
    all_to_all x1, starting transfers between devices, local(): arrived = lax.all_to_all(outgoing, 'zh', 0, 0, tiled=True)  15.8 us
    ppermute x4, starting transfers between devices, along(): lax.ppermute(blocks, 'dp', [(i, (i + near * by) % group) for i in range(g...  12.6 us
    all_to_all x1, starting transfers between devices, local(): parts_back = lax.all_to_all(parts, 'zh', 0, 0, tiled=True)  10.6 us
    all_to_all x1, starting transfers between devices, local(): lax.all_to_all(jnp.broadcast_to(log_total[None], (group, 1, rows)), 'dp',...  10.5 us
    ppermute x3, starting transfers between devices, local(): lax.ppermute(block, 'dp', [(i, i ^ k) for i in range(group)])  8.55 us
  transfers between devices with their start and end apart: 16, of which 7 were waited for; matrix products, arithmetic and copies ran while one was open for 0% of the time, Pallas kernels for 7%

profile of v3, /device:TPU:1, one launch (start us, length us, event | category | flops | bytes accessed | tf_op | source)
XLA Modules:
  0.0 154.0 jit_solution(10962070946090448079)
XLA Ops:
  0.6 0.6 pad_add_fusion.refs_0_
  1.2 2.1 %prepare.1 = (bf16[336,256]{1,0:T(8,128)(2,1)}, bf16[8,176,256]{2,1,0:T(8,128)(2,1)}, f32[1,192]{1,0:T(1,128)}) custom-call(s32[3]{0:T(128)} %pad_add_fusion.refs_0_, bf16[128,256]{1,0:T(8,128)(2,1)} %refs_7_.1, bf16[128,256]{1,0:T(8,128)(2,1)} %refs_8_.1, bf16[64,256]{1,0:T(8,128)(2,1)} %refs_9_.1, s32[1,128]{1,0:T(1,128)} %bitcast.28, s32[1,64]{1,0:T(1,128)} %bitcast.29, ...), custom_call_target="tpu_custom_call" | custom-call | tf_op jit(solution)/shard_map/prepare/pallas_call | solution.py:60
  3.3 15.8 %all-to-all-start = ((bf16[8,176,256]{2,1,0:T(8,128)(2,1)}), bf16[8,176,256]{2,1,0:T(8,128)(2,1)S(1)}, u32[]{:S(2)}, u32[]{:S(2)}) async-start(bf16[8,176,256]{2,1,0:T(8,128)(2,1)} %get-tuple-element.39), calls=%async_computation | async-start | bytes 1441792 | tf_op jit(solution)/shard_map/all_to_all | solution.py:359
  19.1 0.0 copy-done.5
  19.1 2.6 %collective-permute-start.5 = (bf16[1024,256]{1,0:T(8,128)(2,1)S(1)}, bf16[1024,256]{1,0:T(8,128)(2,1)S(1)}, u32[]{:S(2)}, u32[]{:S(2)}) collective-permute-start(bf16[1024,256]{1,0:T(8,128)(2,1)S(1)} %bitcast.19), channel_id=1, source_target_pairs={{0,16},{16,0},{32,48},{48,32},{64,80},{80,64},{96,112},{112,96},{1... | collective-permute-start | bytes 1572872 | tf_op jit(solution)/shard_map/ppermute | solution.py:334
  21.8 0.0 copy-done.10
  21.8 4.3 %collective-permute-start.2 = (bf16[336,256]{1,0:T(8,128)(2,1)S(1)}, bf16[336,256]{1,0:T(8,128)(2,1)S(1)}, u32[]{:S(2)}, u32[]{:S(2)}) collective-permute-start(bf16[336,256]{1,0:T(8,128)(2,1)S(1)} %copy-done.10), channel_id=1, source_target_pairs={{0,3},{1,2},{2,1},{3,0},{4,7},{5,6},{6,5},{7,4},{8,11},{9,10},{10,... | collective-permute-start | bytes 516104 | tf_op jit(solution)/shard_map/ppermute | solution.py:363
  26.1 2.1 %collective-permute-start.1 = (bf16[336,256]{1,0:T(8,128)(2,1)S(1)}, bf16[336,256]{1,0:T(8,128)(2,1)S(1)}, u32[]{:S(2)}, u32[]{:S(2)}) collective-permute-start(bf16[336,256]{1,0:T(8,128)(2,1)S(1)} %copy-done.10), channel_id=1, source_target_pairs={{0,2},{1,3},{2,0},{3,1},{4,6},{5,7},{6,4},{7,5},{8,10},{9,11},{10,... | collective-permute-start | bytes 516104 | tf_op jit(solution)/shard_map/ppermute | solution.py:363
  28.2 2.1 %collective-permute-start = (bf16[336,256]{1,0:T(8,128)(2,1)S(1)}, bf16[336,256]{1,0:T(8,128)(2,1)S(1)}, u32[]{:S(2)}, u32[]{:S(2)}) collective-permute-start(bf16[336,256]{1,0:T(8,128)(2,1)S(1)} %copy-done.10), channel_id=1, source_target_pairs={{0,1},{1,0},{2,3},{3,2},{4,5},{5,4},{6,7},{7,6},{8,9},{9,8},{10,11... | collective-permute-start | bytes 516104 | tf_op jit(solution)/shard_map/ppermute | solution.py:363
  30.4 1.0 collective-permute-done.2
  31.3 3.4 %collective-permute-done.1 = bf16[336,256]{1,0:T(8,128)(2,1)S(1)} collective-permute-done((bf16[336,256]{1,0:T(8,128)(2,1)S(1)}, bf16[336,256]{1,0:T(8,128)(2,1)S(1)}, u32[]{:S(2)}, u32[]{:S(2)}) %collective-permute-start.1) | collective-permute-done | bytes 172064 | tf_op jit(solution)/shard_map/ppermute | solution.py:363
  34.7 0.0 collective-permute-done
  34.7 0.1 pad_maximum_fusion.refs_0_.refs_1_
  34.8 0.0 copy-start.1
  34.9 4.4 %collective-permute-start.4 = (bf16[4,336,256]{2,1,0:T(8,128)(2,1)S(1)}, bf16[4,336,256]{2,1,0:T(8,128)(2,1)S(1)}, u32[]{:S(2)}, u32[]{:S(2)}) collective-permute-start(bf16[4,336,256]{2,1,0:T(8,128)(2,1)S(1)} %pad_maximum_fusion.refs_0_.refs_1_), channel_id=1, source_target_pairs={{0,12},{1,13},{2,14},{3,15},{4,0},{5,1},{6,2},{7,3},{8,4},{9,5},{1... | collective-permute-start | bytes 2064392 | tf_op jit(solution)/shard_map/ppermute | solution.py:369
  39.2 1.9 %collective-permute-start.3 = (bf16[4,336,256]{2,1,0:T(8,128)(2,1)S(1)}, bf16[4,336,256]{2,1,0:T(8,128)(2,1)S(1)}, u32[]{:S(2)}, u32[]{:S(2)}) collective-permute-start(bf16[4,336,256]{2,1,0:T(8,128)(2,1)S(1)} %pad_maximum_fusion.refs_0_.refs_1_), channel_id=1, source_target_pairs={{0,4},{1,5},{2,6},{3,7},{4,8},{5,9},{6,10},{7,11},{8,12},{9,13},{1... | collective-permute-start | bytes 2064392 | tf_op jit(solution)/shard_map/ppermute | solution.py:369
  41.2 4.8 %collective-permute-start.6 = (bf16[1024,256]{1,0:T(8,128)(2,1)S(1)}, bf16[1024,256]{1,0:T(8,128)(2,1)S(1)}, u32[]{:S(2)}, u32[]{:S(2)}) collective-permute-start(bf16[1024,256]{1,0:T(8,128)(2,1)S(1)} %bitcast.20), channel_id=1, source_target_pairs={{0,256},{16,272},{32,288},{48,304},{64,320},{80,336},{96,352},{112... | collective-permute-start | bytes 1572872 | tf_op jit(solution)/shard_map/ppermute | solution.py:334
  46.0 16.4 %collective-permute-done.5.refs_2_ = bf16[1024,256]{1,0:T(8,128)(2,1)S(1)} collective-permute-done((bf16[1024,256]{1,0:T(8,128)(2,1)S(1)}, bf16[1024,256]{1,0:T(8,128)(2,1)S(1)}, u32[]{:S(2)}, u32[]{:S(2)}) %collective-permute-start.5) | collective-permute-done | bytes 524320 | tf_op jit(solution)/shard_map/ppermute | solution.py:334
  62.4 4.8 %collective-permute-start.7 = (bf16[1024,256]{1,0:T(8,128)(2,1)S(1)}, bf16[1024,256]{1,0:T(8,128)(2,1)}, u32[]{:S(2)}, u32[]{:S(2)}) collective-permute-start(bf16[1024,256]{1,0:T(8,128)(2,1)S(1)} %collective-permute-done.5.refs_2_), channel_id=1, source_target_pairs={{0,256},{16,272},{32,288},{48,304},{64,320},{80,336},{96,352},{112... | collective-permute-start | bytes 1572872 | tf_op jit(solution)/shard_map/ppermute | solution.py:334
  67.2 0.0 collective-permute-done.6.refs_3_
  67.2 0.0 copy-start.9
  67.2 0.0 collective-permute-done.4.refs_4_.refs_5_
  67.2 0.0 copy-start.3
  67.2 0.0 collective-permute-done.3.refs_1_.refs_2_
  67.3 0.0 copy-done.8
  67.3 0.7 copy-done.9
  68.0 9.8 %collective-permute-done.7.refs_4_ = bf16[1024,256]{1,0:T(8,128)(2,1)} collective-permute-done((bf16[1024,256]{1,0:T(8,128)(2,1)S(1)}, bf16[1024,256]{1,0:T(8,128)(2,1)}, u32[]{:S(2)}, u32[]{:S(2)}) %collective-permute-start.7) | collective-permute-done | bytes 524320 | tf_op jit(solution)/shard_map/ppermute | solution.py:334
  77.8 0.0 all-to-all-done.refs_0_
  77.8 0.9 copy-done
  78.7 9.0 %memory.1 = bf16[8,144,256]{2,1,0:T(8,128)(2,1)} custom-call(bf16[8,176,256]{2,1,0:T(8,128)(2,1)} %copy-done, bf16[1024,256]{1,0:T(8,128)(2,1)} %bitcast.17, bf16[1024,256]{1,0:T(8,128)(2,1)} %copy-done.8, bf16[1024,256]{1,0:T(8,128)(2,1)} %copy-done.9, bf16[1024,256]{1,0:T(8,128)(2,1)} %collective-permute-done.7.refs_4_), custom_call_target="tpu_custom_call" | custom-call | tf_op jit(solution)/shard_map/memory/pallas_call | solution.py:60
  87.7 0.0 copy-done.1
  87.7 10.6 %all-to-all-start.1 = ((bf16[8,144,256]{2,1,0:T(8,128)(2,1)}), bf16[8,144,256]{2,1,0:T(8,128)(2,1)S(1)}, u32[]{:S(2)}, u32[]{:S(2)}) async-start(bf16[8,144,256]{2,1,0:T(8,128)(2,1)} %memory.1), calls=%async_computation.1 | async-start | bytes 1179648 | tf_op jit(solution)/shard_map/all_to_all | solution.py:383
  98.4 0.0 copy-done.4
  98.4 0.0 copy-done.3
  98.4 4.4 %collective-permute-start.9 = (bf16[2,336,256]{2,1,0:T(8,128)(2,1)S(1)}, bf16[2,336,256]{2,1,0:T(8,128)(2,1)S(1)}, u32[]{:S(2)}, u32[]{:S(2)}) collective-permute-start(bf16[2,336,256]{2,1,0:T(8,128)(2,1)S(1)} %slice.7), channel_id=1, source_target_pairs={{0,12},{1,13},{2,14},{3,15},{4,0},{5,1},{6,2},{7,3},{8,4},{9,5},{1... | collective-permute-start | bytes 1032200 | tf_op jit(solution)/shard_map/ppermute | solution.py:369
  102.8 1.9 %collective-permute-start.8 = (bf16[2,336,256]{2,1,0:T(8,128)(2,1)S(1)}, bf16[2,336,256]{2,1,0:T(8,128)(2,1)S(1)}, u32[]{:S(2)}, u32[]{:S(2)}) collective-permute-start(bf16[2,336,256]{2,1,0:T(8,128)(2,1)S(1)} %slice.6), channel_id=1, source_target_pairs={{0,4},{1,5},{2,6},{3,7},{4,8},{5,9},{6,10},{7,11},{8,12},{9,13},{1... | collective-permute-start | bytes 1032200 | tf_op jit(solution)/shard_map/ppermute | solution.py:369
  104.8 1.8 %forward.1 = (bf16[64,384]{1,0:T(8,128)(2,1)}, bf16[64,384]{1,0:T(8,128)(2,1)}, bf16[64,384]{1,0:T(8,128)(2,1)}, bf16[64,384]{1,0:T(8,128)(2,1)}) custom-call(bf16[8,176,256]{2,1,0:T(8,128)(2,1)} %copy-done), custom_call_target="tpu_custom_call" | custom-call | tf_op jit(solution)/shard_map/forward/pallas_call | solution.py:60
  106.6 5.0 %collective-permute-start.10 = (bf16[64,384]{1,0:T(8,128)(2,1)}, bf16[64,384]{1,0:T(8,128)(2,1)S(1)}, u32[]{:S(2)}, u32[]{:S(2)}) collective-permute-start(bf16[64,384]{1,0:T(8,128)(2,1)} %get-tuple-element.56), channel_id=1, source_target_pairs={{0,16},{16,0},{32,48},{48,32},{64,80},{80,64},{96,112},{112,96},{1... | collective-permute-start | bytes 147464 | tf_op jit(solution)/shard_map/ppermute | solution.py:334
  111.6 4.8 %collective-permute-start.11 = (bf16[64,384]{1,0:T(8,128)(2,1)}, bf16[64,384]{1,0:T(8,128)(2,1)S(1)}, u32[]{:S(2)}, u32[]{:S(2)}) collective-permute-start(bf16[64,384]{1,0:T(8,128)(2,1)} %get-tuple-element.57), channel_id=1, source_target_pairs={{0,256},{16,272},{32,288},{48,304},{64,320},{80,336},{96,352},{112... | collective-permute-start | bytes 147464 | tf_op jit(solution)/shard_map/ppermute | solution.py:334
  116.4 1.9 %collective-permute-start.12 = (bf16[64,384]{1,0:T(8,128)(2,1)}, bf16[64,384]{1,0:T(8,128)(2,1)S(1)}, u32[]{:S(2)}, u32[]{:S(2)}) collective-permute-start(bf16[64,384]{1,0:T(8,128)(2,1)} %get-tuple-element.58), channel_id=1, source_target_pairs={{0,272},{16,256},{32,304},{48,288},{64,336},{80,320},{96,368},{112... | collective-permute-start | bytes 147464 | tf_op jit(solution)/shard_map/ppermute | solution.py:334
  118.4 0.0 collective-permute-done.9.refs_3_.refs_4_
  118.4 0.0 copy-start.6
  118.4 0.0 collective-permute-done.8.refs_2_.refs_3_
  118.4 0.0 copy-start.7
  118.4 0.7 copy-done.6
  119.1 0.1 copy-done.7
  119.2 4.2 %batch.1 = (f32[128,256]{1,0:T(8,128)}, f32[2,128]{1,0:T(2,128)}) custom-call(bf16[4,336,256]{2,1,0:T(8,128)(2,1)} %copy-done.1, bf16[4,336,256]{2,1,0:T(8,128)(2,1)} %copy-done.4, bf16[2,336,256]{2,1,0:T(8,128)(2,1)} %copy-done.7, bf16[2,336,256]{2,1,0:T(8,128)(2,1)} %copy-done.6, bf16[4,336,256]{2,1,0:T(8,128)(2,1)} %copy-done.3, ...), custom_call_target="tpu_custom_call" | custom-call | tf_op jit(solution)/shard_map/batch/pallas_call | solution.py:60
  123.4 3.4 %collective-permute-done.10.refs_2_ = bf16[64,384]{1,0:T(8,128)(2,1)S(1)} collective-permute-done((bf16[64,384]{1,0:T(8,128)(2,1)}, bf16[64,384]{1,0:T(8,128)(2,1)S(1)}, u32[]{:S(2)}, u32[]{:S(2)}) %collective-permute-start.10) | collective-permute-done | bytes 49184 | tf_op jit(solution)/shard_map/ppermute | solution.py:334
  126.8 0.0 collective-permute-done.11.refs_3_
  126.8 3.7 %collective-permute-done.12.refs_4_ = bf16[64,384]{1,0:T(8,128)(2,1)S(1)} collective-permute-done((bf16[64,384]{1,0:T(8,128)(2,1)}, bf16[64,384]{1,0:T(8,128)(2,1)S(1)}, u32[]{:S(2)}, u32[]{:S(2)}) %collective-permute-start.12) | collective-permute-done | bytes 49184 | tf_op jit(solution)/shard_map/ppermute | solution.py:334
  130.5 0.0 all-to-all-done.1.parts_ref
  130.5 0.8 copy-done.2
  131.3 1.6 %total.1 = (f32[1,128]{1,0:T(1,128)}, f32[1,128]{1,0:T(1,128)}) custom-call(bf16[8,144,256]{2,1,0:T(8,128)(2,1)} %copy-done.2, f32[2,128]{1,0:T(2,128)} %get-tuple-element.60.stat_ref), custom_call_target="tpu_custom_call" | custom-call | tf_op jit(solution)/shard_map/total/pallas_call | solution.py:60
  132.9 0.0 copy-done.11
  132.9 0.0 copy-done.12
  132.9 0.0 copy-start.15
  133.0 0.6 copy-done.15
  133.6 0.6 broadcast_in_dim.28
  134.2 10.5 %all-to-all-start.2 = ((f32[16,1,128]{2,1,0:T(1,128)}), f32[16,1,128]{2,1,0:T(1,128)S(1)}, u32[]{:S(2)}, u32[]{:S(2)}) async-start(f32[16,1,128]{2,1,0:T(1,128)} %broadcast_in_dim.28), calls=%async_computation.2 | async-start | bytes 16384 | tf_op jit(solution)/shard_map/all_to_all | solution.py:420
  144.7 2.0 %queries.1 = f32[128,256]{1,0:T(8,128)} custom-call(bf16[8,144,256]{2,1,0:T(8,128)(2,1)} %copy-done.2, f32[1,128]{1,0:T(1,128)} %get-tuple-element.62.lt_ref, f32[128,256]{1,0:T(8,128)} %get-tuple-element.63.batch_ref, f32[2,128]{1,0:T(2,128)} %get-tuple-element.60.stat_ref, bf16[128,256]{1,0:T(8,128)(2,1)} %refs_8_.1), custom_call_target="tpu_custom_call" | custom-call | tf_op jit(solution)/shard_map/queries/pallas_call | solution.py:60
  146.7 2.4 %update.1 = bf16[1024,256]{1,0:T(8,128)(2,1)} custom-call(s32[3]{0:T(128)} %pad_add_fusion.refs_0_, bf16[64,384]{1,0:T(8,128)(2,1)} %get-tuple-element.64.refs_1_, bf16[64,384]{1,0:T(8,128)(2,1)} %copy-done.11, bf16[64,384]{1,0:T(8,128)(2,1)} %copy-done.12, bf16[64,384]{1,0:T(8,128)(2,1)} %copy-done.13, bf16[1024,256]{1,0:T(8,128)(2,1)} %bitcast.18), custom_call_target="tpu_custom_call" | custom-call | tf_op jit(solution)/shard_map/update/pallas_call | solution.py:60
  149.1 1.1 all-to-all-done.2
  150.2 0.6 copy-done.14
  150.8 3.3 %items.1 = (f32[128,256]{1,0:T(8,128)}, f32[64,256]{1,0:T(8,128)}) custom-call(s32[3]{0:T(128)} %pad_add_fusion.refs_0_, bf16[4,336,256]{2,1,0:T(8,128)(2,1)} %copy-done.1, bf16[4,336,256]{2,1,0:T(8,128)(2,1)} %copy-done.4, bf16[2,336,256]{2,1,0:T(8,128)(2,1)} %copy-done.7, bf16[2,336,256]{2,1,0:T(8,128)(2,1)} %copy-done.6, bf16[4,336,256]{2,1,0:T(8,128)(2,1)} %copy-done.3, ...), custom_call_target="tpu_custom_call" | custom-call | tf_op jit(solution)/shard_map/items/pallas_call | solution.py:60
  (13 shorter events, 0.1 us)
Async XLA Ops:
  3.3 15.8 %copy-start.5 = (bf16[1,1024,256]{2,1,0:T(8,128)(2,1)S(1)}, bf16[1,1024,256]{2,1,0:T(8,128)(2,1)}, u32[]{:S(2)}) copy-start(bf16[1,1024,256]{2,1,0:T(8,128)(2,1)} %param.15) | copy-start | bytes 1572868
  3.3 18.4 %copy-start.10 = (bf16[336,256]{1,0:T(8,128)(2,1)S(1)}, bf16[336,256]{1,0:T(8,128)(2,1)}, u32[]{:S(2)}) copy-start(bf16[336,256]{1,0:T(8,128)(2,1)} %get-tuple-element.40) | copy-start | bytes 516100
  3.3 74.4 %all-to-all-start = ((bf16[8,176,256]{2,1,0:T(8,128)(2,1)}), bf16[8,176,256]{2,1,0:T(8,128)(2,1)S(1)}, u32[]{:S(2)}, u32[]{:S(2)}) async-start(bf16[8,176,256]{2,1,0:T(8,128)(2,1)} %get-tuple-element.39), calls=%async_computation | async-start | bytes 1441792 | tf_op jit(solution)/shard_map/all_to_all | solution.py:359
  19.1 43.3 %collective-permute-start.5 = (bf16[1024,256]{1,0:T(8,128)(2,1)S(1)}, bf16[1024,256]{1,0:T(8,128)(2,1)S(1)}, u32[]{:S(2)}, u32[]{:S(2)}) collective-permute-start(bf16[1024,256]{1,0:T(8,128)(2,1)S(1)} %bitcast.19), channel_id=1, source_target_pairs={{0,16},{16,0},{32,48},{48,32},{64,80},{80,64},{96,112},{112,96},{1... | collective-permute-start | bytes 1572872 | tf_op jit(solution)/shard_map/ppermute | solution.py:334
  21.8 9.5 %collective-permute-start.2 = (bf16[336,256]{1,0:T(8,128)(2,1)S(1)}, bf16[336,256]{1,0:T(8,128)(2,1)S(1)}, u32[]{:S(2)}, u32[]{:S(2)}) collective-permute-start(bf16[336,256]{1,0:T(8,128)(2,1)S(1)} %copy-done.10), channel_id=1, source_target_pairs={{0,3},{1,2},{2,1},{3,0},{4,7},{5,6},{6,5},{7,4},{8,11},{9,10},{10,... | collective-permute-start | bytes 516104 | tf_op jit(solution)/shard_map/ppermute | solution.py:363
  26.1 8.6 %collective-permute-start.1 = (bf16[336,256]{1,0:T(8,128)(2,1)S(1)}, bf16[336,256]{1,0:T(8,128)(2,1)S(1)}, u32[]{:S(2)}, u32[]{:S(2)}) collective-permute-start(bf16[336,256]{1,0:T(8,128)(2,1)S(1)} %copy-done.10), channel_id=1, source_target_pairs={{0,2},{1,3},{2,0},{3,1},{4,6},{5,7},{6,4},{7,5},{8,10},{9,11},{10,... | collective-permute-start | bytes 516104 | tf_op jit(solution)/shard_map/ppermute | solution.py:363
  28.2 6.5 %collective-permute-start = (bf16[336,256]{1,0:T(8,128)(2,1)S(1)}, bf16[336,256]{1,0:T(8,128)(2,1)S(1)}, u32[]{:S(2)}, u32[]{:S(2)}) collective-permute-start(bf16[336,256]{1,0:T(8,128)(2,1)S(1)} %copy-done.10), channel_id=1, source_target_pairs={{0,1},{1,0},{2,3},{3,2},{4,5},{5,4},{6,7},{7,6},{8,9},{9,8},{10,11... | collective-permute-start | bytes 516104 | tf_op jit(solution)/shard_map/ppermute | solution.py:363
  34.8 52.9 %copy-start.1 = (bf16[4,336,256]{2,1,0:T(8,128)(2,1)}, bf16[4,336,256]{2,1,0:T(8,128)(2,1)S(1)}, u32[]{:S(2)}) copy-start(bf16[4,336,256]{2,1,0:T(8,128)(2,1)S(1)} %pad_maximum_fusion.refs_0_.refs_1_) | copy-start | bytes 2064388
  34.9 32.4 %collective-permute-start.4 = (bf16[4,336,256]{2,1,0:T(8,128)(2,1)S(1)}, bf16[4,336,256]{2,1,0:T(8,128)(2,1)S(1)}, u32[]{:S(2)}, u32[]{:S(2)}) collective-permute-start(bf16[4,336,256]{2,1,0:T(8,128)(2,1)S(1)} %pad_maximum_fusion.refs_0_.refs_1_), channel_id=1, source_target_pairs={{0,12},{1,13},{2,14},{3,15},{4,0},{5,1},{6,2},{7,3},{8,4},{9,5},{1... | collective-permute-start | bytes 2064392 | tf_op jit(solution)/shard_map/ppermute | solution.py:369
  39.2 28.0 %collective-permute-start.3 = (bf16[4,336,256]{2,1,0:T(8,128)(2,1)S(1)}, bf16[4,336,256]{2,1,0:T(8,128)(2,1)S(1)}, u32[]{:S(2)}, u32[]{:S(2)}) collective-permute-start(bf16[4,336,256]{2,1,0:T(8,128)(2,1)S(1)} %pad_maximum_fusion.refs_0_.refs_1_), channel_id=1, source_target_pairs={{0,4},{1,5},{2,6},{3,7},{4,8},{5,9},{6,10},{7,11},{8,12},{9,13},{1... | collective-permute-start | bytes 2064392 | tf_op jit(solution)/shard_map/ppermute | solution.py:369
  41.2 26.0 %collective-permute-start.6 = (bf16[1024,256]{1,0:T(8,128)(2,1)S(1)}, bf16[1024,256]{1,0:T(8,128)(2,1)S(1)}, u32[]{:S(2)}, u32[]{:S(2)}) collective-permute-start(bf16[1024,256]{1,0:T(8,128)(2,1)S(1)} %bitcast.20), channel_id=1, source_target_pairs={{0,256},{16,272},{32,288},{48,304},{64,320},{80,336},{96,352},{112... | collective-permute-start | bytes 1572872 | tf_op jit(solution)/shard_map/ppermute | solution.py:334
  62.4 4.9 %copy-start.8 = (bf16[1024,256]{1,0:T(8,128)(2,1)}, bf16[1024,256]{1,0:T(8,128)(2,1)S(1)}, u32[]{:S(2)}) copy-start(bf16[1024,256]{1,0:T(8,128)(2,1)S(1)} %collective-permute-done.5.refs_2_) | copy-start | bytes 1572868
  62.4 15.4 %collective-permute-start.7 = (bf16[1024,256]{1,0:T(8,128)(2,1)S(1)}, bf16[1024,256]{1,0:T(8,128)(2,1)}, u32[]{:S(2)}, u32[]{:S(2)}) collective-permute-start(bf16[1024,256]{1,0:T(8,128)(2,1)S(1)} %collective-permute-done.5.refs_2_), channel_id=1, source_target_pairs={{0,256},{16,272},{32,288},{48,304},{64,320},{80,336},{96,352},{112... | collective-permute-start | bytes 1572872 | tf_op jit(solution)/shard_map/ppermute | solution.py:334
  67.2 0.8 copy-start.9
  67.2 31.2 %copy-start.3 = (bf16[4,336,256]{2,1,0:T(8,128)(2,1)}, bf16[4,336,256]{2,1,0:T(8,128)(2,1)S(1)}, u32[]{:S(2)}) copy-start(bf16[4,336,256]{2,1,0:T(8,128)(2,1)S(1)} %collective-permute-done.4.refs_4_.refs_5_) | copy-start | bytes 2064388
  68.0 30.4 %copy-start.4 = (bf16[4,336,256]{2,1,0:T(8,128)(2,1)}, bf16[4,336,256]{2,1,0:T(8,128)(2,1)S(1)}, u32[]{:S(2)}) copy-start(bf16[4,336,256]{2,1,0:T(8,128)(2,1)S(1)} %collective-permute-done.3.refs_1_.refs_2_) | copy-start | bytes 2064388
  77.8 0.9 copy-start
  87.7 42.8 %all-to-all-start.1 = ((bf16[8,144,256]{2,1,0:T(8,128)(2,1)}), bf16[8,144,256]{2,1,0:T(8,128)(2,1)S(1)}, u32[]{:S(2)}, u32[]{:S(2)}) async-start(bf16[8,144,256]{2,1,0:T(8,128)(2,1)} %memory.1), calls=%async_computation.1 | async-start | bytes 1179648 | tf_op jit(solution)/shard_map/all_to_all | solution.py:383
  98.4 19.9 %collective-permute-start.9 = (bf16[2,336,256]{2,1,0:T(8,128)(2,1)S(1)}, bf16[2,336,256]{2,1,0:T(8,128)(2,1)S(1)}, u32[]{:S(2)}, u32[]{:S(2)}) collective-permute-start(bf16[2,336,256]{2,1,0:T(8,128)(2,1)S(1)} %slice.7), channel_id=1, source_target_pairs={{0,12},{1,13},{2,14},{3,15},{4,0},{5,1},{6,2},{7,3},{8,4},{9,5},{1... | collective-permute-start | bytes 1032200 | tf_op jit(solution)/shard_map/ppermute | solution.py:369
  102.8 15.5 %collective-permute-start.8 = (bf16[2,336,256]{2,1,0:T(8,128)(2,1)S(1)}, bf16[2,336,256]{2,1,0:T(8,128)(2,1)S(1)}, u32[]{:S(2)}, u32[]{:S(2)}) collective-permute-start(bf16[2,336,256]{2,1,0:T(8,128)(2,1)S(1)} %slice.6), channel_id=1, source_target_pairs={{0,4},{1,5},{2,6},{3,7},{4,8},{5,9},{6,10},{7,11},{8,12},{9,13},{1... | collective-permute-start | bytes 1032200 | tf_op jit(solution)/shard_map/ppermute | solution.py:369
  106.6 20.2 %collective-permute-start.10 = (bf16[64,384]{1,0:T(8,128)(2,1)}, bf16[64,384]{1,0:T(8,128)(2,1)S(1)}, u32[]{:S(2)}, u32[]{:S(2)}) collective-permute-start(bf16[64,384]{1,0:T(8,128)(2,1)} %get-tuple-element.56), channel_id=1, source_target_pairs={{0,16},{16,0},{32,48},{48,32},{64,80},{80,64},{96,112},{112,96},{1... | collective-permute-start | bytes 147464 | tf_op jit(solution)/shard_map/ppermute | solution.py:334
  111.6 15.2 %collective-permute-start.11 = (bf16[64,384]{1,0:T(8,128)(2,1)}, bf16[64,384]{1,0:T(8,128)(2,1)S(1)}, u32[]{:S(2)}, u32[]{:S(2)}) collective-permute-start(bf16[64,384]{1,0:T(8,128)(2,1)} %get-tuple-element.57), channel_id=1, source_target_pairs={{0,256},{16,272},{32,288},{48,304},{64,320},{80,336},{96,352},{112... | collective-permute-start | bytes 147464 | tf_op jit(solution)/shard_map/ppermute | solution.py:334
  116.4 14.1 %collective-permute-start.12 = (bf16[64,384]{1,0:T(8,128)(2,1)}, bf16[64,384]{1,0:T(8,128)(2,1)S(1)}, u32[]{:S(2)}, u32[]{:S(2)}) collective-permute-start(bf16[64,384]{1,0:T(8,128)(2,1)} %get-tuple-element.58), channel_id=1, source_target_pairs={{0,272},{16,256},{32,304},{48,288},{64,336},{80,320},{96,368},{112... | collective-permute-start | bytes 147464 | tf_op jit(solution)/shard_map/ppermute | solution.py:334
  118.4 0.7 copy-start.6
  118.4 0.8 copy-start.7
  126.8 6.2 %copy-start.11 = (bf16[64,384]{1,0:T(8,128)(2,1)}, bf16[64,384]{1,0:T(8,128)(2,1)S(1)}, u32[]{:S(2)}) copy-start(bf16[64,384]{1,0:T(8,128)(2,1)S(1)} %collective-permute-done.10.refs_2_) | copy-start | bytes 147460
  126.8 6.2 %copy-start.12 = (bf16[64,384]{1,0:T(8,128)(2,1)}, bf16[64,384]{1,0:T(8,128)(2,1)S(1)}, u32[]{:S(2)}) copy-start(bf16[64,384]{1,0:T(8,128)(2,1)S(1)} %collective-permute-done.11.refs_3_) | copy-start | bytes 147460
  130.5 2.5 %copy-start.13 = (bf16[64,384]{1,0:T(8,128)(2,1)}, bf16[64,384]{1,0:T(8,128)(2,1)S(1)}, u32[]{:S(2)}) copy-start(bf16[64,384]{1,0:T(8,128)(2,1)S(1)} %collective-permute-done.12.refs_4_) | copy-start | bytes 147460
  130.5 0.8 copy-start.2
  132.9 0.7 copy-start.15
  134.2 16.0 %all-to-all-start.2 = ((f32[16,1,128]{2,1,0:T(1,128)}), f32[16,1,128]{2,1,0:T(1,128)S(1)}, u32[]{:S(2)}, u32[]{:S(2)}) async-start(f32[16,1,128]{2,1,0:T(1,128)} %broadcast_in_dim.28), calls=%async_computation.2 | async-start | bytes 16384 | tf_op jit(solution)/shard_map/all_to_all | solution.py:420
  150.2 0.6 copy-start.14

commit v4 on v3

--- a/solution.py
+++ b/solution.py
@@ -81,8 +81,9 @@
     owner_ref,
     slot_ref,
     block_ref,
-    out_ref,
+    copies_ref,
     sh_ref,
+    *out_refs,
 ):
     rows, negs = q_ref.shape[0], ng_ref.shape[0]
     keys = rows + negs
@@ -97,7 +98,9 @@
     block_ref[rows + keys :, :] = jnp.zeros((extra, block_ref.shape[1]), BF16)
     block_ref[rows + keys :, 0:keys] = split_rows(sh_ref[...], extra).astype(BF16)
 
-    pairs = out_ref.shape[0]
+    pairs = copies_ref.shape[0]
+    for k in range(pairs):
+        copies_ref[k] = q_ref[...]
     count = it_ref.shape[0]
     own_int = owner_ref[...]
     own_row = own_int.astype(F32)
@@ -113,7 +116,7 @@
     pair = depth // 2
     parity = depth - pair * 2
     other = jnp.where(half == place_ref[0], 0, 2) + jnp.where(parity == place_ref[1], 0, 1)
-    target = (pair * 4 + other) * capacity + rank
+    target = (other * pairs + pair) * capacity + rank
     places = pairs * 4 * capacity
     chosen = jnp.where(
         lax.broadcasted_iota(jnp.int32, (places, count), 0) == target, 1.0, 0.0
@@ -121,59 +124,52 @@
     slot = slot_ref[...]
     high = to_column((slot >> 5).astype(F32))
     low = to_column((slot & 31).astype(F32))
-    lane = lax.broadcasted_iota(jnp.int32, (count, 128), 1)
+    lane = lax.broadcasted_iota(jnp.int32, (count, 128), 1).astype(F32)
+    lane = lane - 8.0 * to_column((other // 2).astype(F32))
     details = jnp.where(
-        lane == 0, high, jnp.where(lane == 1, low, jnp.where(lane == 2, 1.0, 0.0))
-    )
-    sent = dot_plain(chosen, it_ref[...]).astype(BF16)
-    sent_details = dot_plain(chosen, details.astype(BF16)).astype(BF16)
-    span = 4 * capacity
-    for k in range(pairs):
-        out_ref[k, 0:rows, :] = q_ref[...]
-        out_ref[k, rows : rows + span, :] = sent[k * span : (k + 1) * span, :]
-        middle = k * span + span // 2
-        out_ref[k, rows + span :, 0:128] = sent_details[k * span : middle, :]
-        out_ref[k, rows + span :, 128:256] = sent_details[middle : (k + 1) * span, :]
-
-
-def forward_kernel(rows, got_ref, *out_refs):
+        lane == 0.0, high, jnp.where(lane == 1.0, low, jnp.where(lane == 2.0, 1.0, 0.0))
+    )
+    width = it_ref.shape[1]
+    each = places // 4
+    for c, out_ref in enumerate(out_refs):
+        some = chosen[c * each : (c + 1) * each, :]
+        out_ref[:, 0:width] = dot_plain(some, it_ref[...]).astype(BF16)
+        out_ref[:, width:] = dot_plain(some, details.astype(BF16)).astype(BF16)
+
+
+def update_kernel(block, each, place_ref, got_ref, mem_ref, new_ref):
+    rows, width = mem_ref.shape
     pairs = got_ref.shape[0]
-    span = (got_ref.shape[1] - rows) * 2 // 3
-    each = span // 4
-    width = got_ref.shape[2]
-    for k in range(0, pairs, 2):
-        items = [got_ref[k + n, rows : rows + span, :].astype(F32) for n in range(2)]
-        details = [got_ref[k + n, rows + span :, :].astype(F32) for n in range(2)]
-        for c, out_ref in enumerate(out_refs):
-            at, side = (c % 2) * each, (c // 2) * 128
-            out_ref[k * each : (k + 2) * each, 0:width] = jnp.concatenate(
-                [block[c * each : (c + 1) * each, :] for block in items], axis=0
-            ).astype(BF16)
-            out_ref[k * each : (k + 2) * each, width:] = jnp.concatenate(
-                [block[at : at + each, side : side + 128] for block in details], axis=0
-            ).astype(BF16)
-
-
-def update_kernel(pairs, place_ref, got0_ref, got1_ref, got2_ref, got3_ref, mem_ref, new_ref):
-    rows, width = mem_ref.shape
-    got = jnp.concatenate(
-        [ref[...] for ref in (got0_ref, got1_ref, got2_ref, got3_ref)], axis=0
-    )
-    places = got.shape[0]
-    each = places // (4 * pairs)
-    details = jnp.transpose(got[:, width:].astype(F32))
-    slot = details[0:1, :] * 32.0 + details[1:2, :]
-    slot = jnp.where(details[2:3, :] > 0.5, slot, -1.0).astype(jnp.int32)
+    two = 2 * each
+    items = jnp.concatenate(
+        [
+            got_ref[k, block + (1 + n) * two : block + (2 + n) * two, :]
+            for n in range(2)
+            for k in range(pairs)
+        ],
+        axis=0,
+    )
+    details = jnp.transpose(
+        jnp.concatenate(
+            [got_ref[k, block : block + two, block:].astype(F32) for k in range(pairs)], axis=0
+        )
+    )
+    high, low, valid = (
+        jnp.concatenate([details[n : n + 1, :], details[8 + n : 9 + n, :]], axis=1)
+        for n in range(3)
+    )
+    slot = jnp.where(valid > 0.5, high * 32.0 + low, -1.0).astype(jnp.int32)
+    places = items.shape[0]
     entry = lax.broadcasted_iota(jnp.int32, (1, places), 1)
-    other = entry // (pairs * each)
-    inside = entry - other * (pairs * each)
-    pair = inside // each
-    rank = inside - pair * each
-    flipped = other // 2
+    flipped = entry // (pairs * two)
+    inside = entry - flipped * (pairs * two)
+    pair = inside // two
+    inside = inside - pair * two
+    crossed = inside // each
+    rank = inside - crossed * each
     half = jnp.where(flipped == 1, 1 - place_ref[0], place_ref[0])
-    parity = jnp.where(other - 2 * flipped == 1, 1 - place_ref[1], place_ref[1])
+    parity = jnp.where(crossed == 1, 1 - place_ref[1], place_ref[1])
     arrival = (((half * pairs + pair) * 2 + parity) * each + rank).astype(F32)
-    items = got[:, 0:width]
     step = 256
     for start in range(0, rows, step):
         row = lax.broadcasted_iota(jnp.int32, (step, places), 0) + start
@@ -185,9 +181,24 @@
 
 
 def memory_kernel(tile, *refs):
-    q_ref, *mem_refs, out_ref = refs
-    block = 128
-    extra = out_ref.shape[1] - block
+    q_ref, *mem_refs, item0_ref, item1_ref, item2_ref, item3_ref, out_ref = refs
+    pairs, block, width = q_ref.shape
+    each = item0_ref.shape[0] // pairs
+    extra = 2 * each
+    for k in range(0, pairs, 2):
+        group = [
+            ref[k * each : (k + 2) * each, :].astype(F32)
+            for ref in (item0_ref, item1_ref, item2_ref, item3_ref)
+        ]
+        for n in range(2):
+            one = [rows[n * each : (n + 1) * each, :] for rows in group]
+            near = jnp.concatenate(one[0:2], axis=0)
+            far = jnp.concatenate(one[2:4], axis=0)
+            out_ref[k + n, block + extra : block + 2 * extra, :] = near[:, 0:width].astype(BF16)
+            out_ref[k + n, block + 2 * extra :, :] = far[:, 0:width].astype(BF16)
+            out_ref[k + n, block : block + extra, block:] = (
+                near[:, width:] + far[:, width:]
+            ).astype(BF16)
     step = 1024
     pieces, open_piece = [], []
     for ref in mem_refs:
@@ -221,8 +232,7 @@
             at = n * (tile // block) + h
             out_ref[at, 0:block, :] = average[h * block : (h + 1) * block, :]
             lse_row = to_row(lse[h * block : (h + 1) * block, :])
-            out_ref[at, block:, 0:block] = split_rows(lse_row, extra).astype(BF16)
-            out_ref[at, block:, block:] = jnp.zeros((extra, q.shape[1] - block), BF16)
+            out_ref[at, block : block + extra, 0:block] = split_rows(lse_row, extra).astype(BF16)
         return carry
 
     lax.fori_loop(0, q_ref.shape[0] * block // tile, one_tile, 0)
@@ -258,7 +268,7 @@
     rows = total_ref.shape[1]
     shards = parts_ref.shape[0]
     batch = stat_ref[0:1, :]
-    lse = [joined(parts_ref[k, rows:, 0:rows]) for k in range(shards)]
+    lse = [joined(parts_ref[k, rows : rows + 16, 0:rows]) for k in range(shards)]
     top = batch
     for row in lse:
         top = jnp.maximum(top, row)
@@ -299,7 +309,7 @@
     rows = log_total.shape[1]
     out = batch_ref[...] * to_column(jnp.exp(stat_ref[0:1, :] - log_total))
     for k in range(parts_ref.shape[0]):
-        share = to_column(jnp.exp(joined(parts_ref[k, rows:, 0:rows]) - log_total))
+        share = to_column(jnp.exp(joined(parts_ref[k, rows : rows + 16, 0:rows]) - log_total))
         out = out + parts_ref[k, 0:rows, :].astype(F32) * share
     out_ref[...] = out - it_ref[...].astype(F32)
 
@@ -335,8 +345,7 @@
 
     place = jnp.stack([lax.axis_index("yh"), lax.axis_index("zl"), lax.axis_index("dp")])
     capacity = max(2, 2 * rows // cycle)
-    span = 4 * capacity
-    block, outgoing, shift = call(
+    block, copies, shift, *new_items = call(
         lambda *refs: prepare_kernel(capacity, group, *refs),
         (
             place,
@@ -351,35 +360,39 @@
         ),
         (
             jax.ShapeDtypeStruct((rows + keys + 16, width), BF16),
-            jax.ShapeDtypeStruct((shards, rows + span + span // 2, width), BF16),
+            jax.ShapeDtypeStruct((shards, rows, width), BF16),
             jax.ShapeDtypeStruct((1, keys), F32),
-        ),
+        )
+        + (jax.ShapeDtypeStruct((shards * capacity, width + 128), BF16),) * 4,
         "prepare",
     )
-    arrived = lax.all_to_all(outgoing, "zh", 0, 0, tiled=True)
+    new_items = [new_items[0]] + [beside(new_items[c], c // 2, c % 2) for c in range(1, 4)]
 
     near = 4
-    pair_blocks = jnp.stack(
-        [block] + [lax.ppermute(block, "dp", [(i, i ^ k) for i in range(group)]) for k in range(1, near)]
-    )
+    near_blocks = [block] + [
+        lax.ppermute(block, "dp", [(i, i ^ k) for i in range(group)]) for k in range(1, near)
+    ]
+    pair_blocks = jnp.stack(near_blocks)
     z_rows = beside(mem, 0, 1)
+    copies, z_rows, pair_blocks = lax.optimization_barrier((copies, z_rows, pair_blocks))
+    arrived = lax.all_to_all(copies, "zh", 0, 0, tiled=True)
     memory_blocks = [mem, z_rows, beside(mem, 1, 0), beside(z_rows, 1, 0)]
 
     def along(blocks, by):
         return lax.ppermute(blocks, "dp", [(i, (i + near * by) % group) for i in range(group)])
 
     before, after = along(pair_blocks, 1), along(pair_blocks, -1)
-    arrived, before, after, *memory_blocks = lax.optimization_barrier(
-        (arrived, before, after, *memory_blocks)
+    arrived, before, after, memory_blocks = lax.optimization_barrier(
+        (arrived, before, after, memory_blocks)
     )
 
     (parts,) = call(
         lambda *refs: memory_kernel(512, *refs),
-        (arrived, *memory_blocks),
-        (jax.ShapeDtypeStruct((shards, rows + 16, width), BF16),),
+        (arrived, *memory_blocks, *new_items),
+        (jax.ShapeDtypeStruct((shards, rows + 6 * capacity, width), BF16),),
         "memory",
     )
-    parts, arrived, before, after = lax.optimization_barrier((parts, arrived, before, after))
+    parts, before, after = lax.optimization_barrier((parts, before, after))
     parts_back = lax.all_to_all(parts, "zh", 0, 0, tiled=True)
 
     group_blocks = [
@@ -389,15 +402,6 @@
         along(after[near // 2 :], -1),
         after,
     ]
-    own_items, *others_items = call(
-        lambda *refs: forward_kernel(rows, *refs),
-        (arrived,),
-        (jax.ShapeDtypeStruct((shards * capacity, width + 128), BF16),) * 4,
-        "forward",
-    )
-    new_items = [own_items] + [
-        beside(items, c // 2, c % 2) for c, items in enumerate(others_items, start=1)
-    ]
     batch_part, batch_stat = call(
         batch_kernel,
         (*group_blocks, query_vectors, item_vectors, shift),
@@ -408,8 +412,8 @@
         "batch",
         [pltpu.VMEM((group, rows, keys), F32)],
     )
-    parts_back, batch_part, batch_stat, *new_items = lax.optimization_barrier(
-        (parts_back, batch_part, batch_stat, *new_items)
+    parts_back, batch_part, batch_stat = lax.optimization_barrier(
+        (parts_back, batch_part, batch_stat)
     )
     log_total, loss = call(
         total_kernel,
@@ -427,8 +431,8 @@
         "queries",
     )
     (updated,) = call(
-        lambda *refs: update_kernel(shards, *refs),
-        (place, *new_items, mem),
+        lambda *refs: update_kernel(rows, capacity, *refs),
+        (place, parts_back, mem),
         (jax.ShapeDtypeStruct(mem.shape, BF16),),
         "update",
     )

time: 155 us -> 156 us (level)
  the two profiles are of different devices: /device:TPU:1 before, /device:TPU:65 now
where the time goes in v4:
time: 156 us; the launch traced here: 155 us
  starting transfers between devices  74.9 us (48%)
  waiting for transfers between devices  47.6 us (31%)
  Pallas kernels  24.8 us (16%)
  local copies, waits for them, and re-layouts  4.89 us (3%)
  other arithmetic  1.62 us (1%)
    pallas_call x7, Pallas kernels, call(): pl.pallas_call(kernel, out_shape=out_shape, in_specs=[scalars if operand....  24.8 us
    ppermute x6, starting transfers between devices, beside(): return lax.ppermute(block, column, route)  22.9 us
    all_to_all x1, waiting for transfers between devices, local(): parts_back = lax.all_to_all(parts, 'zh', 0, 0, tiled=True)  20.3 us
    ppermute x6, waiting for transfers between devices, beside(): return lax.ppermute(block, column, route)  14.3 us
    all_to_all x1, starting transfers between devices, local(): arrived = lax.all_to_all(copies, 'zh', 0, 0, tiled=True)  13.3 us
    ppermute x4, starting transfers between devices, along(): lax.ppermute(blocks, 'dp', [(i, (i + near * by) % group) for i in range(g...  12.5 us
    all_to_all x1, starting transfers between devices, local(): parts_back = lax.all_to_all(parts, 'zh', 0, 0, tiled=True)  11.5 us
    ppermute x3, starting transfers between devices, local(): lax.ppermute(block, 'dp', [(i, i ^ k) for i in range(group)])  8.25 us
  transfers between devices with their start and end apart: 16, of which 9 were waited for; matrix products, arithmetic and copies ran while one was open for 1% of the time, Pallas kernels for 7%

profile of v4, /device:TPU:65, one launch (start us, length us, event | category | flops | bytes accessed | tf_op | source)
XLA Modules:
  0.0 154.8 jit_solution(14431592794372096941)
XLA Ops:
  0.6 3.5 %collective-permute-start = (bf16[1024,256]{1,0:T(8,128)(2,1)}, bf16[1024,256]{1,0:T(8,128)(2,1)S(1)}, u32[]{:S(2)}, u32[]{:S(2)}) collective-permute-start(bf16[1024,256]{1,0:T(8,128)(2,1)} %bitcast.17), channel_id=1, source_target_pairs={{0,16},{16,0},{32,48},{48,32},{64,80},{80,64},{96,112},{112,96},{1... | collective-permute-start | bytes 1572872 | tf_op jit(solution)/shard_map/ppermute | solution.py:344
  4.2 0.6 pad_add_fusion.refs_0_
  4.8 2.1 %prepare.1 = (bf16[336,256]{1,0:T(8,128)(2,1)}, bf16[8,128,256]{2,1,0:T(8,128)(2,1)}, f32[1,192]{1,0:T(1,128)}, bf16[64,384]{1,0:T(8,128)(2,1)}, bf16[64,384]{1,...) custom-call(s32[3]{0:T(128)} %pad_add_fusion.refs_0_, bf16[128,256]{1,0:T(8,128)(2,1)} %refs_7_.1, ...), custom_call_target="tpu_custom_call" | custom-call | tf_op jit(solution)/shard_map/prepare/pallas_call | solution.py:60
  6.9 4.0 %collective-permute-start.3 = (bf16[336,256]{1,0:T(8,128)(2,1)}, bf16[336,256]{1,0:T(8,128)(2,1)S(1)}, u32[]{:S(2)}, u32[]{:S(2)}) collective-permute-start(bf16[336,256]{1,0:T(8,128)(2,1)} %get-tuple-element.38), channel_id=1, source_target_pairs={{0,3},{1,2},{2,1},{3,0},{4,7},{5,6},{6,5},{7,4},{8,11},{9,10},{10,... | collective-permute-start | bytes 516104 | tf_op jit(solution)/shard_map/ppermute | solution.py:373
  10.9 2.1 %collective-permute-start.2 = (bf16[336,256]{1,0:T(8,128)(2,1)}, bf16[336,256]{1,0:T(8,128)(2,1)S(1)}, u32[]{:S(2)}, u32[]{:S(2)}) collective-permute-start(bf16[336,256]{1,0:T(8,128)(2,1)} %get-tuple-element.38), channel_id=1, source_target_pairs={{0,2},{1,3},{2,0},{3,1},{4,6},{5,7},{6,4},{7,5},{8,10},{9,11},{10,... | collective-permute-start | bytes 516104 | tf_op jit(solution)/shard_map/ppermute | solution.py:373
  13.0 2.1 %collective-permute-start.1 = (bf16[336,256]{1,0:T(8,128)(2,1)}, bf16[336,256]{1,0:T(8,128)(2,1)S(1)}, u32[]{:S(2)}, u32[]{:S(2)}) collective-permute-start(bf16[336,256]{1,0:T(8,128)(2,1)} %get-tuple-element.38), channel_id=1, source_target_pairs={{0,1},{1,0},{2,3},{3,2},{4,5},{5,4},{6,7},{7,6},{8,9},{9,8},{10,11... | collective-permute-start | bytes 516104 | tf_op jit(solution)/shard_map/ppermute | solution.py:373
  15.2 1.2 collective-permute-done.3
  16.4 3.4 %collective-permute-done.2 = bf16[336,256]{1,0:T(8,128)(2,1)S(1)} collective-permute-done((bf16[336,256]{1,0:T(8,128)(2,1)}, bf16[336,256]{1,0:T(8,128)(2,1)S(1)}, u32[]{:S(2)}, u32[]{:S(2)}) %collective-permute-start.2) | collective-permute-done | bytes 172064 | tf_op jit(solution)/shard_map/ppermute | solution.py:373
  19.8 0.0 collective-permute-done.1
  19.8 1.0 pad_maximum_fusion.refs_0_.refs_1_
  20.8 0.0 copy-start.1
  20.8 0.0 collective-permute-done.refs_2_
  20.8 0.0 copy-start.8
  20.8 0.0 copy-start.5
  20.8 0.0 copy-start.18
  20.8 0.0 copy-start.17
  20.8 0.0 copy-start.16
  20.8 0.8 copy-done.8
  21.6 13.3 %all-to-all-start = ((bf16[8,128,256]{2,1,0:T(8,128)(2,1)}), bf16[8,128,256]{2,1,0:T(8,128)(2,1)S(1)}, u32[]{:S(2)}, u32[]{:S(2)}) async-start(bf16[8,128,256]{2,1,0:T(8,128)(2,1)} %get-tuple-element.39), calls=%async_computation | async-start | bytes 1048576 | tf_op jit(solution)/shard_map/all_to_all | solution.py:378
  34.9 4.4 %collective-permute-start.5 = (bf16[4,336,256]{2,1,0:T(8,128)(2,1)S(1)}, bf16[4,336,256]{2,1,0:T(8,128)(2,1)S(1)}, u32[]{:S(2)}, u32[]{:S(2)}) collective-permute-start(bf16[4,336,256]{2,1,0:T(8,128)(2,1)S(1)} %pad_maximum_fusion.refs_0_.refs_1_), channel_id=1, source_target_pairs={{0,12},{1,13},{2,14},{3,15},{4,0},{5,1},{6,2},{7,3},{8,4},{9,5},{1... | collective-permute-start | bytes 2064392 | tf_op jit(solution)/shard_map/ppermute | solution.py:382
  39.3 1.9 %collective-permute-start.4 = (bf16[4,336,256]{2,1,0:T(8,128)(2,1)S(1)}, bf16[4,336,256]{2,1,0:T(8,128)(2,1)S(1)}, u32[]{:S(2)}, u32[]{:S(2)}) collective-permute-start(bf16[4,336,256]{2,1,0:T(8,128)(2,1)S(1)} %pad_maximum_fusion.refs_0_.refs_1_), channel_id=1, source_target_pairs={{0,4},{1,5},{2,6},{3,7},{4,8},{5,9},{6,10},{7,11},{8,12},{9,13},{1... | collective-permute-start | bytes 2064392 | tf_op jit(solution)/shard_map/ppermute | solution.py:382
  41.2 0.0 copy-done.5
  41.2 4.6 %collective-permute-start.6 = (bf16[1024,256]{1,0:T(8,128)(2,1)S(1)}, bf16[1024,256]{1,0:T(8,128)(2,1)S(1)}, u32[]{:S(2)}, u32[]{:S(2)}) collective-permute-start(bf16[1024,256]{1,0:T(8,128)(2,1)S(1)} %bitcast.20), channel_id=1, source_target_pairs={{0,256},{16,272},{32,288},{48,304},{64,320},{80,336},{96,352},{112... | collective-permute-start | bytes 1572872 | tf_op jit(solution)/shard_map/ppermute | solution.py:344
  45.9 2.1 %collective-permute-start.7 = (bf16[1024,256]{1,0:T(8,128)(2,1)}, bf16[1024,256]{1,0:T(8,128)(2,1)S(1)}, u32[]{:S(2)}, u32[]{:S(2)}) collective-permute-start(bf16[1024,256]{1,0:T(8,128)(2,1)} %copy-done.8), channel_id=1, source_target_pairs={{0,256},{16,272},{32,288},{48,304},{64,320},{80,336},{96,352},{112... | collective-permute-start | bytes 1572872 | tf_op jit(solution)/shard_map/ppermute | solution.py:344
  48.0 2.6 %collective-permute-start.8 = (bf16[64,384]{1,0:T(8,128)(2,1)S(1)}, bf16[64,384]{1,0:T(8,128)(2,1)S(1)}, u32[]{:S(2)}, u32[]{:S(2)}) collective-permute-start(bf16[64,384]{1,0:T(8,128)(2,1)S(1)} %copy-done.18), channel_id=1, source_target_pairs={{0,16},{16,0},{32,48},{48,32},{64,80},{80,64},{96,112},{112,96},{1... | collective-permute-start | bytes 147464 | tf_op jit(solution)/shard_map/ppermute | solution.py:344
  50.7 6.0 %collective-permute-done.6.refs_3_ = bf16[1024,256]{1,0:T(8,128)(2,1)S(1)} collective-permute-done((bf16[1024,256]{1,0:T(8,128)(2,1)S(1)}, bf16[1024,256]{1,0:T(8,128)(2,1)S(1)}, u32[]{:S(2)}, u32[]{:S(2)}) %collective-permute-start.6) | collective-permute-done | bytes 524320 | tf_op jit(solution)/shard_map/ppermute | solution.py:344
  56.7 4.8 %collective-permute-start.9 = (bf16[64,384]{1,0:T(8,128)(2,1)S(1)}, bf16[64,384]{1,0:T(8,128)(2,1)S(1)}, u32[]{:S(2)}, u32[]{:S(2)}) collective-permute-start(bf16[64,384]{1,0:T(8,128)(2,1)S(1)} %copy-done.17), channel_id=1, source_target_pairs={{0,256},{16,272},{32,288},{48,304},{64,320},{80,336},{96,352},{112... | collective-permute-start | bytes 147464 | tf_op jit(solution)/shard_map/ppermute | solution.py:344
  61.5 6.5 %collective-permute-done.7.refs_4_ = bf16[1024,256]{1,0:T(8,128)(2,1)S(1)} collective-permute-done((bf16[1024,256]{1,0:T(8,128)(2,1)}, bf16[1024,256]{1,0:T(8,128)(2,1)S(1)}, u32[]{:S(2)}, u32[]{:S(2)}) %collective-permute-start.7) | collective-permute-done | bytes 524320 | tf_op jit(solution)/shard_map/ppermute | solution.py:344
  67.9 0.0 copy-done.16
  67.9 5.2 %collective-permute-start.10 = (bf16[64,384]{1,0:T(8,128)(2,1)S(1)}, bf16[64,384]{1,0:T(8,128)(2,1)S(1)}, u32[]{:S(2)}, u32[]{:S(2)}) collective-permute-start(bf16[64,384]{1,0:T(8,128)(2,1)S(1)} %copy-done.16), channel_id=1, source_target_pairs={{0,272},{16,256},{32,304},{48,288},{64,336},{80,320},{96,368},{112... | collective-permute-start | bytes 147464 | tf_op jit(solution)/shard_map/ppermute | solution.py:344
  73.1 0.0 collective-permute-done.5.refs_4_.refs_5_
  73.2 0.0 copy-done.9
  73.2 0.0 copy-done.10
  73.2 0.0 copy-start.2
  73.2 0.0 collective-permute-done.4.refs_1_.refs_2_
  73.2 0.0 all-to-all-done.refs_0_
  73.2 0.0 copy-start.4
  73.2 0.0 collective-permute-done.8.refs_6_
  73.2 0.0 copy-start.11
  73.2 0.0 collective-permute-done.9.refs_7_
  73.3 0.0 copy-start.12
  73.3 1.9 %collective-permute-done.10.refs_8_ = bf16[64,384]{1,0:T(8,128)(2,1)S(1)} collective-permute-done((bf16[64,384]{1,0:T(8,128)(2,1)S(1)}, bf16[64,384]{1,0:T(8,128)(2,1)S(1)}, u32[]{:S(2)}, u32[]{:S(2)}) %collective-permute-start.10) | collective-permute-done | bytes 49184 | tf_op jit(solution)/shard_map/ppermute | solution.py:344
  75.2 0.0 copy-done.12
  75.2 0.6 copy-done.13
  75.8 9.1 %memory.1 = bf16[8,176,256]{2,1,0:T(8,128)(2,1)} custom-call(bf16[8,128,256]{2,1,0:T(8,128)(2,1)} %copy-done.4, bf16[1024,256]{1,0:T(8,128)(2,1)} %bitcast.18, bf16[1024,256]{1,0:T(8,128)(2,1)} %copy-done.8, bf16[1024,256]{1,0:T(8,128)(2,1)} %copy-done.9, bf16[1024,256]{1,0:T(8,128)(2,1)} %copy-done.10, bf16[64,384]{1,0:T(8,128)(2,1)} %get-tuple-element.47.refs_5_, ...), custom_call_target="tpu_custom_call" | custom-call | tf_op jit(solution)/shard_map/memory/pallas_call | solution.py:60
  84.9 11.5 %all-to-all-start.1 = ((bf16[8,176,256]{2,1,0:T(8,128)(2,1)}), bf16[8,176,256]{2,1,0:T(8,128)(2,1)S(1)}, u32[]{:S(2)}, u32[]{:S(2)}) async-start(bf16[8,176,256]{2,1,0:T(8,128)(2,1)} %memory.1), calls=%async_computation.1 | async-start | bytes 1441792 | tf_op jit(solution)/shard_map/all_to_all | solution.py:396
  96.3 0.0 copy-done.3
  96.4 4.3 %collective-permute-start.12 = (bf16[2,336,256]{2,1,0:T(8,128)(2,1)S(1)}, bf16[2,336,256]{2,1,0:T(8,128)(2,1)S(1)}, u32[]{:S(2)}, u32[]{:S(2)}) collective-permute-start(bf16[2,336,256]{2,1,0:T(8,128)(2,1)S(1)} %slice.7), channel_id=1, source_target_pairs={{0,12},{1,13},{2,14},{3,15},{4,0},{5,1},{6,2},{7,3},{8,4},{9,5},{1... | collective-permute-start | bytes 1032200 | tf_op jit(solution)/shard_map/ppermute | solution.py:382
  100.7 1.9 %collective-permute-start.11 = (bf16[2,336,256]{2,1,0:T(8,128)(2,1)S(1)}, bf16[2,336,256]{2,1,0:T(8,128)(2,1)S(1)}, u32[]{:S(2)}, u32[]{:S(2)}) collective-permute-start(bf16[2,336,256]{2,1,0:T(8,128)(2,1)S(1)} %slice.6), channel_id=1, source_target_pairs={{0,4},{1,5},{2,6},{3,7},{4,8},{5,9},{6,10},{7,11},{8,12},{9,13},{1... | collective-permute-start | bytes 1032200 | tf_op jit(solution)/shard_map/ppermute | solution.py:382
  102.6 2.2 %collective-permute-done.12.refs_3_.refs_4_ = bf16[2,336,256]{2,1,0:T(8,128)(2,1)S(1)} collective-permute-done((bf16[2,336,256]{2,1,0:T(8,128)(2,1)S(1)}, bf16[2,336,256]{2,1,0:T(8,128)(2,1)S(1)}, u32[]{:S(2)}, u32[]{:S(2)}) %collective-permute-start.12) | collective-permute-done | bytes 344096 | tf_op jit(solution)/shard_map/ppermute | solution.py:382
  104.9 5.3 %collective-permute-done.11.refs_2_.refs_3_ = bf16[2,336,256]{2,1,0:T(8,128)(2,1)S(1)} collective-permute-done((bf16[2,336,256]{2,1,0:T(8,128)(2,1)S(1)}, bf16[2,336,256]{2,1,0:T(8,128)(2,1)S(1)}, u32[]{:S(2)}, u32[]{:S(2)}) %collective-permute-start.11) | collective-permute-done | bytes 344096 | tf_op jit(solution)/shard_map/ppermute | solution.py:382
  110.2 0.7 copy-done.7
  110.9 4.2 %batch.1 = (f32[128,256]{1,0:T(8,128)}, f32[2,128]{1,0:T(2,128)}) custom-call(bf16[4,336,256]{2,1,0:T(8,128)(2,1)} %copy-done.1, bf16[4,336,256]{2,1,0:T(8,128)(2,1)} %copy-done.3, bf16[2,336,256]{2,1,0:T(8,128)(2,1)} %copy-done.7, bf16[2,336,256]{2,1,0:T(8,128)(2,1)} %copy-done.6, bf16[4,336,256]{2,1,0:T(8,128)(2,1)} %copy-done.2, ...), custom_call_target="tpu_custom_call" | custom-call | tf_op jit(solution)/shard_map/batch/pallas_call | solution.py:60
  115.1 20.3 %all-to-all-done.1.parts_ref.refs_1_ = bf16[8,176,256]{2,1,0:T(8,128)(2,1)S(1)} async-done(((bf16[8,176,256]{2,1,0:T(8,128)(2,1)}), bf16[8,176,256]{2,1,0:T(8,128)(2,1)S(1)}, u32[]{:S(2)}, u32[]{:S(2)}) %all-to-all-start.1) | async-done | bytes 720928 | tf_op jit(solution)/shard_map/all_to_all | solution.py:396
  135.4 0.9 copy-done
  136.2 1.7 %total.1 = (f32[1,128]{1,0:T(1,128)}, f32[1,128]{1,0:T(1,128)}) custom-call(bf16[8,176,256]{2,1,0:T(8,128)(2,1)} %copy-done, f32[2,128]{1,0:T(2,128)} %get-tuple-element.60.stat_ref), custom_call_target="tpu_custom_call" | custom-call | tf_op jit(solution)/shard_map/total/pallas_call | solution.py:60
  137.9 0.6 copy-done.15
  138.5 0.6 broadcast_in_dim.28
  139.1 6.5 %all-to-all-start.2 = ((f32[16,1,128]{2,1,0:T(1,128)}), f32[16,1,128]{2,1,0:T(1,128)S(1)}, u32[]{:S(2)}, u32[]{:S(2)}) async-start(f32[16,1,128]{2,1,0:T(1,128)} %broadcast_in_dim.28), calls=%async_computation.2 | async-start | bytes 16384 | tf_op jit(solution)/shard_map/all_to_all | solution.py:424
  145.6 2.5 %update.1 = bf16[1024,256]{1,0:T(8,128)(2,1)} custom-call(s32[3]{0:T(128)} %pad_add_fusion.refs_0_, bf16[8,176,256]{2,1,0:T(8,128)(2,1)} %copy-done, bf16[1024,256]{1,0:T(8,128)(2,1)} %bitcast.19), custom_call_target="tpu_custom_call" | custom-call | tf_op jit(solution)/shard_map/update/pallas_call | solution.py:60
  148.1 2.0 %queries.1 = f32[128,256]{1,0:T(8,128)} custom-call(bf16[8,176,256]{2,1,0:T(8,128)(2,1)} %copy-done, f32[1,128]{1,0:T(1,128)} %get-tuple-element.62.lt_ref, f32[128,256]{1,0:T(8,128)} %get-tuple-element.63.batch_ref, f32[2,128]{1,0:T(2,128)} %get-tuple-element.60.stat_ref, bf16[128,256]{1,0:T(8,128)(2,1)} %refs_8_.1), custom_call_target="tpu_custom_call" | custom-call | tf_op jit(solution)/shard_map/queries/pallas_call | solution.py:60
  150.1 0.9 all-to-all-done.2
  151.0 0.6 copy-done.14
  151.6 3.2 %items.1 = (f32[128,256]{1,0:T(8,128)}, f32[64,256]{1,0:T(8,128)}) custom-call(s32[3]{0:T(128)} %pad_add_fusion.refs_0_, bf16[4,336,256]{2,1,0:T(8,128)(2,1)} %copy-done.1, bf16[4,336,256]{2,1,0:T(8,128)(2,1)} %copy-done.3, bf16[2,336,256]{2,1,0:T(8,128)(2,1)} %copy-done.7, bf16[2,336,256]{2,1,0:T(8,128)(2,1)} %copy-done.6, bf16[4,336,256]{2,1,0:T(8,128)(2,1)} %copy-done.2, ...), custom_call_target="tpu_custom_call" | custom-call | tf_op jit(solution)/shard_map/items/pallas_call | solution.py:60
  (18 shorter events, 0.1 us)
Async XLA Ops:
  0.6 20.2 %collective-permute-start = (bf16[1024,256]{1,0:T(8,128)(2,1)}, bf16[1024,256]{1,0:T(8,128)(2,1)S(1)}, u32[]{:S(2)}, u32[]{:S(2)}) collective-permute-start(bf16[1024,256]{1,0:T(8,128)(2,1)} %bitcast.17), channel_id=1, source_target_pairs={{0,16},{16,0},{32,48},{48,32},{64,80},{80,64},{96,112},{112,96},{1... | collective-permute-start | bytes 1572872 | tf_op jit(solution)/shard_map/ppermute | solution.py:344
  6.9 9.5 %collective-permute-start.3 = (bf16[336,256]{1,0:T(8,128)(2,1)}, bf16[336,256]{1,0:T(8,128)(2,1)S(1)}, u32[]{:S(2)}, u32[]{:S(2)}) collective-permute-start(bf16[336,256]{1,0:T(8,128)(2,1)} %get-tuple-element.38), channel_id=1, source_target_pairs={{0,3},{1,2},{2,1},{3,0},{4,7},{5,6},{6,5},{7,4},{8,11},{9,10},{10,... | collective-permute-start | bytes 516104 | tf_op jit(solution)/shard_map/ppermute | solution.py:373
  10.9 8.8 %collective-permute-start.2 = (bf16[336,256]{1,0:T(8,128)(2,1)}, bf16[336,256]{1,0:T(8,128)(2,1)S(1)}, u32[]{:S(2)}, u32[]{:S(2)}) collective-permute-start(bf16[336,256]{1,0:T(8,128)(2,1)} %get-tuple-element.38), channel_id=1, source_target_pairs={{0,2},{1,3},{2,0},{3,1},{4,6},{5,7},{6,4},{7,5},{8,10},{9,11},{10,... | collective-permute-start | bytes 516104 | tf_op jit(solution)/shard_map/ppermute | solution.py:373
  13.0 6.7 %collective-permute-start.1 = (bf16[336,256]{1,0:T(8,128)(2,1)}, bf16[336,256]{1,0:T(8,128)(2,1)S(1)}, u32[]{:S(2)}, u32[]{:S(2)}) collective-permute-start(bf16[336,256]{1,0:T(8,128)(2,1)} %get-tuple-element.38), channel_id=1, source_target_pairs={{0,1},{1,0},{2,3},{3,2},{4,5},{5,4},{6,7},{7,6},{8,9},{9,8},{10,11... | collective-permute-start | bytes 516104 | tf_op jit(solution)/shard_map/ppermute | solution.py:373
  20.8 64.1 %copy-start.1 = (bf16[4,336,256]{2,1,0:T(8,128)(2,1)}, bf16[4,336,256]{2,1,0:T(8,128)(2,1)S(1)}, u32[]{:S(2)}) copy-start(bf16[4,336,256]{2,1,0:T(8,128)(2,1)S(1)} %pad_maximum_fusion.refs_0_.refs_1_) | copy-start | bytes 2064388
  20.8 0.8 copy-start.8
  20.8 20.4 %copy-start.5 = (bf16[1,1024,256]{2,1,0:T(8,128)(2,1)S(1)}, bf16[1,1024,256]{2,1,0:T(8,128)(2,1)}, u32[]{:S(2)}) copy-start(bf16[1,1024,256]{2,1,0:T(8,128)(2,1)} %param.15) | copy-start | bytes 1572868
  20.8 27.2 %copy-start.18 = (bf16[64,384]{1,0:T(8,128)(2,1)S(1)}, bf16[64,384]{1,0:T(8,128)(2,1)}, u32[]{:S(2)}) copy-start(bf16[64,384]{1,0:T(8,128)(2,1)} %get-tuple-element.48) | copy-start | bytes 147460
  20.8 35.9 %copy-start.17 = (bf16[64,384]{1,0:T(8,128)(2,1)S(1)}, bf16[64,384]{1,0:T(8,128)(2,1)}, u32[]{:S(2)}) copy-start(bf16[64,384]{1,0:T(8,128)(2,1)} %get-tuple-element.49) | copy-start | bytes 147460
  20.8 47.1 %copy-start.16 = (bf16[64,384]{1,0:T(8,128)(2,1)S(1)}, bf16[64,384]{1,0:T(8,128)(2,1)}, u32[]{:S(2)}) copy-start(bf16[64,384]{1,0:T(8,128)(2,1)} %get-tuple-element.50) | copy-start | bytes 147460
  21.6 51.6 %all-to-all-start = ((bf16[8,128,256]{2,1,0:T(8,128)(2,1)}), bf16[8,128,256]{2,1,0:T(8,128)(2,1)S(1)}, u32[]{:S(2)}, u32[]{:S(2)}) async-start(bf16[8,128,256]{2,1,0:T(8,128)(2,1)} %get-tuple-element.39), calls=%async_computation | async-start | bytes 1048576 | tf_op jit(solution)/shard_map/all_to_all | solution.py:378
  34.9 38.2 %collective-permute-start.5 = (bf16[4,336,256]{2,1,0:T(8,128)(2,1)S(1)}, bf16[4,336,256]{2,1,0:T(8,128)(2,1)S(1)}, u32[]{:S(2)}, u32[]{:S(2)}) collective-permute-start(bf16[4,336,256]{2,1,0:T(8,128)(2,1)S(1)} %pad_maximum_fusion.refs_0_.refs_1_), channel_id=1, source_target_pairs={{0,12},{1,13},{2,14},{3,15},{4,0},{5,1},{6,2},{7,3},{8,4},{9,5},{1... | collective-permute-start | bytes 2064392 | tf_op jit(solution)/shard_map/ppermute | solution.py:382
  39.3 33.9 %collective-permute-start.4 = (bf16[4,336,256]{2,1,0:T(8,128)(2,1)S(1)}, bf16[4,336,256]{2,1,0:T(8,128)(2,1)S(1)}, u32[]{:S(2)}, u32[]{:S(2)}) collective-permute-start(bf16[4,336,256]{2,1,0:T(8,128)(2,1)S(1)} %pad_maximum_fusion.refs_0_.refs_1_), channel_id=1, source_target_pairs={{0,4},{1,5},{2,6},{3,7},{4,8},{5,9},{6,10},{7,11},{8,12},{9,13},{1... | collective-permute-start | bytes 2064392 | tf_op jit(solution)/shard_map/ppermute | solution.py:382
  41.2 15.4 %collective-permute-start.6 = (bf16[1024,256]{1,0:T(8,128)(2,1)S(1)}, bf16[1024,256]{1,0:T(8,128)(2,1)S(1)}, u32[]{:S(2)}, u32[]{:S(2)}) collective-permute-start(bf16[1024,256]{1,0:T(8,128)(2,1)S(1)} %bitcast.20), channel_id=1, source_target_pairs={{0,256},{16,272},{32,288},{48,304},{64,320},{80,336},{96,352},{112... | collective-permute-start | bytes 1572872 | tf_op jit(solution)/shard_map/ppermute | solution.py:344
  45.9 22.0 %collective-permute-start.7 = (bf16[1024,256]{1,0:T(8,128)(2,1)}, bf16[1024,256]{1,0:T(8,128)(2,1)S(1)}, u32[]{:S(2)}, u32[]{:S(2)}) collective-permute-start(bf16[1024,256]{1,0:T(8,128)(2,1)} %copy-done.8), channel_id=1, source_target_pairs={{0,256},{16,272},{32,288},{48,304},{64,320},{80,336},{96,352},{112... | collective-permute-start | bytes 1572872 | tf_op jit(solution)/shard_map/ppermute | solution.py:344
  48.0 25.2 %collective-permute-start.8 = (bf16[64,384]{1,0:T(8,128)(2,1)S(1)}, bf16[64,384]{1,0:T(8,128)(2,1)S(1)}, u32[]{:S(2)}, u32[]{:S(2)}) collective-permute-start(bf16[64,384]{1,0:T(8,128)(2,1)S(1)} %copy-done.18), channel_id=1, source_target_pairs={{0,16},{16,0},{32,48},{48,32},{64,80},{80,64},{96,112},{112,96},{1... | collective-permute-start | bytes 147464 | tf_op jit(solution)/shard_map/ppermute | solution.py:344
  56.7 16.5 %copy-start.9 = (bf16[1024,256]{1,0:T(8,128)(2,1)}, bf16[1024,256]{1,0:T(8,128)(2,1)S(1)}, u32[]{:S(2)}) copy-start(bf16[1024,256]{1,0:T(8,128)(2,1)S(1)} %collective-permute-done.6.refs_3_) | copy-start | bytes 1572868
  56.7 16.6 %collective-permute-start.9 = (bf16[64,384]{1,0:T(8,128)(2,1)S(1)}, bf16[64,384]{1,0:T(8,128)(2,1)S(1)}, u32[]{:S(2)}, u32[]{:S(2)}) collective-permute-start(bf16[64,384]{1,0:T(8,128)(2,1)S(1)} %copy-done.17), channel_id=1, source_target_pairs={{0,256},{16,272},{32,288},{48,304},{64,320},{80,336},{96,352},{112... | collective-permute-start | bytes 147464 | tf_op jit(solution)/shard_map/ppermute | solution.py:344
  67.9 5.2 %copy-start.10 = (bf16[1024,256]{1,0:T(8,128)(2,1)}, bf16[1024,256]{1,0:T(8,128)(2,1)S(1)}, u32[]{:S(2)}) copy-start(bf16[1024,256]{1,0:T(8,128)(2,1)S(1)} %collective-permute-done.7.refs_4_) | copy-start | bytes 1572868
  67.9 7.2 %collective-permute-start.10 = (bf16[64,384]{1,0:T(8,128)(2,1)S(1)}, bf16[64,384]{1,0:T(8,128)(2,1)S(1)}, u32[]{:S(2)}, u32[]{:S(2)}) collective-permute-start(bf16[64,384]{1,0:T(8,128)(2,1)S(1)} %copy-done.16), channel_id=1, source_target_pairs={{0,272},{16,256},{32,304},{48,288},{64,336},{80,320},{96,368},{112... | collective-permute-start | bytes 147464 | tf_op jit(solution)/shard_map/ppermute | solution.py:344
  73.2 23.2 %copy-start.2 = (bf16[4,336,256]{2,1,0:T(8,128)(2,1)}, bf16[4,336,256]{2,1,0:T(8,128)(2,1)S(1)}, u32[]{:S(2)}) copy-start(bf16[4,336,256]{2,1,0:T(8,128)(2,1)S(1)} %collective-permute-done.5.refs_4_.refs_5_) | copy-start | bytes 2064388
  73.2 23.1 %copy-start.3 = (bf16[4,336,256]{2,1,0:T(8,128)(2,1)}, bf16[4,336,256]{2,1,0:T(8,128)(2,1)S(1)}, u32[]{:S(2)}) copy-start(bf16[4,336,256]{2,1,0:T(8,128)(2,1)S(1)} %collective-permute-done.4.refs_1_.refs_2_) | copy-start | bytes 2064388
  73.2 1.9 %copy-start.4 = (bf16[8,128,256]{2,1,0:T(8,128)(2,1)}, bf16[8,128,256]{2,1,0:T(8,128)(2,1)S(1)}, u32[]{:S(2)}) copy-start(bf16[8,128,256]{2,1,0:T(8,128)(2,1)S(1)} %all-to-all-done.refs_0_) | copy-start | bytes 1572868
  73.2 1.9 %copy-start.11 = (bf16[64,384]{1,0:T(8,128)(2,1)}, bf16[64,384]{1,0:T(8,128)(2,1)S(1)}, u32[]{:S(2)}) copy-start(bf16[64,384]{1,0:T(8,128)(2,1)S(1)} %collective-permute-done.8.refs_6_) | copy-start | bytes 147460
  73.3 1.9 %copy-start.12 = (bf16[64,384]{1,0:T(8,128)(2,1)}, bf16[64,384]{1,0:T(8,128)(2,1)S(1)}, u32[]{:S(2)}) copy-start(bf16[64,384]{1,0:T(8,128)(2,1)S(1)} %collective-permute-done.9.refs_7_) | copy-start | bytes 147460
  75.1 0.6 copy-start.13
  84.9 50.5 %all-to-all-start.1 = ((bf16[8,176,256]{2,1,0:T(8,128)(2,1)}), bf16[8,176,256]{2,1,0:T(8,128)(2,1)S(1)}, u32[]{:S(2)}, u32[]{:S(2)}) async-start(bf16[8,176,256]{2,1,0:T(8,128)(2,1)} %memory.1), calls=%async_computation.1 | async-start | bytes 1441792 | tf_op jit(solution)/shard_map/all_to_all | solution.py:396
  96.4 8.5 %collective-permute-start.12 = (bf16[2,336,256]{2,1,0:T(8,128)(2,1)S(1)}, bf16[2,336,256]{2,1,0:T(8,128)(2,1)S(1)}, u32[]{:S(2)}, u32[]{:S(2)}) collective-permute-start(bf16[2,336,256]{2,1,0:T(8,128)(2,1)S(1)} %slice.7), channel_id=1, source_target_pairs={{0,12},{1,13},{2,14},{3,15},{4,0},{5,1},{6,2},{7,3},{8,4},{9,5},{1... | collective-permute-start | bytes 1032200 | tf_op jit(solution)/shard_map/ppermute | solution.py:382
  100.7 9.5 %collective-permute-start.11 = (bf16[2,336,256]{2,1,0:T(8,128)(2,1)S(1)}, bf16[2,336,256]{2,1,0:T(8,128)(2,1)S(1)}, u32[]{:S(2)}, u32[]{:S(2)}) collective-permute-start(bf16[2,336,256]{2,1,0:T(8,128)(2,1)S(1)} %slice.6), channel_id=1, source_target_pairs={{0,4},{1,5},{2,6},{3,7},{4,8},{5,9},{6,10},{7,11},{8,12},{9,13},{1... | collective-permute-start | bytes 1032200 | tf_op jit(solution)/shard_map/ppermute | solution.py:382
  104.9 5.3 %copy-start.6 = (bf16[2,336,256]{2,1,0:T(8,128)(2,1)}, bf16[2,336,256]{2,1,0:T(8,128)(2,1)S(1)}, u32[]{:S(2)}) copy-start(bf16[2,336,256]{2,1,0:T(8,128)(2,1)S(1)} %collective-permute-done.12.refs_3_.refs_4_) | copy-start | bytes 1032196
  110.2 0.7 copy-start.7
  135.4 0.9 copy-start
  137.9 0.6 copy-start.15
  139.1 11.9 %all-to-all-start.2 = ((f32[16,1,128]{2,1,0:T(1,128)}), f32[16,1,128]{2,1,0:T(1,128)S(1)}, u32[]{:S(2)}, u32[]{:S(2)}) async-start(f32[16,1,128]{2,1,0:T(1,128)} %broadcast_in_dim.28), calls=%async_computation.2 | async-start | bytes 16384 | tf_op jit(solution)/shard_map/all_to_all | solution.py:424
  151.0 0.6 copy-start.14

commit v5 on v4

--- a/solution.py
+++ b/solution.py
@@ -80,10 +80,13 @@
     ng_count_ref,
     owner_ref,
     slot_ref,
+    mem_ref,
     block_ref,
     copies_ref,
     sh_ref,
-    *out_refs,
+    z_ref,
+    y_ref,
+    own_ref,
 ):
     rows, negs = q_ref.shape[0], ng_ref.shape[0]
     keys = rows + negs
@@ -129,12 +132,18 @@
     details = jnp.where(
         lane == 0.0, high, jnp.where(lane == 1.0, low, jnp.where(lane == 2.0, 1.0, 0.0))
     )
-    width = it_ref.shape[1]
     each = places // 4
-    for c, out_ref in enumerate(out_refs):
+    held = mem_ref.shape[0]
+    z_ref[0:held, :] = mem_ref[...]
+    y_ref[0:held, :] = mem_ref[...]
+    for c, (ref, at) in enumerate(
+        ((own_ref, 0), (z_ref, held), (y_ref, held), (z_ref, held + each + each // 2))
+    ):
         some = chosen[c * each : (c + 1) * each, :]
-        out_ref[:, 0:width] = dot_plain(some, it_ref[...]).astype(BF16)
-        out_ref[:, width:] = dot_plain(some, details.astype(BF16)).astype(BF16)
+        ref[at : at + each, :] = dot_plain(some, it_ref[...]).astype(BF16)
+        slots = dot_plain(some, details.astype(BF16)).astype(BF16)
+        ref[at + each : at + each + each // 2, 0:128] = slots[0 : each // 2, :]
+        ref[at + each : at + each + each // 2, 128:256] = slots[each // 2 :, :]
 
 
 def update_kernel(block, each, place_ref, got_ref, mem_ref, new_ref):
@@ -181,28 +190,36 @@
 
 
 def memory_kernel(tile, *refs):
-    q_ref, *mem_refs, item0_ref, item1_ref, item2_ref, item3_ref, out_ref = refs
+    q_ref, own_ref, mem_ref, z_ref, y_ref, zy_ref, out_ref = refs
+    mem_refs = (mem_ref, z_ref, y_ref, zy_ref)
+    held = mem_ref.shape[0]
     pairs, block, width = q_ref.shape
-    each = item0_ref.shape[0] // pairs
+    span = own_ref.shape[0]
+    total = span * 2 // 3
+    each = total // pairs
     extra = 2 * each
+    sources = ((own_ref, 0), (z_ref, held), (y_ref, held), (zy_ref, held + span))
     for k in range(0, pairs, 2):
-        group = [
-            ref[k * each : (k + 2) * each, :].astype(F32)
-            for ref in (item0_ref, item1_ref, item2_ref, item3_ref)
-        ]
+        items, slots = [], []
+        for ref, at in sources:
+            items.append(ref[at + k * each : at + (k + 2) * each, :].astype(F32))
+            row, side = (k * each) % (total // 2), (k * each) // (total // 2) * 128
+            slots.append(
+                ref[at + total + row : at + total + row + extra, side : side + 128].astype(F32)
+            )
         for n in range(2):
-            one = [rows[n * each : (n + 1) * each, :] for rows in group]
-            near = jnp.concatenate(one[0:2], axis=0)
-            far = jnp.concatenate(one[2:4], axis=0)
-            out_ref[k + n, block + extra : block + 2 * extra, :] = near[:, 0:width].astype(BF16)
-            out_ref[k + n, block + 2 * extra :, :] = far[:, 0:width].astype(BF16)
-            out_ref[k + n, block : block + extra, block:] = (
-                near[:, width:] + far[:, width:]
+            cut = slice(n * each, (n + 1) * each)
+            for h in range(2):
+                out_ref[k + n, block + (1 + h) * extra : block + (2 + h) * extra, :] = (
+                    jnp.concatenate([items[2 * h][cut], items[2 * h + 1][cut]], axis=0)
+                ).astype(BF16)
+            out_ref[k + n, block : block + extra, block:] = jnp.concatenate(
+                [slots[0][cut] + slots[2][cut], slots[1][cut] + slots[3][cut]], axis=0
             ).astype(BF16)
     step = 1024
     pieces, open_piece = [], []
     for ref in mem_refs:
-        for at in range(0, ref.shape[0], step):
+        for at in range(0, held, step):
             open_piece.append(ref[at : at + step, :])
             if sum(p.shape[0] for p in open_piece) >= step:
                 pieces.append(jnp.concatenate(open_piece, axis=0))
@@ -345,7 +362,9 @@
 
     place = jnp.stack([lax.axis_index("yh"), lax.axis_index("zl"), lax.axis_index("dp")])
     capacity = max(2, 2 * rows // cycle)
-    block, copies, shift, *new_items = call(
+    held = mem.shape[0]
+    span = shards * capacity * 3 // 2
+    block, copies, shift, z_sent, y_sent, own_items = call(
         lambda *refs: prepare_kernel(capacity, group, *refs),
         (
             place,
@@ -357,26 +376,31 @@
             negative_counts[None, :],
             owners.reshape(1, rows),
             memory_slots[None, :],
+            mem,
         ),
         (
             jax.ShapeDtypeStruct((rows + keys + 16, width), BF16),
             jax.ShapeDtypeStruct((shards, rows, width), BF16),
             jax.ShapeDtypeStruct((1, keys), F32),
-        )
-        + (jax.ShapeDtypeStruct((shards * capacity, width + 128), BF16),) * 4,
+            jax.ShapeDtypeStruct((held + 2 * span, width), BF16),
+            jax.ShapeDtypeStruct((held + span, width), BF16),
+            jax.ShapeDtypeStruct((span, width), BF16),
+        ),
         "prepare",
     )
-    new_items = [new_items[0]] + [beside(new_items[c], c // 2, c % 2) for c in range(1, 4)]
-
     near = 4
     near_blocks = [block] + [
         lax.ppermute(block, "dp", [(i, i ^ k) for i in range(group)]) for k in range(1, near)
     ]
     pair_blocks = jnp.stack(near_blocks)
-    z_rows = beside(mem, 0, 1)
-    copies, z_rows, pair_blocks = lax.optimization_barrier((copies, z_rows, pair_blocks))
+    z_rows = beside(z_sent, 0, 1)
+    y_rows = beside(y_sent, 1, 0)
+    copies, z_rows, y_rows, pair_blocks = lax.optimization_barrier(
+        (copies, z_rows, y_rows, pair_blocks)
+    )
+    zy_rows = beside(z_rows, 1, 0)
+    memory_blocks = [own_items, mem, z_rows, y_rows, zy_rows]
     arrived = lax.all_to_all(copies, "zh", 0, 0, tiled=True)
-    memory_blocks = [mem, z_rows, beside(mem, 1, 0), beside(z_rows, 1, 0)]
 
     def along(blocks, by):
         return lax.ppermute(blocks, "dp", [(i, (i + near * by) % group) for i in range(group)])
@@ -388,7 +412,7 @@
 
     (parts,) = call(
         lambda *refs: memory_kernel(512, *refs),
-        (arrived, *memory_blocks, *new_items),
+        (arrived, *memory_blocks),
         (jax.ShapeDtypeStruct((shards, rows + 6 * capacity, width), BF16),),
         "memory",
     )

time: 156 us -> 153 us (0.981)
  the two profiles are of different devices: /device:TPU:65 before, /device:TPU:33 now
where the time goes in v5:
time: 153 us; the launch traced here: 152 us
  starting transfers between devices  66.6 us (44%)
  waiting for transfers between devices  51.2 us (33%)
  Pallas kernels  25.6 us (17%)
  local copies, waits for them, and re-layouts  5.93 us (4%)
  other arithmetic  1.66 us (1%)
    pallas_call x7, Pallas kernels, call(): pl.pallas_call(kernel, out_shape=out_shape, in_specs=[scalars if operand....  25.6 us
    all_to_all x1, waiting for transfers between devices, local(): parts_back = lax.all_to_all(parts, 'zh', 0, 0, tiled=True)  17 us
    all_to_all x1, starting transfers between devices, local(): arrived = lax.all_to_all(copies, 'zh', 0, 0, tiled=True)  14.4 us
    ppermute x3, waiting for transfers between devices, beside(): return lax.ppermute(block, column, route)  13 us
    ppermute x4, starting transfers between devices, along(): lax.ppermute(blocks, 'dp', [(i, (i + near * by) % group) for i in range(g...  12.6 us
    ppermute x3, starting transfers between devices, local(): lax.ppermute(block, 'dp', [(i, i ^ k) for i in range(group)])  10.3 us
    ppermute x3, starting transfers between devices, beside(): return lax.ppermute(block, column, route)  10.2 us
    all_to_all x1, starting transfers between devices, local(): lax.all_to_all(jnp.broadcast_to(log_total[None], (group, 1, rows)), 'dp',...  10.2 us
  transfers between devices with their start and end apart: 13, of which 8 were waited for; matrix products, arithmetic and copies ran while one was open for 1% of the time, Pallas kernels for 6%

profile of v5, /device:TPU:33, one launch (start us, length us, event | category | flops | bytes accessed | tf_op | source)
XLA Modules:
  0.0 151.7 jit_solution(1989324628132854258)
XLA Ops:
  0.6 0.7 pad_add_fusion.refs_0_
  1.3 2.8 %prepare.1 = (bf16[336,256]{1,0:T(8,128)(2,1)}, bf16[8,128,256]{2,1,0:T(8,128)(2,1)}, f32[1,192]{1,0:T(1,128)}, bf16[1216,256]{1,0:T(8,128)(2,1)}, bf16[1120,256]{1,0:T(8,128)(2,1)}, /*index=5*/bf16[96,256]{1,0:T(8,128)(2,1)}) custom-call(s32[3]{0:T(128)} %pad_add_fusion.refs_0_, bf16[128,256]{1,0:T(8,128)(2,1)} %refs_7_.1, bf16[128,256]{1,0:T(8,128)(2,1)} %refs_8_.1, ...), custom_call_target="tpu_custom_call" | custom-call | tf_op jit(solution)/shard_map/prepare/pallas_call | solution.py:60
  4.0 1.9 %collective-permute-start = (bf16[1216,256]{1,0:T(8,128)(2,1)}, bf16[1216,256]{1,0:T(8,128)(2,1)S(1)}, u32[]{:S(2)}, u32[]{:S(2)}) collective-permute-start(bf16[1216,256]{1,0:T(8,128)(2,1)} %get-tuple-element.39), channel_id=1, source_target_pairs={{0,16},{16,0},{32,48},{48,32},{64,80},{80,64},{96,112},{112,96},{1... | collective-permute-start | bytes 1867784 | tf_op jit(solution)/shard_map/ppermute | solution.py:361
  6.0 4.8 %collective-permute-start.1 = (bf16[1120,256]{1,0:T(8,128)(2,1)}, bf16[1120,256]{1,0:T(8,128)(2,1)S(1)}, u32[]{:S(2)}, u32[]{:S(2)}) collective-permute-start(bf16[1120,256]{1,0:T(8,128)(2,1)} %get-tuple-element.40), channel_id=1, source_target_pairs={{0,256},{16,272},{32,288},{48,304},{64,320},{80,336},{96,352},{112... | collective-permute-start | bytes 1720328 | tf_op jit(solution)/shard_map/ppermute | solution.py:361
  10.8 3.2 %collective-permute-start.4 = (bf16[336,256]{1,0:T(8,128)(2,1)}, bf16[336,256]{1,0:T(8,128)(2,1)S(1)}, u32[]{:S(2)}, u32[]{:S(2)}) collective-permute-start(bf16[336,256]{1,0:T(8,128)(2,1)} %get-tuple-element.41), channel_id=1, source_target_pairs={{0,3},{1,2},{2,1},{3,0},{4,7},{5,6},{6,5},{7,4},{8,11},{9,10},{10,... | collective-permute-start | bytes 516104 | tf_op jit(solution)/shard_map/ppermute | solution.py:393
  14.0 5.2 %collective-permute-start.3 = (bf16[336,256]{1,0:T(8,128)(2,1)}, bf16[336,256]{1,0:T(8,128)(2,1)S(1)}, u32[]{:S(2)}, u32[]{:S(2)}) collective-permute-start(bf16[336,256]{1,0:T(8,128)(2,1)} %get-tuple-element.41), channel_id=1, source_target_pairs={{0,2},{1,3},{2,0},{3,1},{4,6},{5,7},{6,4},{7,5},{8,10},{9,11},{10,... | collective-permute-start | bytes 516104 | tf_op jit(solution)/shard_map/ppermute | solution.py:393
  19.2 1.9 %collective-permute-start.2 = (bf16[336,256]{1,0:T(8,128)(2,1)}, bf16[336,256]{1,0:T(8,128)(2,1)S(1)}, u32[]{:S(2)}, u32[]{:S(2)}) collective-permute-start(bf16[336,256]{1,0:T(8,128)(2,1)} %get-tuple-element.41), channel_id=1, source_target_pairs={{0,1},{1,0},{2,3},{3,2},{4,5},{5,4},{6,7},{7,6},{8,9},{9,8},{10,11... | collective-permute-start | bytes 516104 | tf_op jit(solution)/shard_map/ppermute | solution.py:393
  21.1 8.4 %collective-permute-done.4 = bf16[336,256]{1,0:T(8,128)(2,1)S(1)} collective-permute-done((bf16[336,256]{1,0:T(8,128)(2,1)}, bf16[336,256]{1,0:T(8,128)(2,1)S(1)}, u32[]{:S(2)}, u32[]{:S(2)}) %collective-permute-start.4) | collective-permute-done | bytes 172064 | tf_op jit(solution)/shard_map/ppermute | solution.py:393
  29.6 1.5 collective-permute-done.3
  31.0 0.0 collective-permute-done.2
  31.0 1.0 pad_maximum_fusion.refs_0_.refs_1_
  32.0 0.0 copy-start.1
  32.0 0.0 collective-permute-done.1.refs_4_
  32.1 0.0 copy-start.9
  32.1 0.0 collective-permute-done.refs_3_
  32.1 0.0 copy-start.7
  32.1 0.8 copy-done.9
  32.9 14.4 %all-to-all-start = ((bf16[8,128,256]{2,1,0:T(8,128)(2,1)}), bf16[8,128,256]{2,1,0:T(8,128)(2,1)S(1)}, u32[]{:S(2)}, u32[]{:S(2)}) async-start(bf16[8,128,256]{2,1,0:T(8,128)(2,1)} %get-tuple-element.42), calls=%async_computation | async-start | bytes 1048576 | tf_op jit(solution)/shard_map/all_to_all | solution.py:403
  47.3 4.4 %collective-permute-start.6 = (bf16[4,336,256]{2,1,0:T(8,128)(2,1)S(1)}, bf16[4,336,256]{2,1,0:T(8,128)(2,1)S(1)}, u32[]{:S(2)}, u32[]{:S(2)}) collective-permute-start(bf16[4,336,256]{2,1,0:T(8,128)(2,1)S(1)} %pad_maximum_fusion.refs_0_.refs_1_), channel_id=1, source_target_pairs={{0,12},{1,13},{2,14},{3,15},{4,0},{5,1},{6,2},{7,3},{8,4},{9,5},{1... | collective-permute-start | bytes 2064392 | tf_op jit(solution)/shard_map/ppermute | solution.py:406
  51.7 1.9 %collective-permute-start.5 = (bf16[4,336,256]{2,1,0:T(8,128)(2,1)S(1)}, bf16[4,336,256]{2,1,0:T(8,128)(2,1)S(1)}, u32[]{:S(2)}, u32[]{:S(2)}) collective-permute-start(bf16[4,336,256]{2,1,0:T(8,128)(2,1)S(1)} %pad_maximum_fusion.refs_0_.refs_1_), channel_id=1, source_target_pairs={{0,4},{1,5},{2,6},{3,7},{4,8},{5,9},{6,10},{7,11},{8,12},{9,13},{1... | collective-permute-start | bytes 2064392 | tf_op jit(solution)/shard_map/ppermute | solution.py:406
  53.6 3.5 %collective-permute-start.7 = (bf16[1216,256]{1,0:T(8,128)(2,1)S(1)}, bf16[1216,256]{1,0:T(8,128)(2,1)S(1)}, u32[]{:S(2)}, u32[]{:S(2)}) collective-permute-start(bf16[1216,256]{1,0:T(8,128)(2,1)S(1)} %collective-permute-done.refs_3_), channel_id=1, source_target_pairs={{0,256},{16,272},{32,288},{48,304},{64,320},{80,336},{96,352},{112... | collective-permute-start | bytes 1867784 | tf_op jit(solution)/shard_map/ppermute | solution.py:361
  57.1 13.0 %collective-permute-done.7.refs_5_ = bf16[1216,256]{1,0:T(8,128)(2,1)S(1)} collective-permute-done((bf16[1216,256]{1,0:T(8,128)(2,1)S(1)}, bf16[1216,256]{1,0:T(8,128)(2,1)S(1)}, u32[]{:S(2)}, u32[]{:S(2)}) %collective-permute-start.7) | collective-permute-done | bytes 622624 | tf_op jit(solution)/shard_map/ppermute | solution.py:361
  70.1 0.0 copy-start.8
  70.1 0.0 collective-permute-done.6.refs_4_.refs_5_
  70.1 0.8 copy-done.8
  71.0 0.0 copy-start.2
  71.0 0.0 collective-permute-done.5.refs_1_.refs_2_
  71.0 0.0 copy-start.3
  71.0 3.0 %all-to-all-done.refs_0_ = bf16[8,128,256]{2,1,0:T(8,128)(2,1)S(1)} async-done(((bf16[8,128,256]{2,1,0:T(8,128)(2,1)}), bf16[8,128,256]{2,1,0:T(8,128)(2,1)S(1)}, u32[]{:S(2)}, u32[]{:S(2)}) %all-to-all-start) | async-done | bytes 524320 | tf_op jit(solution)/shard_map/all_to_all | solution.py:403
  73.9 0.0 copy-start.4
  73.9 0.0 copy-done.7
  73.9 0.8 copy-done.4
  74.7 9.2 %memory.1 = bf16[8,176,256]{2,1,0:T(8,128)(2,1)} custom-call(bf16[8,128,256]{2,1,0:T(8,128)(2,1)} %copy-done.4, bf16[96,256]{1,0:T(8,128)(2,1)} %get-tuple-element.48.refs_1_, bf16[1024,256]{1,0:T(8,128)(2,1)} %bitcast.18, bf16[1216,256]{1,0:T(8,128)(2,1)} %copy-done.7, bf16[1120,256]{1,0:T(8,128)(2,1)} %copy-done.9, bf16[1216,256]{1,0:T(8,128)(2,1)} %copy-done.8), custom_call_target="tpu_custom_call" | custom-call | tf_op jit(solution)/shard_map/memory/pallas_call | solution.py:60
  83.9 0.0 copy-done.1
  83.9 8.8 %all-to-all-start.1 = ((bf16[8,176,256]{2,1,0:T(8,128)(2,1)}), bf16[8,176,256]{2,1,0:T(8,128)(2,1)S(1)}, u32[]{:S(2)}, u32[]{:S(2)}) async-start(bf16[8,176,256]{2,1,0:T(8,128)(2,1)} %memory.1), calls=%async_computation.1 | async-start | bytes 1441792 | tf_op jit(solution)/shard_map/all_to_all | solution.py:420
  92.7 0.0 copy-done.3
  92.8 0.0 copy-done.2
  92.8 4.4 %collective-permute-start.9 = (bf16[2,336,256]{2,1,0:T(8,128)(2,1)S(1)}, bf16[2,336,256]{2,1,0:T(8,128)(2,1)S(1)}, u32[]{:S(2)}, u32[]{:S(2)}) collective-permute-start(bf16[2,336,256]{2,1,0:T(8,128)(2,1)S(1)} %slice.7), channel_id=1, source_target_pairs={{0,12},{1,13},{2,14},{3,15},{4,0},{5,1},{6,2},{7,3},{8,4},{9,5},{1... | collective-permute-start | bytes 1032200 | tf_op jit(solution)/shard_map/ppermute | solution.py:406
  97.2 1.9 %collective-permute-start.8 = (bf16[2,336,256]{2,1,0:T(8,128)(2,1)S(1)}, bf16[2,336,256]{2,1,0:T(8,128)(2,1)S(1)}, u32[]{:S(2)}, u32[]{:S(2)}) collective-permute-start(bf16[2,336,256]{2,1,0:T(8,128)(2,1)S(1)} %slice.6), channel_id=1, source_target_pairs={{0,4},{1,5},{2,6},{3,7},{4,8},{5,9},{6,10},{7,11},{8,12},{9,13},{1... | collective-permute-start | bytes 1032200 | tf_op jit(solution)/shard_map/ppermute | solution.py:406
  99.1 2.2 %collective-permute-done.9.refs_3_.refs_4_ = bf16[2,336,256]{2,1,0:T(8,128)(2,1)S(1)} collective-permute-done((bf16[2,336,256]{2,1,0:T(8,128)(2,1)S(1)}, bf16[2,336,256]{2,1,0:T(8,128)(2,1)S(1)}, u32[]{:S(2)}, u32[]{:S(2)}) %collective-permute-start.9) | collective-permute-done | bytes 344096 | tf_op jit(solution)/shard_map/ppermute | solution.py:406
  101.4 0.0 copy-start.5
  101.4 5.2 %collective-permute-done.8.refs_2_.refs_3_ = bf16[2,336,256]{2,1,0:T(8,128)(2,1)S(1)} collective-permute-done((bf16[2,336,256]{2,1,0:T(8,128)(2,1)S(1)}, bf16[2,336,256]{2,1,0:T(8,128)(2,1)S(1)}, u32[]{:S(2)}, u32[]{:S(2)}) %collective-permute-start.8) | collective-permute-done | bytes 344096 | tf_op jit(solution)/shard_map/ppermute | solution.py:406
  106.6 0.0 copy-start.6
  106.6 0.0 copy-done.5
  106.6 0.7 copy-done.6
  107.3 4.2 %batch.1 = (f32[128,256]{1,0:T(8,128)}, f32[2,128]{1,0:T(2,128)}) custom-call(bf16[4,336,256]{2,1,0:T(8,128)(2,1)} %copy-done.1, bf16[4,336,256]{2,1,0:T(8,128)(2,1)} %copy-done.3, bf16[2,336,256]{2,1,0:T(8,128)(2,1)} %copy-done.6, bf16[2,336,256]{2,1,0:T(8,128)(2,1)} %copy-done.5, bf16[4,336,256]{2,1,0:T(8,128)(2,1)} %copy-done.2, ...), custom_call_target="tpu_custom_call" | custom-call | tf_op jit(solution)/shard_map/batch/pallas_call | solution.py:60
  111.5 17.0 %all-to-all-done.1.parts_ref.refs_1_ = bf16[8,176,256]{2,1,0:T(8,128)(2,1)S(1)} async-done(((bf16[8,176,256]{2,1,0:T(8,128)(2,1)}), bf16[8,176,256]{2,1,0:T(8,128)(2,1)S(1)}, u32[]{:S(2)}, u32[]{:S(2)}) %all-to-all-start.1) | async-done | bytes 720928 | tf_op jit(solution)/shard_map/all_to_all | solution.py:420
  128.5 0.0 copy-start
  128.5 0.9 copy-done
  129.3 1.7 %total.1 = (f32[1,128]{1,0:T(1,128)}, f32[1,128]{1,0:T(1,128)}) custom-call(bf16[8,176,256]{2,1,0:T(8,128)(2,1)} %copy-done, f32[2,128]{1,0:T(2,128)} %get-tuple-element.62.stat_ref), custom_call_target="tpu_custom_call" | custom-call | tf_op jit(solution)/shard_map/total/pallas_call | solution.py:60
  131.0 0.0 copy-start.11
  131.0 0.7 copy-done.11
  131.7 0.6 broadcast_in_dim.28
  132.3 10.2 %all-to-all-start.2 = ((f32[16,1,128]{2,1,0:T(1,128)}), f32[16,1,128]{2,1,0:T(1,128)S(1)}, u32[]{:S(2)}, u32[]{:S(2)}) async-start(f32[16,1,128]{2,1,0:T(1,128)} %broadcast_in_dim.28), calls=%async_computation.2 | async-start | bytes 16384 | tf_op jit(solution)/shard_map/all_to_all | solution.py:448
  142.5 2.5 %update.1 = bf16[1024,256]{1,0:T(8,128)(2,1)} custom-call(s32[3]{0:T(128)} %pad_add_fusion.refs_0_, bf16[8,176,256]{2,1,0:T(8,128)(2,1)} %copy-done, bf16[1024,256]{1,0:T(8,128)(2,1)} %bitcast.19), custom_call_target="tpu_custom_call" | custom-call | tf_op jit(solution)/shard_map/update/pallas_call | solution.py:60
  145.0 2.0 %queries.1 = f32[128,256]{1,0:T(8,128)} custom-call(bf16[8,176,256]{2,1,0:T(8,128)(2,1)} %copy-done, f32[1,128]{1,0:T(1,128)} %get-tuple-element.64.lt_ref, f32[128,256]{1,0:T(8,128)} %get-tuple-element.65.batch_ref, f32[2,128]{1,0:T(2,128)} %get-tuple-element.62.stat_ref, bf16[128,256]{1,0:T(8,128)(2,1)} %refs_8_.1), custom_call_target="tpu_custom_call" | custom-call | tf_op jit(solution)/shard_map/queries/pallas_call | solution.py:60
  147.0 0.9 all-to-all-done.2
  147.9 0.0 copy-start.10
  147.9 0.6 copy-done.10
  148.5 3.2 %items.1 = (f32[128,256]{1,0:T(8,128)}, f32[64,256]{1,0:T(8,128)}) custom-call(s32[3]{0:T(128)} %pad_add_fusion.refs_0_, bf16[4,336,256]{2,1,0:T(8,128)(2,1)} %copy-done.1, bf16[4,336,256]{2,1,0:T(8,128)(2,1)} %copy-done.3, bf16[2,336,256]{2,1,0:T(8,128)(2,1)} %copy-done.6, bf16[2,336,256]{2,1,0:T(8,128)(2,1)} %copy-done.5, bf16[4,336,256]{2,1,0:T(8,128)(2,1)} %copy-done.2, ...), custom_call_target="tpu_custom_call" | custom-call | tf_op jit(solution)/shard_map/items/pallas_call | solution.py:60
  (2 shorter events, 0.0 us)
Async XLA Ops:
  4.0 28.0 %collective-permute-start = (bf16[1216,256]{1,0:T(8,128)(2,1)}, bf16[1216,256]{1,0:T(8,128)(2,1)S(1)}, u32[]{:S(2)}, u32[]{:S(2)}) collective-permute-start(bf16[1216,256]{1,0:T(8,128)(2,1)} %get-tuple-element.39), channel_id=1, source_target_pairs={{0,16},{16,0},{32,48},{48,32},{64,80},{80,64},{96,112},{112,96},{1... | collective-permute-start | bytes 1867784 | tf_op jit(solution)/shard_map/ppermute | solution.py:361
  6.0 26.1 %collective-permute-start.1 = (bf16[1120,256]{1,0:T(8,128)(2,1)}, bf16[1120,256]{1,0:T(8,128)(2,1)S(1)}, u32[]{:S(2)}, u32[]{:S(2)}) collective-permute-start(bf16[1120,256]{1,0:T(8,128)(2,1)} %get-tuple-element.40), channel_id=1, source_target_pairs={{0,256},{16,272},{32,288},{48,304},{64,320},{80,336},{96,352},{112... | collective-permute-start | bytes 1720328 | tf_op jit(solution)/shard_map/ppermute | solution.py:361
  10.8 18.8 %collective-permute-start.4 = (bf16[336,256]{1,0:T(8,128)(2,1)}, bf16[336,256]{1,0:T(8,128)(2,1)S(1)}, u32[]{:S(2)}, u32[]{:S(2)}) collective-permute-start(bf16[336,256]{1,0:T(8,128)(2,1)} %get-tuple-element.41), channel_id=1, source_target_pairs={{0,3},{1,2},{2,1},{3,0},{4,7},{5,6},{6,5},{7,4},{8,11},{9,10},{10,... | collective-permute-start | bytes 516104 | tf_op jit(solution)/shard_map/ppermute | solution.py:393
  14.0 17.0 %collective-permute-start.3 = (bf16[336,256]{1,0:T(8,128)(2,1)}, bf16[336,256]{1,0:T(8,128)(2,1)S(1)}, u32[]{:S(2)}, u32[]{:S(2)}) collective-permute-start(bf16[336,256]{1,0:T(8,128)(2,1)} %get-tuple-element.41), channel_id=1, source_target_pairs={{0,2},{1,3},{2,0},{3,1},{4,6},{5,7},{6,4},{7,5},{8,10},{9,11},{10,... | collective-permute-start | bytes 516104 | tf_op jit(solution)/shard_map/ppermute | solution.py:393
  19.2 11.8 %collective-permute-start.2 = (bf16[336,256]{1,0:T(8,128)(2,1)}, bf16[336,256]{1,0:T(8,128)(2,1)S(1)}, u32[]{:S(2)}, u32[]{:S(2)}) collective-permute-start(bf16[336,256]{1,0:T(8,128)(2,1)} %get-tuple-element.41), channel_id=1, source_target_pairs={{0,1},{1,0},{2,3},{3,2},{4,5},{5,4},{6,7},{7,6},{8,9},{9,8},{10,11... | collective-permute-start | bytes 516104 | tf_op jit(solution)/shard_map/ppermute | solution.py:393
  32.0 51.9 %copy-start.1 = (bf16[4,336,256]{2,1,0:T(8,128)(2,1)}, bf16[4,336,256]{2,1,0:T(8,128)(2,1)S(1)}, u32[]{:S(2)}) copy-start(bf16[4,336,256]{2,1,0:T(8,128)(2,1)S(1)} %pad_maximum_fusion.refs_0_.refs_1_) | copy-start | bytes 2064388
  32.1 0.9 copy-start.9
  32.1 41.9 %copy-start.7 = (bf16[1216,256]{1,0:T(8,128)(2,1)}, bf16[1216,256]{1,0:T(8,128)(2,1)S(1)}, u32[]{:S(2)}) copy-start(bf16[1216,256]{1,0:T(8,128)(2,1)S(1)} %collective-permute-done.refs_3_) | copy-start | bytes 1867780
  32.9 41.0 %all-to-all-start = ((bf16[8,128,256]{2,1,0:T(8,128)(2,1)}), bf16[8,128,256]{2,1,0:T(8,128)(2,1)S(1)}, u32[]{:S(2)}, u32[]{:S(2)}) async-start(bf16[8,128,256]{2,1,0:T(8,128)(2,1)} %get-tuple-element.42), calls=%async_computation | async-start | bytes 1048576 | tf_op jit(solution)/shard_map/all_to_all | solution.py:403
  47.3 22.8 %collective-permute-start.6 = (bf16[4,336,256]{2,1,0:T(8,128)(2,1)S(1)}, bf16[4,336,256]{2,1,0:T(8,128)(2,1)S(1)}, u32[]{:S(2)}, u32[]{:S(2)}) collective-permute-start(bf16[4,336,256]{2,1,0:T(8,128)(2,1)S(1)} %pad_maximum_fusion.refs_0_.refs_1_), channel_id=1, source_target_pairs={{0,12},{1,13},{2,14},{3,15},{4,0},{5,1},{6,2},{7,3},{8,4},{9,5},{1... | collective-permute-start | bytes 2064392 | tf_op jit(solution)/shard_map/ppermute | solution.py:406
  51.7 19.2 %collective-permute-start.5 = (bf16[4,336,256]{2,1,0:T(8,128)(2,1)S(1)}, bf16[4,336,256]{2,1,0:T(8,128)(2,1)S(1)}, u32[]{:S(2)}, u32[]{:S(2)}) collective-permute-start(bf16[4,336,256]{2,1,0:T(8,128)(2,1)S(1)} %pad_maximum_fusion.refs_0_.refs_1_), channel_id=1, source_target_pairs={{0,4},{1,5},{2,6},{3,7},{4,8},{5,9},{6,10},{7,11},{8,12},{9,13},{1... | collective-permute-start | bytes 2064392 | tf_op jit(solution)/shard_map/ppermute | solution.py:406
  53.6 16.5 %collective-permute-start.7 = (bf16[1216,256]{1,0:T(8,128)(2,1)S(1)}, bf16[1216,256]{1,0:T(8,128)(2,1)S(1)}, u32[]{:S(2)}, u32[]{:S(2)}) collective-permute-start(bf16[1216,256]{1,0:T(8,128)(2,1)S(1)} %collective-permute-done.refs_3_), channel_id=1, source_target_pairs={{0,256},{16,272},{32,288},{48,304},{64,320},{80,336},{96,352},{112... | collective-permute-start | bytes 1867784 | tf_op jit(solution)/shard_map/ppermute | solution.py:361
  70.1 0.8 copy-start.8
  71.0 21.8 %copy-start.2 = (bf16[4,336,256]{2,1,0:T(8,128)(2,1)}, bf16[4,336,256]{2,1,0:T(8,128)(2,1)S(1)}, u32[]{:S(2)}) copy-start(bf16[4,336,256]{2,1,0:T(8,128)(2,1)S(1)} %collective-permute-done.6.refs_4_.refs_5_) | copy-start | bytes 2064388
  71.0 21.8 %copy-start.3 = (bf16[4,336,256]{2,1,0:T(8,128)(2,1)}, bf16[4,336,256]{2,1,0:T(8,128)(2,1)S(1)}, u32[]{:S(2)}) copy-start(bf16[4,336,256]{2,1,0:T(8,128)(2,1)S(1)} %collective-permute-done.5.refs_1_.refs_2_) | copy-start | bytes 2064388
  73.9 0.8 copy-start.4
  83.9 44.6 %all-to-all-start.1 = ((bf16[8,176,256]{2,1,0:T(8,128)(2,1)}), bf16[8,176,256]{2,1,0:T(8,128)(2,1)S(1)}, u32[]{:S(2)}, u32[]{:S(2)}) async-start(bf16[8,176,256]{2,1,0:T(8,128)(2,1)} %memory.1), calls=%async_computation.1 | async-start | bytes 1441792 | tf_op jit(solution)/shard_map/all_to_all | solution.py:420
  92.8 8.6 %collective-permute-start.9 = (bf16[2,336,256]{2,1,0:T(8,128)(2,1)S(1)}, bf16[2,336,256]{2,1,0:T(8,128)(2,1)S(1)}, u32[]{:S(2)}, u32[]{:S(2)}) collective-permute-start(bf16[2,336,256]{2,1,0:T(8,128)(2,1)S(1)} %slice.7), channel_id=1, source_target_pairs={{0,12},{1,13},{2,14},{3,15},{4,0},{5,1},{6,2},{7,3},{8,4},{9,5},{1... | collective-permute-start | bytes 1032200 | tf_op jit(solution)/shard_map/ppermute | solution.py:406
  97.2 9.3 %collective-permute-start.8 = (bf16[2,336,256]{2,1,0:T(8,128)(2,1)S(1)}, bf16[2,336,256]{2,1,0:T(8,128)(2,1)S(1)}, u32[]{:S(2)}, u32[]{:S(2)}) collective-permute-start(bf16[2,336,256]{2,1,0:T(8,128)(2,1)S(1)} %slice.6), channel_id=1, source_target_pairs={{0,4},{1,5},{2,6},{3,7},{4,8},{5,9},{6,10},{7,11},{8,12},{9,13},{1... | collective-permute-start | bytes 1032200 | tf_op jit(solution)/shard_map/ppermute | solution.py:406
  101.4 5.2 %copy-start.5 = (bf16[2,336,256]{2,1,0:T(8,128)(2,1)}, bf16[2,336,256]{2,1,0:T(8,128)(2,1)S(1)}, u32[]{:S(2)}) copy-start(bf16[2,336,256]{2,1,0:T(8,128)(2,1)S(1)} %collective-permute-done.9.refs_3_.refs_4_) | copy-start | bytes 1032196
  106.6 0.7 copy-start.6
  128.5 0.9 copy-start
  131.0 0.7 copy-start.11
  132.3 15.6 %all-to-all-start.2 = ((f32[16,1,128]{2,1,0:T(1,128)}), f32[16,1,128]{2,1,0:T(1,128)S(1)}, u32[]{:S(2)}, u32[]{:S(2)}) async-start(f32[16,1,128]{2,1,0:T(1,128)} %broadcast_in_dim.28), calls=%async_computation.2 | async-start | bytes 16384 | tf_op jit(solution)/shard_map/all_to_all | solution.py:448
  147.9 0.6 copy-start.10

commit v6 on v5

--- a/solution.py
+++ b/solution.py
@@ -60,7 +60,7 @@
     return pl.pallas_call(
         kernel,
         out_shape=out_shape,
-        in_specs=[scalars if operand.shape == (3,) else here for operand in operands],
+        in_specs=[scalars if operand.shape == (2,) else here for operand in operands],
         out_specs=(here,) * len(out_shape),
         scratch_shapes=list(scratch),
         name=name,
@@ -71,6 +71,7 @@
 def prepare_kernel(
     capacity,
     group,
+    pairs,
     place_ref,
     q_ref,
     it_ref,
@@ -82,7 +83,6 @@
     slot_ref,
     mem_ref,
     block_ref,
-    copies_ref,
     sh_ref,
     z_ref,
     y_ref,
@@ -90,20 +90,21 @@
 ):
     rows, negs = q_ref.shape[0], ng_ref.shape[0]
     keys = rows + negs
-    extra = block_ref.shape[0] - rows - keys
+    extra = block_ref.shape[1] - rows - keys
     sh_ref[:, 0:rows] = -jnp.log(rows * group * sample_chance(id_ref[...]))
     sh_ref[:, rows:] = jnp.log(ng_count_ref[...].astype(F32)) - jnp.log(
         negs * group * sample_chance(ng_id_ref[...])
     )
-    block_ref[0:rows, :] = q_ref[...]
-    block_ref[rows : 2 * rows, :] = it_ref[...]
-    block_ref[2 * rows : rows + keys, :] = ng_ref[...]
-    block_ref[rows + keys :, :] = jnp.zeros((extra, block_ref.shape[1]), BF16)
-    block_ref[rows + keys :, 0:keys] = split_rows(sh_ref[...], extra).astype(BF16)
-
-    pairs = copies_ref.shape[0]
-    for k in range(pairs):
-        copies_ref[k] = q_ref[...]
+    shifts = split_rows(sh_ref[...], extra).astype(BF16)
+    for k in range(group):
+        block_ref[k, 0:rows, :] = q_ref[...]
+        block_ref[k, rows : 2 * rows, :] = it_ref[...]
+        block_ref[k, 2 * rows : rows + keys, :] = ng_ref[...]
+        block_ref[k, rows + keys :, 0:keys] = shifts
+        block_ref[k, rows + keys :, keys:] = jnp.zeros(
+            (extra, block_ref.shape[2] - keys), BF16
+        )
+
     count = it_ref.shape[0]
     own_int = owner_ref[...]
     own_row = own_int.astype(F32)
@@ -255,25 +256,23 @@
     lax.fori_loop(0, q_ref.shape[0] * block // tile, one_tile, 0)
 
 
-def batch_kernel(*refs):
-    *g_refs, q_ref, it_ref, sh_ref, out_ref, stat_ref, s_ref = refs
+def batch_kernel(g_ref, q_ref, it_ref, sh_ref, out_ref, stat_ref, s_ref):
     rows = q_ref.shape[0]
     keys = sh_ref.shape[1]
-    blocks = [(ref, k) for ref in g_refs for k in range(ref.shape[0])]
     q = q_ref[...]
     highest = None
-    for n, (ref, k) in enumerate(blocks):
-        shift = joined(ref[k, rows + keys :, 0:keys])
-        s = dot_rows(q, ref[k, rows : rows + keys, :]) + shift
-        s_ref[n] = s
+    for k in range(g_ref.shape[0]):
+        shift = joined(g_ref[k, rows + keys :, 0:keys])
+        s = dot_rows(q, g_ref[k, rows : rows + keys, :]) + shift
+        s_ref[k] = s
         highest = s if highest is None else jnp.maximum(highest, s)
     top = jnp.max(highest, axis=1, keepdims=True)
     total = jnp.zeros((rows, keys), F32)
     acc = jnp.zeros(q.shape, F32)
-    for n, (ref, k) in enumerate(blocks):
-        p = jnp.exp(s_ref[n] - top)
+    for k in range(g_ref.shape[0]):
+        p = jnp.exp(s_ref[k] - top)
         total = total + p
-        acc = acc + dot_plain(p.astype(BF16), ref[k, rows : rows + keys, :])
+        acc = acc + dot_plain(p.astype(BF16), g_ref[k, rows : rows + keys, :])
     total = jnp.sum(total, axis=1, keepdims=True)
     out_ref[...] = acc / total
     stat_ref[0:1, :] = to_row(top + jnp.log(total))
@@ -297,24 +296,14 @@
     loss_ref[...] = log_total - stat_ref[1:2, :]
 
 
-def item_kernel(*refs):
-    place_ref, *g_refs, lt_ref, q_ref, it_ref, ng_ref, sh_ref, item_ref, neg_ref = refs
+def item_kernel(g_ref, lt_ref, q_ref, it_ref, ng_ref, sh_ref, item_ref, neg_ref):
     rows = q_ref.shape[0]
-    here = place_ref[2]
-    near = g_refs[0].shape[0]
-    peers = sum(ref.shape[0] for ref in g_refs)
     keys = jnp.concatenate([it_ref[...], ng_ref[...]], axis=0)
     shift = to_column(sh_ref[...])
     acc = jnp.zeros(keys.shape, F32)
-    low = lax.rem(here, near)
-    blocks = [(ref, k) for ref in g_refs for k in range(ref.shape[0])]
-    for at in range(0, peers, 2):
-        base = lax.rem(here - low - (at // near) * near + peers, peers)
-        pair = blocks[at : at + 2]
-        queries = jnp.concatenate([ref[k, 0:rows, :] for ref, k in pair], axis=0)
-        log_total = jnp.concatenate(
-            [lt_ref[pl.ds(base + (low ^ ((at + n) % near)), 1), :] for n in range(2)], axis=1
-        )
+    for k in range(0, g_ref.shape[0], 2):
+        queries = jnp.concatenate([g_ref[k + n, 0:rows, :] for n in range(2)], axis=0)
+        log_total = jnp.concatenate([lt_ref[k + n : k + n + 1, :] for n in range(2)], axis=1)
         w = jnp.exp(dot_rows(keys, queries) + shift - log_total).astype(BF16)
         acc = acc + dot_plain(w, queries)
     item_ref[...] = acc[0:rows, :] - q_ref[...].astype(F32)
@@ -360,12 +349,12 @@
         ]
         return lax.ppermute(block, column, route)
 
-    place = jnp.stack([lax.axis_index("yh"), lax.axis_index("zl"), lax.axis_index("dp")])
+    place = jnp.stack([lax.axis_index("yh"), lax.axis_index("zl")])
     capacity = max(2, 2 * rows // cycle)
     held = mem.shape[0]
     span = shards * capacity * 3 // 2
-    block, copies, shift, z_sent, y_sent, own_items = call(
-        lambda *refs: prepare_kernel(capacity, group, *refs),
+    block, shift, z_sent, y_sent, own_items = call(
+        lambda *refs: prepare_kernel(capacity, group, shards, *refs),
         (
             place,
             query_vectors,
@@ -379,8 +368,7 @@
             mem,
         ),
         (
-            jax.ShapeDtypeStruct((rows + keys + 16, width), BF16),
-            jax.ShapeDtypeStruct((shards, rows, width), BF16),
+            jax.ShapeDtypeStruct((group, rows + keys + 16, width), BF16),
             jax.ShapeDtypeStruct((1, keys), F32),
             jax.ShapeDtypeStruct((held + 2 * span, width), BF16),
             jax.ShapeDtypeStruct((held + span, width), BF16),
@@ -388,27 +376,13 @@
         ),
         "prepare",
     )
-    near = 4
-    near_blocks = [block] + [
-        lax.ppermute(block, "dp", [(i, i ^ k) for i in range(group)]) for k in range(1, near)
-    ]
-    pair_blocks = jnp.stack(near_blocks)
+    gathered = lax.all_to_all(block, "dp", 0, 0, tiled=True)
     z_rows = beside(z_sent, 0, 1)
     y_rows = beside(y_sent, 1, 0)
-    copies, z_rows, y_rows, pair_blocks = lax.optimization_barrier(
-        (copies, z_rows, y_rows, pair_blocks)
-    )
+    z_rows, queries = lax.optimization_barrier((z_rows, query_vectors))
     zy_rows = beside(z_rows, 1, 0)
     memory_blocks = [own_items, mem, z_rows, y_rows, zy_rows]
-    arrived = lax.all_to_all(copies, "zh", 0, 0, tiled=True)
-
-    def along(blocks, by):
-        return lax.ppermute(blocks, "dp", [(i, (i + near * by) % group) for i in range(group)])
-
-    before, after = along(pair_blocks, 1), along(pair_blocks, -1)
-    arrived, before, after, memory_blocks = lax.optimization_barrier(
-        (arrived, before, after, memory_blocks)
-    )
+    arrived = lax.all_gather(queries, "zh", axis=0, tiled=False)
 
     (parts,) = call(
         lambda *refs: memory_kernel(512, *refs),
@@ -416,19 +390,12 @@
         (jax.ShapeDtypeStruct((shards, rows + 6 * capacity, width), BF16),),
         "memory",
     )
-    parts, before, after = lax.optimization_barrier((parts, before, after))
+    parts, gathered = lax.optimization_barrier((parts, gathered))
     parts_back = lax.all_to_all(parts, "zh", 0, 0, tiled=True)
 
-    group_blocks = [
-        pair_blocks,
-        before,
-        along(before[: near // 2], 1),
-        along(after[near // 2 :], -1),
-        after,
-    ]
     batch_part, batch_stat = call(
         batch_kernel,
-        (*group_blocks, query_vectors, item_vectors, shift),
+        (gathered, query_vectors, item_vectors, shift),
         (
             jax.ShapeDtypeStruct((rows, width), F32),
             jax.ShapeDtypeStruct((2, rows), F32),
@@ -466,8 +433,7 @@
     item_grad, negative_grad = call(
         item_kernel,
         (
-            place,
-            *group_blocks,
+            gathered,
             group_totals,
             query_vectors,
             item_vectors,

time: 153 us -> 155 us (1.013)
  the two profiles are of different devices: /device:TPU:33 before, /device:TPU:65 now
where the time goes in v6:
time: 155 us; the launch traced here: 154 us
  waiting for transfers between devices  53.3 us (34%)
  starting transfers between devices  36 us (23%)
  blocking collectives  33 us (21%)
  Pallas kernels  26.7 us (17%)
  local copies, waits for them, and re-layouts  3.77 us (2%)
    all_to_all x1, waiting for transfers between devices, local(): parts_back = lax.all_to_all(parts, 'zh', 0, 0, tiled=True)  35.5 us
    all_gather x1, blocking collectives, local(): arrived = lax.all_gather(queries, 'zh', axis=0, tiled=False)  33 us
    pallas_call x7, Pallas kernels, call(): pl.pallas_call(kernel, out_shape=out_shape, in_specs=[scalars if operand....  26.7 us
    ppermute x3, waiting for transfers between devices, beside(): return lax.ppermute(block, column, route)  16.8 us
    all_to_all x1, starting transfers between devices, local(): parts_back = lax.all_to_all(parts, 'zh', 0, 0, tiled=True)  13.9 us
    ppermute x3, starting transfers between devices, beside(): return lax.ppermute(block, column, route)  10.3 us
    all_to_all x1, starting transfers between devices, local(): gathered = lax.all_to_all(block, 'dp', 0, 0, tiled=True)  6.14 us
    all_to_all x1, starting transfers between devices, local(): lax.all_to_all(jnp.broadcast_to(log_total[None], (group, 1, rows)), 'dp',...  5.6 us
  transfers between devices with their start and end apart: 6, of which 4 were waited for; matrix products, arithmetic and copies ran while one was open for 0% of the time, Pallas kernels for 12%

profile of v6, /device:TPU:65, one launch (start us, length us, event | category | flops | bytes accessed | tf_op | source)
XLA Modules:
  0.0 154.0 jit_solution(9198039735819917971)
XLA Ops:
  0.6 0.6 pad_add_fusion.refs_0_
  1.2 3.6 %prepare.1 = (bf16[16,336,256]{2,1,0:T(8,128)(2,1)}, f32[1,192]{1,0:T(1,128)}, bf16[1216,256]{1,0:T(8,128)(2,1)}, bf16[1120,256]{1,0:T(8,128)(2,1)}, bf16[96,256]{1,0:T(8,128)(2,1)}) custom-call(s32[2]{0:T(128)} %pad_add_fusion.refs_0_, bf16[128,256]{1,0:T(8,128)(2,1)} %q_ref.3, bf16[128,256]{1,0:T(8,128)(2,1)} %it_ref.5, bf16[64,256]{1,0:T(8,128)(2,1)} %ng_ref.1, ...), custom_call_target="tpu_custom_call" | custom-call | tf_op jit(solution)/shard_map/prepare/pallas_call | solution.py:60
  4.9 0.0 copy-start.7
  4.9 0.0 copy-start.2
  4.9 6.1 %all-to-all-start = ((bf16[16,336,256]{2,1,0:T(8,128)(2,1)}), bf16[16,336,256]{2,1,0:T(8,128)(2,1)S(1)}, u32[]{:S(2)}, u32[]{:S(2)}) async-start(bf16[16,336,256]{2,1,0:T(8,128)(2,1)} %get-tuple-element.31), calls=%async_computation | async-start | bytes 5505024 | tf_op jit(solution)/shard_map/all_to_all | solution.py:379
  11.0 0.0 copy-done.7
  11.0 3.6 %collective-permute-start = (bf16[1216,256]{1,0:T(8,128)(2,1)S(1)}, bf16[1216,256]{1,0:T(8,128)(2,1)S(1)}, u32[]{:S(2)}, u32[]{:S(2)}) collective-permute-start(bf16[1216,256]{1,0:T(8,128)(2,1)S(1)} %copy-done.7), channel_id=1, source_target_pairs={{0,16},{16,0},{32,48},{48,32},{64,80},{80,64},{96,112},{112,96},{1... | collective-permute-start | bytes 1867784 | tf_op jit(solution)/shard_map/ppermute | solution.py:350
  14.6 14.3 %collective-permute-done.refs_3_ = bf16[1216,256]{1,0:T(8,128)(2,1)S(1)} collective-permute-done((bf16[1216,256]{1,0:T(8,128)(2,1)S(1)}, bf16[1216,256]{1,0:T(8,128)(2,1)S(1)}, u32[]{:S(2)}, u32[]{:S(2)}) %collective-permute-start) | collective-permute-done | bytes 622624 | tf_op jit(solution)/shard_map/ppermute | solution.py:350
  28.8 0.0 copy-start.3
  28.8 4.5 %collective-permute-start.2 = (bf16[1216,256]{1,0:T(8,128)(2,1)S(1)}, bf16[1216,256]{1,0:T(8,128)(2,1)S(1)}, u32[]{:S(2)}, u32[]{:S(2)}) collective-permute-start(bf16[1216,256]{1,0:T(8,128)(2,1)S(1)} %collective-permute-done.refs_3_), channel_id=1, source_target_pairs={{0,256},{16,272},{32,288},{48,304},{64,320},{80,336},{96,352},{112... | collective-permute-start | bytes 1867784 | tf_op jit(solution)/shard_map/ppermute | solution.py:350
  33.4 2.3 %collective-permute-start.1 = (bf16[1120,256]{1,0:T(8,128)(2,1)}, bf16[1120,256]{1,0:T(8,128)(2,1)S(1)}, u32[]{:S(2)}, u32[]{:S(2)}) collective-permute-start(bf16[1120,256]{1,0:T(8,128)(2,1)} %get-tuple-element.30), channel_id=1, source_target_pairs={{0,256},{16,272},{32,288},{48,304},{64,320},{80,336},{96,352},{112... | collective-permute-start | bytes 1720328 | tf_op jit(solution)/shard_map/ppermute | solution.py:350
  35.6 0.0 copy-done.2
  35.6 33.0 %all-gather = bf16[1024,256]{1,0:T(8,128)(2,1)} all-gather(bf16[128,256]{1,0:T(8,128)(2,1)S(1)} %copy-done.2), channel_id=2, replica_groups=mesh['yh'=2,'zh'=8,'zl'=2,'dp'=16] {'zh'}, dimensions={0}, use_global_device_ids=true | all-gather | bytes 589824 | tf_op jit(solution)/shard_map/all_gather | solution.py:385
  68.7 2.6 %collective-permute-done.1.refs_4_ = bf16[1120,256]{1,0:T(8,128)(2,1)S(1)} collective-permute-done((bf16[1120,256]{1,0:T(8,128)(2,1)}, bf16[1120,256]{1,0:T(8,128)(2,1)S(1)}, u32[]{:S(2)}, u32[]{:S(2)}) %collective-permute-start.1) | collective-permute-done | bytes 573472 | tf_op jit(solution)/shard_map/ppermute | solution.py:350
  71.3 0.0 copy-start.5
  71.3 0.0 collective-permute-done.2.refs_5_
  71.3 0.0 copy-start.4
  71.3 0.0 copy-done.3
  71.3 0.8 copy-done.5
  72.1 0.2 copy-done.4
  72.3 9.2 %memory.1 = bf16[8,176,256]{2,1,0:T(8,128)(2,1)} custom-call(bf16[8,128,256]{2,1,0:T(8,128)(2,1)} %bitcast.16, bf16[96,256]{1,0:T(8,128)(2,1)} %get-tuple-element.28.refs_1_, bf16[1024,256]{1,0:T(8,128)(2,1)} %bitcast.14, bf16[1216,256]{1,0:T(8,128)(2,1)} %copy-done.3, bf16[1120,256]{1,0:T(8,128)(2,1)} %copy-done.5, bf16[1216,256]{1,0:T(8,128)(2,1)} %copy-done.4), custom_call_target="tpu_custom_call" | custom-call | tf_op jit(solution)/shard_map/memory/pallas_call | solution.py:60
  81.5 0.0 all-to-all-done.g_ref
  81.5 0.0 copy-start
  81.5 13.9 %all-to-all-start.1 = ((bf16[8,176,256]{2,1,0:T(8,128)(2,1)}), bf16[8,176,256]{2,1,0:T(8,128)(2,1)S(1)}, u32[]{:S(2)}, u32[]{:S(2)}) async-start(bf16[8,176,256]{2,1,0:T(8,128)(2,1)} %memory.1), calls=%async_computation.1 | async-start | bytes 1441792 | tf_op jit(solution)/shard_map/all_to_all | solution.py:394
  95.4 0.0 copy-done
  95.4 4.3 %batch.1 = (f32[128,256]{1,0:T(8,128)}, f32[2,128]{1,0:T(2,128)}) custom-call(bf16[16,336,256]{2,1,0:T(8,128)(2,1)} %copy-done, bf16[128,256]{1,0:T(8,128)(2,1)} %q_ref.3, bf16[128,256]{1,0:T(8,128)(2,1)} %it_ref.5, f32[1,192]{1,0:T(1,128)} %get-tuple-element.34.sh_ref), custom_call_target="tpu_custom_call" | custom-call | tf_op jit(solution)/shard_map/batch/pallas_call | solution.py:60
  99.6 35.5 %all-to-all-done.1.parts_ref.refs_1_ = bf16[8,176,256]{2,1,0:T(8,128)(2,1)S(1)} async-done(((bf16[8,176,256]{2,1,0:T(8,128)(2,1)}), bf16[8,176,256]{2,1,0:T(8,128)(2,1)S(1)}, u32[]{:S(2)}, u32[]{:S(2)}) %all-to-all-start.1) | async-done | bytes 720928 | tf_op jit(solution)/shard_map/all_to_all | solution.py:394
  135.2 0.0 copy-start.1
  135.2 0.9 copy-done.1
  136.1 1.7 %total.1 = (f32[1,128]{1,0:T(1,128)}, f32[1,128]{1,0:T(1,128)}) custom-call(bf16[8,176,256]{2,1,0:T(8,128)(2,1)} %copy-done.1, f32[2,128]{1,0:T(2,128)} %get-tuple-element.38.stat_ref), custom_call_target="tpu_custom_call" | custom-call | tf_op jit(solution)/shard_map/total/pallas_call | solution.py:60
  137.8 1.3 broadcast_in_dim.28
  139.1 5.6 %all-to-all-start.2 = ((f32[16,1,128]{2,1,0:T(1,128)}), f32[16,1,128]{2,1,0:T(1,128)S(1)}, u32[]{:S(2)}, u32[]{:S(2)}) async-start(f32[16,1,128]{2,1,0:T(1,128)} %broadcast_in_dim.28), calls=%async_computation.2 | async-start | bytes 16384 | tf_op jit(solution)/shard_map/all_to_all | solution.py:415
  144.7 2.5 %update.1 = bf16[1024,256]{1,0:T(8,128)(2,1)} custom-call(s32[2]{0:T(128)} %pad_add_fusion.refs_0_, bf16[8,176,256]{2,1,0:T(8,128)(2,1)} %copy-done.1, bf16[1024,256]{1,0:T(8,128)(2,1)} %bitcast.15), custom_call_target="tpu_custom_call" | custom-call | tf_op jit(solution)/shard_map/update/pallas_call | solution.py:60
  147.2 2.0 %queries.1 = f32[128,256]{1,0:T(8,128)} custom-call(bf16[8,176,256]{2,1,0:T(8,128)(2,1)} %copy-done.1, f32[1,128]{1,0:T(1,128)} %get-tuple-element.40.lt_ref, f32[128,256]{1,0:T(8,128)} %get-tuple-element.41.batch_ref, f32[2,128]{1,0:T(2,128)} %get-tuple-element.38.stat_ref, bf16[128,256]{1,0:T(8,128)(2,1)} %it_ref.5), custom_call_target="tpu_custom_call" | custom-call | tf_op jit(solution)/shard_map/queries/pallas_call | solution.py:60
  149.2 0.9 all-to-all-done.2
  150.1 0.0 copy-start.6
  150.1 0.6 copy-done.6
  150.7 3.3 %items.1 = (f32[128,256]{1,0:T(8,128)}, f32[64,256]{1,0:T(8,128)}) custom-call(bf16[16,336,256]{2,1,0:T(8,128)(2,1)} %copy-done, f32[16,128]{1,0:T(8,128)} %bitcast.18, bf16[128,256]{1,0:T(8,128)(2,1)} %q_ref.3, bf16[128,256]{1,0:T(8,128)(2,1)} %it_ref.5, bf16[64,256]{1,0:T(8,128)(2,1)} %ng_ref.1, f32[1,192]{1,0:T(1,128)} %get-tuple-element.34.sh_ref), custom_call_target="tpu_custom_call" | custom-call | tf_op jit(solution)/shard_map/items/pallas_call | solution.py:60
Async XLA Ops:
  4.9 6.2 %copy-start.7 = (bf16[1216,256]{1,0:T(8,128)(2,1)S(1)}, bf16[1216,256]{1,0:T(8,128)(2,1)}, u32[]{:S(2)}) copy-start(bf16[1216,256]{1,0:T(8,128)(2,1)} %get-tuple-element.26) | copy-start | bytes 1867780
  4.9 30.8 %copy-start.2 = (bf16[128,256]{1,0:T(8,128)(2,1)S(1)}, bf16[128,256]{1,0:T(8,128)(2,1)}, u32[]{:S(2)}) copy-start(bf16[128,256]{1,0:T(8,128)(2,1)} %q_ref.3) | copy-start | bytes 196612
  4.9 76.6 %all-to-all-start = ((bf16[16,336,256]{2,1,0:T(8,128)(2,1)}), bf16[16,336,256]{2,1,0:T(8,128)(2,1)S(1)}, u32[]{:S(2)}, u32[]{:S(2)}) async-start(bf16[16,336,256]{2,1,0:T(8,128)(2,1)} %get-tuple-element.31), calls=%async_computation | async-start | bytes 5505024 | tf_op jit(solution)/shard_map/all_to_all | solution.py:379
  11.0 17.8 %collective-permute-start = (bf16[1216,256]{1,0:T(8,128)(2,1)S(1)}, bf16[1216,256]{1,0:T(8,128)(2,1)S(1)}, u32[]{:S(2)}, u32[]{:S(2)}) collective-permute-start(bf16[1216,256]{1,0:T(8,128)(2,1)S(1)} %copy-done.7), channel_id=1, source_target_pairs={{0,16},{16,0},{32,48},{48,32},{64,80},{80,64},{96,112},{112,96},{1... | collective-permute-start | bytes 1867784 | tf_op jit(solution)/shard_map/ppermute | solution.py:350
  28.8 42.4 %copy-start.3 = (bf16[1216,256]{1,0:T(8,128)(2,1)}, bf16[1216,256]{1,0:T(8,128)(2,1)S(1)}, u32[]{:S(2)}) copy-start(bf16[1216,256]{1,0:T(8,128)(2,1)S(1)} %collective-permute-done.refs_3_) | copy-start | bytes 1867780
  28.8 42.4 %collective-permute-start.2 = (bf16[1216,256]{1,0:T(8,128)(2,1)S(1)}, bf16[1216,256]{1,0:T(8,128)(2,1)S(1)}, u32[]{:S(2)}, u32[]{:S(2)}) collective-permute-start(bf16[1216,256]{1,0:T(8,128)(2,1)S(1)} %collective-permute-done.refs_3_), channel_id=1, source_target_pairs={{0,256},{16,272},{32,288},{48,304},{64,320},{80,336},{96,352},{112... | collective-permute-start | bytes 1867784 | tf_op jit(solution)/shard_map/ppermute | solution.py:350
  33.4 37.9 %collective-permute-start.1 = (bf16[1120,256]{1,0:T(8,128)(2,1)}, bf16[1120,256]{1,0:T(8,128)(2,1)S(1)}, u32[]{:S(2)}, u32[]{:S(2)}) collective-permute-start(bf16[1120,256]{1,0:T(8,128)(2,1)} %get-tuple-element.30), channel_id=1, source_target_pairs={{0,256},{16,272},{32,288},{48,304},{64,320},{80,336},{96,352},{112... | collective-permute-start | bytes 1720328 | tf_op jit(solution)/shard_map/ppermute | solution.py:350
  71.3 0.8 copy-start.5
  71.3 1.0 copy-start.4
  81.5 13.9 %copy-start = (bf16[16,336,256]{2,1,0:T(8,128)(2,1)}, bf16[16,336,256]{2,1,0:T(8,128)(2,1)S(1)}, u32[]{:S(2)}) copy-start(bf16[16,336,256]{2,1,0:T(8,128)(2,1)S(1)} %all-to-all-done.g_ref) | copy-start | bytes 8257540
  81.5 53.7 %all-to-all-start.1 = ((bf16[8,176,256]{2,1,0:T(8,128)(2,1)}), bf16[8,176,256]{2,1,0:T(8,128)(2,1)S(1)}, u32[]{:S(2)}, u32[]{:S(2)}) async-start(bf16[8,176,256]{2,1,0:T(8,128)(2,1)} %memory.1), calls=%async_computation.1 | async-start | bytes 1441792 | tf_op jit(solution)/shard_map/all_to_all | solution.py:394
  135.2 0.9 copy-start.1
  139.1 11.0 %all-to-all-start.2 = ((f32[16,1,128]{2,1,0:T(1,128)}), f32[16,1,128]{2,1,0:T(1,128)S(1)}, u32[]{:S(2)}, u32[]{:S(2)}) async-start(f32[16,1,128]{2,1,0:T(1,128)} %broadcast_in_dim.28), calls=%async_computation.2 | async-start | bytes 16384 | tf_op jit(solution)/shard_map/all_to_all | solution.py:415
  150.1 0.6 copy-start.6

commit v7 on v6

--- a/solution.py
+++ b/solution.py
@@ -86,6 +86,7 @@
     sh_ref,
     z_ref,
     y_ref,
+    zy_ref,
     own_ref,
 ):
     rows, negs = q_ref.shape[0], ng_ref.shape[0]
@@ -135,11 +136,9 @@
     )
     each = places // 4
     held = mem_ref.shape[0]
-    z_ref[0:held, :] = mem_ref[...]
-    y_ref[0:held, :] = mem_ref[...]
-    for c, (ref, at) in enumerate(
-        ((own_ref, 0), (z_ref, held), (y_ref, held), (z_ref, held + each + each // 2))
-    ):
+    for ref in (z_ref, y_ref, zy_ref):
+        ref[0:held, :] = mem_ref[...]
+    for c, (ref, at) in enumerate(((own_ref, 0), (z_ref, held), (y_ref, held), (zy_ref, held))):
         some = chosen[c * each : (c + 1) * each, :]
         ref[at : at + each, :] = dot_plain(some, it_ref[...]).astype(BF16)
         slots = dot_plain(some, details.astype(BF16)).astype(BF16)
@@ -199,7 +198,7 @@
     total = span * 2 // 3
     each = total // pairs
     extra = 2 * each
-    sources = ((own_ref, 0), (z_ref, held), (y_ref, held), (zy_ref, held + span))
+    sources = ((own_ref, 0), (z_ref, held), (y_ref, held), (zy_ref, held))
     for k in range(0, pairs, 2):
         items, slots = [], []
         for ref, at in sources:
@@ -280,7 +279,7 @@
     stat_ref[1:2, :] = jnp.sum(jnp.where(eye(rows), own, 0.0), axis=0, keepdims=True)
 
 
-def total_kernel(parts_ref, stat_ref, total_ref, loss_ref):
+def total_kernel(parts_ref, stat_ref, total_ref, copies_ref, loss_ref):
     rows = total_ref.shape[1]
     shards = parts_ref.shape[0]
     batch = stat_ref[0:1, :]
@@ -293,6 +292,8 @@
         summed = summed + jnp.exp(row - top)
     log_total = top + jnp.log(summed)
     total_ref[...] = log_total
+    for k in range(copies_ref.shape[0]):
+        copies_ref[k] = log_total
     loss_ref[...] = log_total - stat_ref[1:2, :]
 
 
@@ -353,7 +354,7 @@
     capacity = max(2, 2 * rows // cycle)
     held = mem.shape[0]
     span = shards * capacity * 3 // 2
-    block, shift, z_sent, y_sent, own_items = call(
+    block, shift, z_sent, y_sent, zy_sent, own_items = call(
         lambda *refs: prepare_kernel(capacity, group, shards, *refs),
         (
             place,
@@ -370,19 +371,20 @@
         (
             jax.ShapeDtypeStruct((group, rows + keys + 16, width), BF16),
             jax.ShapeDtypeStruct((1, keys), F32),
-            jax.ShapeDtypeStruct((held + 2 * span, width), BF16),
-            jax.ShapeDtypeStruct((held + span, width), BF16),
-            jax.ShapeDtypeStruct((span, width), BF16),
-        ),
+        )
+        + (jax.ShapeDtypeStruct((held + span, width), BF16),) * 3
+        + (jax.ShapeDtypeStruct((span, width), BF16),),
         "prepare",
     )
     gathered = lax.all_to_all(block, "dp", 0, 0, tiled=True)
-    z_rows = beside(z_sent, 0, 1)
-    y_rows = beside(y_sent, 1, 0)
-    z_rows, queries = lax.optimization_barrier((z_rows, query_vectors))
-    zy_rows = beside(z_rows, 1, 0)
-    memory_blocks = [own_items, mem, z_rows, y_rows, zy_rows]
-    arrived = lax.all_gather(queries, "zh", axis=0, tiled=False)
+    memory_blocks = [
+        own_items,
+        mem,
+        beside(z_sent, 0, 1),
+        beside(y_sent, 1, 0),
+        beside(zy_sent, 1, 1),
+    ]
+    arrived = lax.all_gather(query_vectors, "zh", axis=0, tiled=False)
 
     (parts,) = call(
         lambda *refs: memory_kernel(512, *refs),
@@ -406,15 +408,17 @@
     parts_back, batch_part, batch_stat = lax.optimization_barrier(
         (parts_back, batch_part, batch_stat)
     )
-    log_total, loss = call(
+    log_total, total_copies, loss = call(
         total_kernel,
         (parts_back, batch_stat),
-        (jax.ShapeDtypeStruct((1, rows), F32), jax.ShapeDtypeStruct((1, rows), F32)),
+        (
+            jax.ShapeDtypeStruct((1, rows), F32),
+            jax.ShapeDtypeStruct((group, 1, rows), F32),
+            jax.ShapeDtypeStruct((1, rows), F32),
+        ),
         "total",
     )
-    group_totals = lax.all_to_all(
-        jnp.broadcast_to(log_total[None], (group, 1, rows)), "dp", 0, 0, tiled=True
-    ).reshape(group, rows)
+    group_totals = lax.all_to_all(total_copies, "dp", 0, 0, tiled=True).reshape(group, rows)
     (query_grad,) = call(
         query_kernel,
         (parts_back, log_total, batch_part, batch_stat, item_vectors),

time: 155 us -> 158 us (1.019)
  the two profiles are of different devices: /device:TPU:65 before, /device:TPU:1 now
where the time goes in v7:
time: 158 us; the launch traced here: 157 us
  blocking collectives  57.6 us (36%)
  starting transfers between devices  43.7 us (28%)
  Pallas kernels  26.8 us (17%)
  waiting for transfers between devices  25.1 us (16%)
  local copies, waits for them, and re-layouts  2.64 us (2%)
    all_gather x1, blocking collectives, local(): arrived = lax.all_gather(query_vectors, 'zh', axis=0, tiled=False)  57.6 us
    pallas_call x7, Pallas kernels, call(): pl.pallas_call(kernel, out_shape=out_shape, in_specs=[scalars if operand....  26.8 us
    all_to_all x1, waiting for transfers between devices, local(): parts_back = lax.all_to_all(parts, 'zh', 0, 0, tiled=True)  24.2 us
    all_to_all x1, starting transfers between devices, local(): lax.all_to_all(total_copies, 'dp', 0, 0, tiled=True).reshape(group, rows)  16.8 us
    all_to_all x1, starting transfers between devices, local(): gathered = lax.all_to_all(block, 'dp', 0, 0, tiled=True)  10.5 us
    ppermute x3, starting transfers between devices, beside(): return lax.ppermute(block, column, route)  9.86 us
    all_to_all x1, starting transfers between devices, local(): parts_back = lax.all_to_all(parts, 'zh', 0, 0, tiled=True)  6.5 us
  transfers between devices with their start and end apart: 6, of which 2 were waited for; matrix products, arithmetic and copies ran while one was open for 0% of the time, Pallas kernels for 11%

profile of v7, /device:TPU:1, one launch (start us, length us, event | category | flops | bytes accessed | tf_op | source)
XLA Modules:
  0.0 157.2 jit_solution(6963472561021444427)
XLA Ops:
  0.6 0.6 pad_add_fusion.refs_0_
  1.2 3.8 %prepare.1 = (bf16[16,336,256]{2,1,0:T(8,128)(2,1)}, f32[1,192]{1,0:T(1,128)}, bf16[1120,256]{1,0:T(8,128)(2,1)}, bf16[1120,256]{1,0:T(8,128)(2,1)}, bf16[1120,256]{1,0:T(8,128)(2,1)}, /*index=5*/bf16[96,256]{1,0:T(8,128)(2,1)}) custom-call(s32[2]{0:T(128)} %pad_add_fusion.refs_0_, bf16[128,256]{1,0:T(8,128)(2,1)} %q_ref.3, bf16[128,256]{1,0:T(8,128)(2,1)} %it_ref.5, ...), custom_call_target="tpu_custom_call" | custom-call | tf_op jit(solution)/shard_map/prepare/pallas_call | solution.py:60
  5.0 0.0 copy-start.7
  5.0 0.0 copy-start.2
  5.0 10.5 %all-to-all-start = ((bf16[16,336,256]{2,1,0:T(8,128)(2,1)}), bf16[16,336,256]{2,1,0:T(8,128)(2,1)S(1)}, u32[]{:S(2)}, u32[]{:S(2)}) async-start(bf16[16,336,256]{2,1,0:T(8,128)(2,1)} %get-tuple-element.30), calls=%async_computation | async-start | bytes 5505024 | tf_op jit(solution)/shard_map/all_to_all | solution.py:379
  15.6 1.9 %collective-permute-start = (bf16[1120,256]{1,0:T(8,128)(2,1)}, bf16[1120,256]{1,0:T(8,128)(2,1)S(1)}, u32[]{:S(2)}, u32[]{:S(2)}) collective-permute-start(bf16[1120,256]{1,0:T(8,128)(2,1)} %get-tuple-element.27), channel_id=1, source_target_pairs={{0,16},{16,0},{32,48},{48,32},{64,80},{80,64},{96,112},{112,96},{1... | collective-permute-start | bytes 1720328 | tf_op jit(solution)/shard_map/ppermute | solution.py:351
  17.5 2.6 %collective-permute-start.1 = (bf16[1120,256]{1,0:T(8,128)(2,1)}, bf16[1120,256]{1,0:T(8,128)(2,1)S(1)}, u32[]{:S(2)}, u32[]{:S(2)}) collective-permute-start(bf16[1120,256]{1,0:T(8,128)(2,1)} %get-tuple-element.28), channel_id=1, source_target_pairs={{0,256},{16,272},{32,288},{48,304},{64,320},{80,336},{96,352},{112... | collective-permute-start | bytes 1720328 | tf_op jit(solution)/shard_map/ppermute | solution.py:351
  20.1 0.0 copy-done.7
  20.1 5.3 %collective-permute-start.2 = (bf16[1120,256]{1,0:T(8,128)(2,1)S(1)}, bf16[1120,256]{1,0:T(8,128)(2,1)S(1)}, u32[]{:S(2)}, u32[]{:S(2)}) collective-permute-start(bf16[1120,256]{1,0:T(8,128)(2,1)S(1)} %copy-done.7), channel_id=1, source_target_pairs={{0,272},{16,256},{32,304},{48,288},{64,336},{80,320},{96,368},{112... | collective-permute-start | bytes 1720328 | tf_op jit(solution)/shard_map/ppermute | solution.py:351
  25.5 0.0 copy-done.2
  25.5 57.6 %all-gather = bf16[1024,256]{1,0:T(8,128)(2,1)} all-gather(bf16[128,256]{1,0:T(8,128)(2,1)S(1)} %copy-done.2), channel_id=2, replica_groups=mesh['yh'=2,'zh'=8,'zl'=2,'dp'=16] {'zh'}, dimensions={0}, use_global_device_ids=true | all-gather | bytes 589824 | tf_op jit(solution)/shard_map/all_gather | solution.py:387
  83.1 0.0 collective-permute-done.refs_3_
  83.1 0.0 copy-start.3
  83.1 0.0 collective-permute-done.1.refs_4_
  83.1 0.0 copy-start.4
  83.1 0.0 collective-permute-done.2.refs_5_
  83.1 0.0 copy-start.5
  83.1 0.8 copy-done.3
  83.9 0.2 copy-done.4
  84.1 0.2 copy-done.5
  84.3 9.2 %memory.1 = bf16[8,176,256]{2,1,0:T(8,128)(2,1)} custom-call(bf16[8,128,256]{2,1,0:T(8,128)(2,1)} %bitcast.15, bf16[96,256]{1,0:T(8,128)(2,1)} %get-tuple-element.26.refs_1_, bf16[1024,256]{1,0:T(8,128)(2,1)} %bitcast.13, bf16[1120,256]{1,0:T(8,128)(2,1)} %copy-done.3, bf16[1120,256]{1,0:T(8,128)(2,1)} %copy-done.4, bf16[1120,256]{1,0:T(8,128)(2,1)} %copy-done.5), custom_call_target="tpu_custom_call" | custom-call | tf_op jit(solution)/shard_map/memory/pallas_call | solution.py:60
  93.5 0.0 all-to-all-done.g_ref
  93.5 0.0 copy-start
  93.5 6.5 %all-to-all-start.1 = ((bf16[8,176,256]{2,1,0:T(8,128)(2,1)}), bf16[8,176,256]{2,1,0:T(8,128)(2,1)S(1)}, u32[]{:S(2)}, u32[]{:S(2)}) async-start(bf16[8,176,256]{2,1,0:T(8,128)(2,1)} %memory.1), calls=%async_computation.1 | async-start | bytes 1441792 | tf_op jit(solution)/shard_map/all_to_all | solution.py:396
  100.0 0.0 copy-done
  100.0 4.3 %batch.1 = (f32[128,256]{1,0:T(8,128)}, f32[2,128]{1,0:T(2,128)}) custom-call(bf16[16,336,256]{2,1,0:T(8,128)(2,1)} %copy-done, bf16[128,256]{1,0:T(8,128)(2,1)} %q_ref.3, bf16[128,256]{1,0:T(8,128)(2,1)} %it_ref.5, f32[1,192]{1,0:T(1,128)} %get-tuple-element.33.sh_ref), custom_call_target="tpu_custom_call" | custom-call | tf_op jit(solution)/shard_map/batch/pallas_call | solution.py:60
  104.2 24.2 %all-to-all-done.1.parts_ref.refs_1_ = bf16[8,176,256]{2,1,0:T(8,128)(2,1)S(1)} async-done(((bf16[8,176,256]{2,1,0:T(8,128)(2,1)}), bf16[8,176,256]{2,1,0:T(8,128)(2,1)S(1)}, u32[]{:S(2)}, u32[]{:S(2)}) %all-to-all-start.1) | async-done | bytes 720928 | tf_op jit(solution)/shard_map/all_to_all | solution.py:396
  128.4 0.0 copy-start.1
  128.4 0.9 copy-done.1
  129.3 1.8 %total.1 = (f32[1,128]{1,0:T(1,128)}, f32[16,1,128]{2,1,0:T(1,128)}, f32[1,128]{1,0:T(1,128)}) custom-call(bf16[8,176,256]{2,1,0:T(8,128)(2,1)} %copy-done.1, f32[2,128]{1,0:T(2,128)} %get-tuple-element.37.stat_ref), custom_call_target="tpu_custom_call" | custom-call | tf_op jit(solution)/shard_map/total/pallas_call | solution.py:60
  131.1 16.8 %all-to-all-start.2 = ((f32[16,1,128]{2,1,0:T(1,128)}), f32[16,1,128]{2,1,0:T(1,128)S(1)}, u32[]{:S(2)}, u32[]{:S(2)}) async-start(f32[16,1,128]{2,1,0:T(1,128)} %get-tuple-element.39), calls=%async_computation.2 | async-start | bytes 16384 | tf_op jit(solution)/shard_map/all_to_all | solution.py:421
  147.8 2.5 %update.1 = bf16[1024,256]{1,0:T(8,128)(2,1)} custom-call(s32[2]{0:T(128)} %pad_add_fusion.refs_0_, bf16[8,176,256]{2,1,0:T(8,128)(2,1)} %copy-done.1, bf16[1024,256]{1,0:T(8,128)(2,1)} %bitcast.14), custom_call_target="tpu_custom_call" | custom-call | tf_op jit(solution)/shard_map/update/pallas_call | solution.py:60
  150.3 2.0 %queries.1 = f32[128,256]{1,0:T(8,128)} custom-call(bf16[8,176,256]{2,1,0:T(8,128)(2,1)} %copy-done.1, f32[1,128]{1,0:T(1,128)} %get-tuple-element.40.lt_ref, f32[128,256]{1,0:T(8,128)} %get-tuple-element.41.batch_ref, f32[2,128]{1,0:T(2,128)} %get-tuple-element.37.stat_ref, bf16[128,256]{1,0:T(8,128)(2,1)} %it_ref.5), custom_call_target="tpu_custom_call" | custom-call | tf_op jit(solution)/shard_map/queries/pallas_call | solution.py:60
  152.4 0.9 all-to-all-done.2
  153.3 0.0 copy-start.6
  153.3 0.6 copy-done.6
  153.8 3.3 %items.1 = (f32[128,256]{1,0:T(8,128)}, f32[64,256]{1,0:T(8,128)}) custom-call(bf16[16,336,256]{2,1,0:T(8,128)(2,1)} %copy-done, f32[16,128]{1,0:T(8,128)} %bitcast.17, bf16[128,256]{1,0:T(8,128)(2,1)} %q_ref.3, bf16[128,256]{1,0:T(8,128)(2,1)} %it_ref.5, bf16[64,256]{1,0:T(8,128)(2,1)} %ng_ref.1, f32[1,192]{1,0:T(1,128)} %get-tuple-element.33.sh_ref), custom_call_target="tpu_custom_call" | custom-call | tf_op jit(solution)/shard_map/items/pallas_call | solution.py:60
Async XLA Ops:
  5.0 15.1 %copy-start.7 = (bf16[1120,256]{1,0:T(8,128)(2,1)S(1)}, bf16[1120,256]{1,0:T(8,128)(2,1)}, u32[]{:S(2)}) copy-start(bf16[1120,256]{1,0:T(8,128)(2,1)} %get-tuple-element.29) | copy-start | bytes 1720324
  5.0 20.4 %copy-start.2 = (bf16[128,256]{1,0:T(8,128)(2,1)S(1)}, bf16[128,256]{1,0:T(8,128)(2,1)}, u32[]{:S(2)}) copy-start(bf16[128,256]{1,0:T(8,128)(2,1)} %q_ref.3) | copy-start | bytes 196612
  5.0 88.4 %all-to-all-start = ((bf16[16,336,256]{2,1,0:T(8,128)(2,1)}), bf16[16,336,256]{2,1,0:T(8,128)(2,1)S(1)}, u32[]{:S(2)}, u32[]{:S(2)}) async-start(bf16[16,336,256]{2,1,0:T(8,128)(2,1)} %get-tuple-element.30), calls=%async_computation | async-start | bytes 5505024 | tf_op jit(solution)/shard_map/all_to_all | solution.py:379
  15.6 67.5 %collective-permute-start = (bf16[1120,256]{1,0:T(8,128)(2,1)}, bf16[1120,256]{1,0:T(8,128)(2,1)S(1)}, u32[]{:S(2)}, u32[]{:S(2)}) collective-permute-start(bf16[1120,256]{1,0:T(8,128)(2,1)} %get-tuple-element.27), channel_id=1, source_target_pairs={{0,16},{16,0},{32,48},{48,32},{64,80},{80,64},{96,112},{112,96},{1... | collective-permute-start | bytes 1720328 | tf_op jit(solution)/shard_map/ppermute | solution.py:351
  17.5 65.6 %collective-permute-start.1 = (bf16[1120,256]{1,0:T(8,128)(2,1)}, bf16[1120,256]{1,0:T(8,128)(2,1)S(1)}, u32[]{:S(2)}, u32[]{:S(2)}) collective-permute-start(bf16[1120,256]{1,0:T(8,128)(2,1)} %get-tuple-element.28), channel_id=1, source_target_pairs={{0,256},{16,272},{32,288},{48,304},{64,320},{80,336},{96,352},{112... | collective-permute-start | bytes 1720328 | tf_op jit(solution)/shard_map/ppermute | solution.py:351
  20.1 63.0 %collective-permute-start.2 = (bf16[1120,256]{1,0:T(8,128)(2,1)S(1)}, bf16[1120,256]{1,0:T(8,128)(2,1)S(1)}, u32[]{:S(2)}, u32[]{:S(2)}) collective-permute-start(bf16[1120,256]{1,0:T(8,128)(2,1)S(1)} %copy-done.7), channel_id=1, source_target_pairs={{0,272},{16,256},{32,304},{48,288},{64,336},{80,320},{96,368},{112... | collective-permute-start | bytes 1720328 | tf_op jit(solution)/shard_map/ppermute | solution.py:351
  83.1 0.8 copy-start.3
  83.1 1.0 copy-start.4
  83.1 1.2 copy-start.5
  93.5 6.5 %copy-start = (bf16[16,336,256]{2,1,0:T(8,128)(2,1)}, bf16[16,336,256]{2,1,0:T(8,128)(2,1)S(1)}, u32[]{:S(2)}) copy-start(bf16[16,336,256]{2,1,0:T(8,128)(2,1)S(1)} %all-to-all-done.g_ref) | copy-start | bytes 8257540
  93.5 35.0 %all-to-all-start.1 = ((bf16[8,176,256]{2,1,0:T(8,128)(2,1)}), bf16[8,176,256]{2,1,0:T(8,128)(2,1)S(1)}, u32[]{:S(2)}, u32[]{:S(2)}) async-start(bf16[8,176,256]{2,1,0:T(8,128)(2,1)} %memory.1), calls=%async_computation.1 | async-start | bytes 1441792 | tf_op jit(solution)/shard_map/all_to_all | solution.py:396
  128.4 0.9 copy-start.1
  131.1 22.2 %all-to-all-start.2 = ((f32[16,1,128]{2,1,0:T(1,128)}), f32[16,1,128]{2,1,0:T(1,128)S(1)}, u32[]{:S(2)}, u32[]{:S(2)}) async-start(f32[16,1,128]{2,1,0:T(1,128)} %get-tuple-element.39), calls=%async_computation.2 | async-start | bytes 16384 | tf_op jit(solution)/shard_map/all_to_all | solution.py:421
  153.3 0.6 copy-start.6

commit v8 on v6

--- a/solution.py
+++ b/solution.py
@@ -280,7 +280,7 @@
     stat_ref[1:2, :] = jnp.sum(jnp.where(eye(rows), own, 0.0), axis=0, keepdims=True)
 
 
-def total_kernel(parts_ref, stat_ref, total_ref, loss_ref):
+def total_kernel(parts_ref, stat_ref, total_ref, copies_ref, loss_ref):
     rows = total_ref.shape[1]
     shards = parts_ref.shape[0]
     batch = stat_ref[0:1, :]
@@ -293,6 +293,8 @@
         summed = summed + jnp.exp(row - top)
     log_total = top + jnp.log(summed)
     total_ref[...] = log_total
+    for k in range(copies_ref.shape[0]):
+        copies_ref[k] = log_total
     loss_ref[...] = log_total - stat_ref[1:2, :]
 
 
@@ -376,10 +378,12 @@
         ),
         "prepare",
     )
-    gathered = lax.all_to_all(block, "dp", 0, 0, tiled=True)
     z_rows = beside(z_sent, 0, 1)
     y_rows = beside(y_sent, 1, 0)
-    z_rows, queries = lax.optimization_barrier((z_rows, query_vectors))
+    z_rows, y_rows, queries, block = lax.optimization_barrier(
+        (z_rows, y_rows, query_vectors, block)
+    )
+    gathered = lax.all_to_all(block, "dp", 0, 0, tiled=True)
     zy_rows = beside(z_rows, 1, 0)
     memory_blocks = [own_items, mem, z_rows, y_rows, zy_rows]
     arrived = lax.all_gather(queries, "zh", axis=0, tiled=False)
@@ -406,15 +410,17 @@
     parts_back, batch_part, batch_stat = lax.optimization_barrier(
         (parts_back, batch_part, batch_stat)
     )
-    log_total, loss = call(
+    log_total, total_copies, loss = call(
         total_kernel,
         (parts_back, batch_stat),
-        (jax.ShapeDtypeStruct((1, rows), F32), jax.ShapeDtypeStruct((1, rows), F32)),
+        (
+            jax.ShapeDtypeStruct((1, rows), F32),
+            jax.ShapeDtypeStruct((group, 1, rows), F32),
+            jax.ShapeDtypeStruct((1, rows), F32),
+        ),
         "total",
     )
-    group_totals = lax.all_to_all(
-        jnp.broadcast_to(log_total[None], (group, 1, rows)), "dp", 0, 0, tiled=True
-    ).reshape(group, rows)
+    group_totals = lax.all_to_all(total_copies, "dp", 0, 0, tiled=True).reshape(group, rows)
     (query_grad,) = call(
         query_kernel,
         (parts_back, log_total, batch_part, batch_stat, item_vectors),

time: 155 us -> 162 us (1.045)
  waiting for transfers between devices: 53.3 us -> 59 us
  starting transfers between devices: 36 us -> 39.1 us
    ppermute x3, waiting for transfers between devices: 16.8 us -> 22.6 us  [beside(): return lax.ppermute(block, column, route)]
    ppermute x3, starting transfers between devices: 10.3 us -> 12.9 us  [beside(): return lax.ppermute(block, column, route)]
  transfers between devices with their start and end apart: 6 -> 6, of which waited for: 4 -> 4; matrix products, arithmetic and copies ran while one was open for 0% -> 0% of each run, Pallas kernels for 12% -> 11%
where the time goes in v8:
time: 162 us; the launch traced here: 161 us
  waiting for transfers between devices  59 us (36%)
  starting transfers between devices  39.1 us (24%)
  blocking collectives  31.9 us (20%)
  Pallas kernels  26.7 us (16%)
  local copies, waits for them, and re-layouts  3.09 us (2%)
    all_to_all x1, waiting for transfers between devices, local(): parts_back = lax.all_to_all(parts, 'zh', 0, 0, tiled=True)  35.6 us
    all_gather x1, blocking collectives, local(): arrived = lax.all_gather(queries, 'zh', axis=0, tiled=False)  31.9 us
    pallas_call x7, Pallas kernels, call(): pl.pallas_call(kernel, out_shape=out_shape, in_specs=[scalars if operand....  26.7 us
    ppermute x3, waiting for transfers between devices, beside(): return lax.ppermute(block, column, route)  22.6 us
    all_to_all x1, starting transfers between devices, local(): parts_back = lax.all_to_all(parts, 'zh', 0, 0, tiled=True)  13.3 us
    ppermute x3, starting transfers between devices, beside(): return lax.ppermute(block, column, route)  12.9 us
    all_to_all x1, starting transfers between devices, local(): gathered = lax.all_to_all(block, 'dp', 0, 0, tiled=True)  7.32 us
    all_to_all x1, starting transfers between devices, local(): lax.all_to_all(total_copies, 'dp', 0, 0, tiled=True).reshape(group, rows)  5.64 us
  transfers between devices with their start and end apart: 6, of which 4 were waited for; matrix products, arithmetic and copies ran while one was open for 0% of the time, Pallas kernels for 11%

profile of v8, /device:TPU:65, one launch (start us, length us, event | category | flops | bytes accessed | tf_op | source)
XLA Modules:
  0.0 161.0 jit_solution(15012878662884562888)
XLA Ops:
  0.6 0.6 pad_add_fusion.refs_0_
  1.2 3.6 %prepare.1 = (bf16[16,336,256]{2,1,0:T(8,128)(2,1)}, f32[1,192]{1,0:T(1,128)}, bf16[1216,256]{1,0:T(8,128)(2,1)}, bf16[1120,256]{1,0:T(8,128)(2,1)}, bf16[96,256]{1,0:T(8,128)(2,1)}) custom-call(s32[2]{0:T(128)} %pad_add_fusion.refs_0_, bf16[128,256]{1,0:T(8,128)(2,1)} %q_ref.3, bf16[128,256]{1,0:T(8,128)(2,1)} %it_ref.5, bf16[64,256]{1,0:T(8,128)(2,1)} %ng_ref.1, ...), custom_call_target="tpu_custom_call" | custom-call | tf_op jit(solution)/shard_map/prepare/pallas_call | solution.py:60
  4.9 3.5 %collective-permute-start = (bf16[1216,256]{1,0:T(8,128)(2,1)}, bf16[1216,256]{1,0:T(8,128)(2,1)S(1)}, u32[]{:S(2)}, u32[]{:S(2)}) collective-permute-start(bf16[1216,256]{1,0:T(8,128)(2,1)} %get-tuple-element.29), channel_id=1, source_target_pairs={{0,16},{16,0},{32,48},{48,32},{64,80},{80,64},{96,112},{112,96},{1... | collective-permute-start | bytes 1867784 | tf_op jit(solution)/shard_map/ppermute | solution.py:352
  8.4 4.8 %collective-permute-start.1 = (bf16[1120,256]{1,0:T(8,128)(2,1)}, bf16[1120,256]{1,0:T(8,128)(2,1)S(1)}, u32[]{:S(2)}, u32[]{:S(2)}) collective-permute-start(bf16[1120,256]{1,0:T(8,128)(2,1)} %get-tuple-element.30), channel_id=1, source_target_pairs={{0,256},{16,272},{32,288},{48,304},{64,320},{80,336},{96,352},{112... | collective-permute-start | bytes 1720328 | tf_op jit(solution)/shard_map/ppermute | solution.py:352
  13.2 12.3 %collective-permute-done.1.refs_4_ = bf16[1120,256]{1,0:T(8,128)(2,1)S(1)} collective-permute-done((bf16[1120,256]{1,0:T(8,128)(2,1)}, bf16[1120,256]{1,0:T(8,128)(2,1)S(1)}, u32[]{:S(2)}, u32[]{:S(2)}) %collective-permute-start.1) | collective-permute-done | bytes 573472 | tf_op jit(solution)/shard_map/ppermute | solution.py:352
  25.5 0.0 copy-start.5
  25.5 0.0 collective-permute-done.refs_3_
  25.5 0.8 copy-done.5
  26.3 0.0 copy-start.3
  26.3 0.0 copy-start.2
  26.3 7.3 %all-to-all-start = ((bf16[16,336,256]{2,1,0:T(8,128)(2,1)}), bf16[16,336,256]{2,1,0:T(8,128)(2,1)S(1)}, u32[]{:S(2)}, u32[]{:S(2)}) async-start(bf16[16,336,256]{2,1,0:T(8,128)(2,1)} %get-tuple-element.36), calls=%async_computation | async-start | bytes 5505024 | tf_op jit(solution)/shard_map/all_to_all | solution.py:386
  33.7 0.0 copy-done.3
  33.7 4.6 %collective-permute-start.2 = (bf16[1216,256]{1,0:T(8,128)(2,1)S(1)}, bf16[1216,256]{1,0:T(8,128)(2,1)S(1)}, u32[]{:S(2)}, u32[]{:S(2)}) collective-permute-start(bf16[1216,256]{1,0:T(8,128)(2,1)S(1)} %collective-permute-done.refs_3_), channel_id=1, source_target_pairs={{0,256},{16,272},{32,288},{48,304},{64,320},{80,336},{96,352},{112... | collective-permute-start | bytes 1867784 | tf_op jit(solution)/shard_map/ppermute | solution.py:352
  38.2 0.0 copy-done.2
  38.2 31.9 %all-gather = bf16[1024,256]{1,0:T(8,128)(2,1)} all-gather(bf16[128,256]{1,0:T(8,128)(2,1)S(1)} %copy-done.2), channel_id=2, replica_groups=mesh['yh'=2,'zh'=8,'zl'=2,'dp'=16] {'zh'}, dimensions={0}, use_global_device_ids=true | all-gather | bytes 589824 | tf_op jit(solution)/shard_map/all_gather | solution.py:389
  70.1 10.3 %collective-permute-done.2.refs_5_ = bf16[1216,256]{1,0:T(8,128)(2,1)S(1)} collective-permute-done((bf16[1216,256]{1,0:T(8,128)(2,1)S(1)}, bf16[1216,256]{1,0:T(8,128)(2,1)S(1)}, u32[]{:S(2)}, u32[]{:S(2)}) %collective-permute-start.2) | collective-permute-done | bytes 622624 | tf_op jit(solution)/shard_map/ppermute | solution.py:352
  80.3 0.0 copy-start.4
  80.3 0.8 copy-done.4
  81.2 9.2 %memory.1 = bf16[8,176,256]{2,1,0:T(8,128)(2,1)} custom-call(bf16[8,128,256]{2,1,0:T(8,128)(2,1)} %bitcast.15, bf16[96,256]{1,0:T(8,128)(2,1)} %get-tuple-element.33.refs_1_, bf16[1024,256]{1,0:T(8,128)(2,1)} %bitcast.13, bf16[1216,256]{1,0:T(8,128)(2,1)} %copy-done.3, bf16[1120,256]{1,0:T(8,128)(2,1)} %copy-done.5, bf16[1216,256]{1,0:T(8,128)(2,1)} %copy-done.4), custom_call_target="tpu_custom_call" | custom-call | tf_op jit(solution)/shard_map/memory/pallas_call | solution.py:60
  90.3 0.0 all-to-all-done.g_ref
  90.3 0.0 copy-start
  90.3 13.3 %all-to-all-start.1 = ((bf16[8,176,256]{2,1,0:T(8,128)(2,1)}), bf16[8,176,256]{2,1,0:T(8,128)(2,1)S(1)}, u32[]{:S(2)}, u32[]{:S(2)}) async-start(bf16[8,176,256]{2,1,0:T(8,128)(2,1)} %memory.1), calls=%async_computation.1 | async-start | bytes 1441792 | tf_op jit(solution)/shard_map/all_to_all | solution.py:398
  103.6 0.0 copy-done
  103.6 4.3 %batch.1 = (f32[128,256]{1,0:T(8,128)}, f32[2,128]{1,0:T(2,128)}) custom-call(bf16[16,336,256]{2,1,0:T(8,128)(2,1)} %copy-done, bf16[128,256]{1,0:T(8,128)(2,1)} %q_ref.3, bf16[128,256]{1,0:T(8,128)(2,1)} %it_ref.5, f32[1,192]{1,0:T(1,128)} %get-tuple-element.39.sh_ref), custom_call_target="tpu_custom_call" | custom-call | tf_op jit(solution)/shard_map/batch/pallas_call | solution.py:60
  107.9 35.6 %all-to-all-done.1.parts_ref.refs_1_ = bf16[8,176,256]{2,1,0:T(8,128)(2,1)S(1)} async-done(((bf16[8,176,256]{2,1,0:T(8,128)(2,1)}), bf16[8,176,256]{2,1,0:T(8,128)(2,1)S(1)}, u32[]{:S(2)}, u32[]{:S(2)}) %all-to-all-start.1) | async-done | bytes 720928 | tf_op jit(solution)/shard_map/all_to_all | solution.py:398
  143.5 0.0 copy-start.1
  143.5 0.9 copy-done.1
  144.3 1.8 %total.1 = (f32[1,128]{1,0:T(1,128)}, f32[16,1,128]{2,1,0:T(1,128)}, f32[1,128]{1,0:T(1,128)}) custom-call(bf16[8,176,256]{2,1,0:T(8,128)(2,1)} %copy-done.1, f32[2,128]{1,0:T(2,128)} %get-tuple-element.43.stat_ref), custom_call_target="tpu_custom_call" | custom-call | tf_op jit(solution)/shard_map/total/pallas_call | solution.py:60
  146.1 5.6 %all-to-all-start.2 = ((f32[16,1,128]{2,1,0:T(1,128)}), f32[16,1,128]{2,1,0:T(1,128)S(1)}, u32[]{:S(2)}, u32[]{:S(2)}) async-start(f32[16,1,128]{2,1,0:T(1,128)} %get-tuple-element.45), calls=%async_computation.2 | async-start | bytes 16384 | tf_op jit(solution)/shard_map/all_to_all | solution.py:423
  151.7 2.5 %update.1 = bf16[1024,256]{1,0:T(8,128)(2,1)} custom-call(s32[2]{0:T(128)} %pad_add_fusion.refs_0_, bf16[8,176,256]{2,1,0:T(8,128)(2,1)} %copy-done.1, bf16[1024,256]{1,0:T(8,128)(2,1)} %bitcast.14), custom_call_target="tpu_custom_call" | custom-call | tf_op jit(solution)/shard_map/update/pallas_call | solution.py:60
  154.2 2.0 %queries.1 = f32[128,256]{1,0:T(8,128)} custom-call(bf16[8,176,256]{2,1,0:T(8,128)(2,1)} %copy-done.1, f32[1,128]{1,0:T(1,128)} %get-tuple-element.46.lt_ref, f32[128,256]{1,0:T(8,128)} %get-tuple-element.47.batch_ref, f32[2,128]{1,0:T(2,128)} %get-tuple-element.43.stat_ref, bf16[128,256]{1,0:T(8,128)(2,1)} %it_ref.5), custom_call_target="tpu_custom_call" | custom-call | tf_op jit(solution)/shard_map/queries/pallas_call | solution.py:60
  156.3 0.9 all-to-all-done.2
  157.1 0.0 copy-start.6
  157.1 0.6 copy-done.6
  157.7 3.3 %items.1 = (f32[128,256]{1,0:T(8,128)}, f32[64,256]{1,0:T(8,128)}) custom-call(bf16[16,336,256]{2,1,0:T(8,128)(2,1)} %copy-done, f32[16,128]{1,0:T(8,128)} %bitcast.17, bf16[128,256]{1,0:T(8,128)(2,1)} %q_ref.3, bf16[128,256]{1,0:T(8,128)(2,1)} %it_ref.5, bf16[64,256]{1,0:T(8,128)(2,1)} %ng_ref.1, f32[1,192]{1,0:T(1,128)} %get-tuple-element.39.sh_ref), custom_call_target="tpu_custom_call" | custom-call | tf_op jit(solution)/shard_map/items/pallas_call | solution.py:60
Async XLA Ops:
  4.9 20.7 %collective-permute-start = (bf16[1216,256]{1,0:T(8,128)(2,1)}, bf16[1216,256]{1,0:T(8,128)(2,1)S(1)}, u32[]{:S(2)}, u32[]{:S(2)}) collective-permute-start(bf16[1216,256]{1,0:T(8,128)(2,1)} %get-tuple-element.29), channel_id=1, source_target_pairs={{0,16},{16,0},{32,48},{48,32},{64,80},{80,64},{96,112},{112,96},{1... | collective-permute-start | bytes 1867784 | tf_op jit(solution)/shard_map/ppermute | solution.py:352
  8.4 17.1 %collective-permute-start.1 = (bf16[1120,256]{1,0:T(8,128)(2,1)}, bf16[1120,256]{1,0:T(8,128)(2,1)S(1)}, u32[]{:S(2)}, u32[]{:S(2)}) collective-permute-start(bf16[1120,256]{1,0:T(8,128)(2,1)} %get-tuple-element.30), channel_id=1, source_target_pairs={{0,256},{16,272},{32,288},{48,304},{64,320},{80,336},{96,352},{112... | collective-permute-start | bytes 1720328 | tf_op jit(solution)/shard_map/ppermute | solution.py:352
  25.5 0.8 copy-start.5
  26.3 7.3 %copy-start.3 = (bf16[1216,256]{1,0:T(8,128)(2,1)}, bf16[1216,256]{1,0:T(8,128)(2,1)S(1)}, u32[]{:S(2)}) copy-start(bf16[1216,256]{1,0:T(8,128)(2,1)S(1)} %collective-permute-done.refs_3_) | copy-start | bytes 1867780
  26.3 11.9 %copy-start.2 = (bf16[128,256]{1,0:T(8,128)(2,1)S(1)}, bf16[128,256]{1,0:T(8,128)(2,1)}, u32[]{:S(2)}) copy-start(bf16[128,256]{1,0:T(8,128)(2,1)} %q_ref.3) | copy-start | bytes 196612
  26.3 64.0 %all-to-all-start = ((bf16[16,336,256]{2,1,0:T(8,128)(2,1)}), bf16[16,336,256]{2,1,0:T(8,128)(2,1)S(1)}, u32[]{:S(2)}, u32[]{:S(2)}) async-start(bf16[16,336,256]{2,1,0:T(8,128)(2,1)} %get-tuple-element.36), calls=%async_computation | async-start | bytes 5505024 | tf_op jit(solution)/shard_map/all_to_all | solution.py:386
  33.7 46.7 %collective-permute-start.2 = (bf16[1216,256]{1,0:T(8,128)(2,1)S(1)}, bf16[1216,256]{1,0:T(8,128)(2,1)S(1)}, u32[]{:S(2)}, u32[]{:S(2)}) collective-permute-start(bf16[1216,256]{1,0:T(8,128)(2,1)S(1)} %collective-permute-done.refs_3_), channel_id=1, source_target_pairs={{0,256},{16,272},{32,288},{48,304},{64,320},{80,336},{96,352},{112... | collective-permute-start | bytes 1867784 | tf_op jit(solution)/shard_map/ppermute | solution.py:352
  80.3 0.8 copy-start.4
  90.3 13.3 %copy-start = (bf16[16,336,256]{2,1,0:T(8,128)(2,1)}, bf16[16,336,256]{2,1,0:T(8,128)(2,1)S(1)}, u32[]{:S(2)}) copy-start(bf16[16,336,256]{2,1,0:T(8,128)(2,1)S(1)} %all-to-all-done.g_ref) | copy-start | bytes 8257540
  90.3 53.1 %all-to-all-start.1 = ((bf16[8,176,256]{2,1,0:T(8,128)(2,1)}), bf16[8,176,256]{2,1,0:T(8,128)(2,1)S(1)}, u32[]{:S(2)}, u32[]{:S(2)}) async-start(bf16[8,176,256]{2,1,0:T(8,128)(2,1)} %memory.1), calls=%async_computation.1 | async-start | bytes 1441792 | tf_op jit(solution)/shard_map/all_to_all | solution.py:398
  143.5 0.9 copy-start.1
  146.1 11.1 %all-to-all-start.2 = ((f32[16,1,128]{2,1,0:T(1,128)}), f32[16,1,128]{2,1,0:T(1,128)S(1)}, u32[]{:S(2)}, u32[]{:S(2)}) async-start(f32[16,1,128]{2,1,0:T(1,128)} %get-tuple-element.45), calls=%async_computation.2 | async-start | bytes 16384 | tf_op jit(solution)/shard_map/all_to_all | solution.py:423
  157.1 0.6 copy-start.6

commit v9 on v5

--- a/solution.py
+++ b/solution.py
@@ -281,7 +281,7 @@
     stat_ref[1:2, :] = jnp.sum(jnp.where(eye(rows), own, 0.0), axis=0, keepdims=True)
 
 
-def total_kernel(parts_ref, stat_ref, total_ref, loss_ref):
+def total_kernel(parts_ref, stat_ref, total_ref, copies_ref, loss_ref):
     rows = total_ref.shape[1]
     shards = parts_ref.shape[0]
     batch = stat_ref[0:1, :]
@@ -294,6 +294,8 @@
         summed = summed + jnp.exp(row - top)
     log_total = top + jnp.log(summed)
     total_ref[...] = log_total
+    for k in range(copies_ref.shape[0]):
+        copies_ref[k] = log_total
     loss_ref[...] = log_total - stat_ref[1:2, :]
 
 
@@ -395,9 +397,7 @@
     pair_blocks = jnp.stack(near_blocks)
     z_rows = beside(z_sent, 0, 1)
     y_rows = beside(y_sent, 1, 0)
-    copies, z_rows, y_rows, pair_blocks = lax.optimization_barrier(
-        (copies, z_rows, y_rows, pair_blocks)
-    )
+    copies, z_rows, pair_blocks = lax.optimization_barrier((copies, z_rows, pair_blocks))
     zy_rows = beside(z_rows, 1, 0)
     memory_blocks = [own_items, mem, z_rows, y_rows, zy_rows]
     arrived = lax.all_to_all(copies, "zh", 0, 0, tiled=True)
@@ -439,15 +439,17 @@
     parts_back, batch_part, batch_stat = lax.optimization_barrier(
         (parts_back, batch_part, batch_stat)
     )
-    log_total, loss = call(
+    log_total, total_copies, loss = call(
         total_kernel,
         (parts_back, batch_stat),
-        (jax.ShapeDtypeStruct((1, rows), F32), jax.ShapeDtypeStruct((1, rows), F32)),
+        (
+            jax.ShapeDtypeStruct((1, rows), F32),
+            jax.ShapeDtypeStruct((group, 1, rows), F32),
+            jax.ShapeDtypeStruct((1, rows), F32),
+        ),
         "total",
     )
-    group_totals = lax.all_to_all(
-        jnp.broadcast_to(log_total[None], (group, 1, rows)), "dp", 0, 0, tiled=True
-    ).reshape(group, rows)
+    group_totals = lax.all_to_all(total_copies, "dp", 0, 0, tiled=True).reshape(group, rows)
     (query_grad,) = call(
         query_kernel,
         (parts_back, log_total, batch_part, batch_stat, item_vectors),

time: 153 us -> 151 us (0.987)
  the two profiles are of different devices: /device:TPU:33 before, /device:TPU:65 now
where the time goes in v9:
time: 151 us
  starting transfers between devices  63.1 us (42%)
  waiting for transfers between devices  55.2 us (37%)
  Pallas kernels  25.7 us (17%)
  local copies, waits for them, and re-layouts  4.13 us (3%)
  other arithmetic  1.66 us (1%)
    pallas_call x7, Pallas kernels, call(): pl.pallas_call(kernel, out_shape=out_shape, in_specs=[scalars if operand....  25.7 us
    ppermute x3, waiting for transfers between devices, beside(): return lax.ppermute(block, column, route)  22 us
    all_to_all x1, waiting for transfers between devices, local(): parts_back = lax.all_to_all(parts, 'zh', 0, 0, tiled=True)  20.2 us
    all_to_all x1, starting transfers between devices, local(): arrived = lax.all_to_all(copies, 'zh', 0, 0, tiled=True)  13.7 us
    ppermute x4, starting transfers between devices, along(): lax.ppermute(blocks, 'dp', [(i, (i + near * by) % group) for i in range(g...  12.5 us
    all_to_all x1, starting transfers between devices, local(): parts_back = lax.all_to_all(parts, 'zh', 0, 0, tiled=True)  11.5 us
    ppermute x3, starting transfers between devices, beside(): return lax.ppermute(block, column, route)  10.3 us
    ppermute x3, starting transfers between devices, local(): lax.ppermute(block, 'dp', [(i, i ^ k) for i in range(group)])  8.27 us
  transfers between devices with their start and end apart: 13, of which 7 were waited for; matrix products, arithmetic and copies ran while one was open for 1% of the time, Pallas kernels for 6%

profile of v9, /device:TPU:65, one launch (start us, length us, event | category | flops | bytes accessed | tf_op | source)
XLA Modules:
  0.0 150.6 jit_solution(11513898872614405540)
XLA Ops:
  0.6 0.7 pad_add_fusion.refs_0_
  1.3 2.8 %prepare.1 = (bf16[336,256]{1,0:T(8,128)(2,1)}, bf16[8,128,256]{2,1,0:T(8,128)(2,1)}, f32[1,192]{1,0:T(1,128)}, bf16[1216,256]{1,0:T(8,128)(2,1)}, bf16[1120,256]{1,0:T(8,128)(2,1)}, /*index=5*/bf16[96,256]{1,0:T(8,128)(2,1)}) custom-call(s32[3]{0:T(128)} %pad_add_fusion.refs_0_, bf16[128,256]{1,0:T(8,128)(2,1)} %refs_7_.1, bf16[128,256]{1,0:T(8,128)(2,1)} %refs_8_.1, ...), custom_call_target="tpu_custom_call" | custom-call | tf_op jit(solution)/shard_map/prepare/pallas_call | solution.py:60
  4.1 3.5 %collective-permute-start = (bf16[1216,256]{1,0:T(8,128)(2,1)}, bf16[1216,256]{1,0:T(8,128)(2,1)S(1)}, u32[]{:S(2)}, u32[]{:S(2)}) collective-permute-start(bf16[1216,256]{1,0:T(8,128)(2,1)} %get-tuple-element.39), channel_id=1, source_target_pairs={{0,16},{16,0},{32,48},{48,32},{64,80},{80,64},{96,112},{112,96},{1... | collective-permute-start | bytes 1867784 | tf_op jit(solution)/shard_map/ppermute | solution.py:363
  7.6 4.0 %collective-permute-start.3 = (bf16[336,256]{1,0:T(8,128)(2,1)}, bf16[336,256]{1,0:T(8,128)(2,1)S(1)}, u32[]{:S(2)}, u32[]{:S(2)}) collective-permute-start(bf16[336,256]{1,0:T(8,128)(2,1)} %get-tuple-element.40), channel_id=1, source_target_pairs={{0,3},{1,2},{2,1},{3,0},{4,7},{5,6},{6,5},{7,4},{8,11},{9,10},{10,... | collective-permute-start | bytes 516104 | tf_op jit(solution)/shard_map/ppermute | solution.py:395
  11.6 2.1 %collective-permute-start.2 = (bf16[336,256]{1,0:T(8,128)(2,1)}, bf16[336,256]{1,0:T(8,128)(2,1)S(1)}, u32[]{:S(2)}, u32[]{:S(2)}) collective-permute-start(bf16[336,256]{1,0:T(8,128)(2,1)} %get-tuple-element.40), channel_id=1, source_target_pairs={{0,2},{1,3},{2,0},{3,1},{4,6},{5,7},{6,4},{7,5},{8,10},{9,11},{10,... | collective-permute-start | bytes 516104 | tf_op jit(solution)/shard_map/ppermute | solution.py:395
  13.7 2.1 %collective-permute-start.1 = (bf16[336,256]{1,0:T(8,128)(2,1)}, bf16[336,256]{1,0:T(8,128)(2,1)S(1)}, u32[]{:S(2)}, u32[]{:S(2)}) collective-permute-start(bf16[336,256]{1,0:T(8,128)(2,1)} %get-tuple-element.40), channel_id=1, source_target_pairs={{0,1},{1,0},{2,3},{3,2},{4,5},{5,4},{6,7},{7,6},{8,9},{9,8},{10,11... | collective-permute-start | bytes 516104 | tf_op jit(solution)/shard_map/ppermute | solution.py:395
  15.9 1.2 collective-permute-done.3
  17.1 3.4 %collective-permute-done.2 = bf16[336,256]{1,0:T(8,128)(2,1)S(1)} collective-permute-done((bf16[336,256]{1,0:T(8,128)(2,1)}, bf16[336,256]{1,0:T(8,128)(2,1)S(1)}, u32[]{:S(2)}, u32[]{:S(2)}) %collective-permute-start.2) | collective-permute-done | bytes 172064 | tf_op jit(solution)/shard_map/ppermute | solution.py:395
  20.5 0.0 collective-permute-done.1
  20.5 1.0 pad_maximum_fusion.refs_0_.refs_1_
  21.5 0.0 copy-start.1
  21.5 0.0 collective-permute-done.refs_3_
  21.5 0.0 copy-start.7
  21.5 13.7 %all-to-all-start = ((bf16[8,128,256]{2,1,0:T(8,128)(2,1)}), bf16[8,128,256]{2,1,0:T(8,128)(2,1)S(1)}, u32[]{:S(2)}, u32[]{:S(2)}) async-start(bf16[8,128,256]{2,1,0:T(8,128)(2,1)} %get-tuple-element.41), calls=%async_computation | async-start | bytes 1048576 | tf_op jit(solution)/shard_map/all_to_all | solution.py:403
  35.2 4.4 %collective-permute-start.5 = (bf16[4,336,256]{2,1,0:T(8,128)(2,1)S(1)}, bf16[4,336,256]{2,1,0:T(8,128)(2,1)S(1)}, u32[]{:S(2)}, u32[]{:S(2)}) collective-permute-start(bf16[4,336,256]{2,1,0:T(8,128)(2,1)S(1)} %pad_maximum_fusion.refs_0_.refs_1_), channel_id=1, source_target_pairs={{0,12},{1,13},{2,14},{3,15},{4,0},{5,1},{6,2},{7,3},{8,4},{9,5},{1... | collective-permute-start | bytes 2064392 | tf_op jit(solution)/shard_map/ppermute | solution.py:406
  39.6 1.9 %collective-permute-start.4 = (bf16[4,336,256]{2,1,0:T(8,128)(2,1)S(1)}, bf16[4,336,256]{2,1,0:T(8,128)(2,1)S(1)}, u32[]{:S(2)}, u32[]{:S(2)}) collective-permute-start(bf16[4,336,256]{2,1,0:T(8,128)(2,1)S(1)} %pad_maximum_fusion.refs_0_.refs_1_), channel_id=1, source_target_pairs={{0,4},{1,5},{2,6},{3,7},{4,8},{5,9},{6,10},{7,11},{8,12},{9,13},{1... | collective-permute-start | bytes 2064392 | tf_op jit(solution)/shard_map/ppermute | solution.py:406
  41.5 4.8 %collective-permute-start.7 = (bf16[1216,256]{1,0:T(8,128)(2,1)S(1)}, bf16[1216,256]{1,0:T(8,128)(2,1)S(1)}, u32[]{:S(2)}, u32[]{:S(2)}) collective-permute-start(bf16[1216,256]{1,0:T(8,128)(2,1)S(1)} %collective-permute-done.refs_3_), channel_id=1, source_target_pairs={{0,256},{16,272},{32,288},{48,304},{64,320},{80,336},{96,352},{112... | collective-permute-start | bytes 1867784 | tf_op jit(solution)/shard_map/ppermute | solution.py:363
  46.4 2.0 %collective-permute-start.6 = (bf16[1120,256]{1,0:T(8,128)(2,1)}, bf16[1120,256]{1,0:T(8,128)(2,1)S(1)}, u32[]{:S(2)}, u32[]{:S(2)}) collective-permute-start(bf16[1120,256]{1,0:T(8,128)(2,1)} %get-tuple-element.45), channel_id=1, source_target_pairs={{0,256},{16,272},{32,288},{48,304},{64,320},{80,336},{96,352},{112... | collective-permute-start | bytes 1720328 | tf_op jit(solution)/shard_map/ppermute | solution.py:363
  48.3 22.0 %collective-permute-done.6.refs_4_ = bf16[1120,256]{1,0:T(8,128)(2,1)S(1)} collective-permute-done((bf16[1120,256]{1,0:T(8,128)(2,1)}, bf16[1120,256]{1,0:T(8,128)(2,1)S(1)}, u32[]{:S(2)}, u32[]{:S(2)}) %collective-permute-start.6) | collective-permute-done | bytes 573472 | tf_op jit(solution)/shard_map/ppermute | solution.py:363
  70.4 0.0 copy-start.9
  70.4 0.0 collective-permute-done.7.refs_5_
  70.4 0.0 copy-start.8
  70.4 0.0 collective-permute-done.5.refs_4_.refs_5_
  70.4 0.8 copy-done.9
  71.2 0.2 copy-done.8
  71.4 0.0 copy-start.2
  71.4 0.0 collective-permute-done.4.refs_1_.refs_2_
  71.4 0.0 copy-start.3
  71.4 0.0 all-to-all-done.refs_0_
  71.4 0.0 copy-start.4
  71.4 0.0 copy-done.7
  71.5 0.8 copy-done.4
  72.3 9.2 %memory.1 = bf16[8,176,256]{2,1,0:T(8,128)(2,1)} custom-call(bf16[8,128,256]{2,1,0:T(8,128)(2,1)} %copy-done.4, bf16[96,256]{1,0:T(8,128)(2,1)} %get-tuple-element.47.refs_1_, bf16[1024,256]{1,0:T(8,128)(2,1)} %bitcast.17, bf16[1216,256]{1,0:T(8,128)(2,1)} %copy-done.7, bf16[1120,256]{1,0:T(8,128)(2,1)} %copy-done.9, bf16[1216,256]{1,0:T(8,128)(2,1)} %copy-done.8), custom_call_target="tpu_custom_call" | custom-call | tf_op jit(solution)/shard_map/memory/pallas_call | solution.py:60
  81.5 0.0 copy-done.1
  81.5 11.5 %all-to-all-start.1 = ((bf16[8,176,256]{2,1,0:T(8,128)(2,1)}), bf16[8,176,256]{2,1,0:T(8,128)(2,1)S(1)}, u32[]{:S(2)}, u32[]{:S(2)}) async-start(bf16[8,176,256]{2,1,0:T(8,128)(2,1)} %memory.1), calls=%async_computation.1 | async-start | bytes 1441792 | tf_op jit(solution)/shard_map/all_to_all | solution.py:420
  92.9 0.0 copy-done.3
  92.9 0.0 copy-done.2
  93.0 4.3 %collective-permute-start.9 = (bf16[2,336,256]{2,1,0:T(8,128)(2,1)S(1)}, bf16[2,336,256]{2,1,0:T(8,128)(2,1)S(1)}, u32[]{:S(2)}, u32[]{:S(2)}) collective-permute-start(bf16[2,336,256]{2,1,0:T(8,128)(2,1)S(1)} %slice.7), channel_id=1, source_target_pairs={{0,12},{1,13},{2,14},{3,15},{4,0},{5,1},{6,2},{7,3},{8,4},{9,5},{1... | collective-permute-start | bytes 1032200 | tf_op jit(solution)/shard_map/ppermute | solution.py:406
  97.3 1.9 %collective-permute-start.8 = (bf16[2,336,256]{2,1,0:T(8,128)(2,1)S(1)}, bf16[2,336,256]{2,1,0:T(8,128)(2,1)S(1)}, u32[]{:S(2)}, u32[]{:S(2)}) collective-permute-start(bf16[2,336,256]{2,1,0:T(8,128)(2,1)S(1)} %slice.6), channel_id=1, source_target_pairs={{0,4},{1,5},{2,6},{3,7},{4,8},{5,9},{6,10},{7,11},{8,12},{9,13},{1... | collective-permute-start | bytes 1032200 | tf_op jit(solution)/shard_map/ppermute | solution.py:406
  99.2 2.2 %collective-permute-done.9.refs_3_.refs_4_ = bf16[2,336,256]{2,1,0:T(8,128)(2,1)S(1)} collective-permute-done((bf16[2,336,256]{2,1,0:T(8,128)(2,1)S(1)}, bf16[2,336,256]{2,1,0:T(8,128)(2,1)S(1)}, u32[]{:S(2)}, u32[]{:S(2)}) %collective-permute-start.9) | collective-permute-done | bytes 344096 | tf_op jit(solution)/shard_map/ppermute | solution.py:406
  101.5 0.0 copy-start.5
  101.5 5.3 %collective-permute-done.8.refs_2_.refs_3_ = bf16[2,336,256]{2,1,0:T(8,128)(2,1)S(1)} collective-permute-done((bf16[2,336,256]{2,1,0:T(8,128)(2,1)S(1)}, bf16[2,336,256]{2,1,0:T(8,128)(2,1)S(1)}, u32[]{:S(2)}, u32[]{:S(2)}) %collective-permute-start.8) | collective-permute-done | bytes 344096 | tf_op jit(solution)/shard_map/ppermute | solution.py:406
  106.8 0.0 copy-start.6
  106.8 0.0 copy-done.5
  106.8 0.7 copy-done.6
  107.5 4.2 %batch.1 = (f32[128,256]{1,0:T(8,128)}, f32[2,128]{1,0:T(2,128)}) custom-call(bf16[4,336,256]{2,1,0:T(8,128)(2,1)} %copy-done.1, bf16[4,336,256]{2,1,0:T(8,128)(2,1)} %copy-done.3, bf16[2,336,256]{2,1,0:T(8,128)(2,1)} %copy-done.6, bf16[2,336,256]{2,1,0:T(8,128)(2,1)} %copy-done.5, bf16[4,336,256]{2,1,0:T(8,128)(2,1)} %copy-done.2, ...), custom_call_target="tpu_custom_call" | custom-call | tf_op jit(solution)/shard_map/batch/pallas_call | solution.py:60
  111.7 20.2 %all-to-all-done.1.parts_ref.refs_1_ = bf16[8,176,256]{2,1,0:T(8,128)(2,1)S(1)} async-done(((bf16[8,176,256]{2,1,0:T(8,128)(2,1)}), bf16[8,176,256]{2,1,0:T(8,128)(2,1)S(1)}, u32[]{:S(2)}, u32[]{:S(2)}) %all-to-all-start.1) | async-done | bytes 720928 | tf_op jit(solution)/shard_map/all_to_all | solution.py:420
  131.9 0.0 copy-start
  131.9 0.9 copy-done
  132.7 1.8 %total.1 = (f32[1,128]{1,0:T(1,128)}, f32[16,1,128]{2,1,0:T(1,128)}, f32[1,128]{1,0:T(1,128)}) custom-call(bf16[8,176,256]{2,1,0:T(8,128)(2,1)} %copy-done, f32[2,128]{1,0:T(2,128)} %get-tuple-element.61.stat_ref), custom_call_target="tpu_custom_call" | custom-call | tf_op jit(solution)/shard_map/total/pallas_call | solution.py:60
  134.5 6.8 %all-to-all-start.2 = ((f32[16,1,128]{2,1,0:T(1,128)}), f32[16,1,128]{2,1,0:T(1,128)S(1)}, u32[]{:S(2)}, u32[]{:S(2)}) async-start(f32[16,1,128]{2,1,0:T(1,128)} %get-tuple-element.63), calls=%async_computation.2 | async-start | bytes 16384 | tf_op jit(solution)/shard_map/all_to_all | solution.py:452
  141.3 2.5 %update.1 = bf16[1024,256]{1,0:T(8,128)(2,1)} custom-call(s32[3]{0:T(128)} %pad_add_fusion.refs_0_, bf16[8,176,256]{2,1,0:T(8,128)(2,1)} %copy-done, bf16[1024,256]{1,0:T(8,128)(2,1)} %bitcast.18), custom_call_target="tpu_custom_call" | custom-call | tf_op jit(solution)/shard_map/update/pallas_call | solution.py:60
  143.8 2.0 %queries.1 = f32[128,256]{1,0:T(8,128)} custom-call(bf16[8,176,256]{2,1,0:T(8,128)(2,1)} %copy-done, f32[1,128]{1,0:T(1,128)} %get-tuple-element.64.lt_ref, f32[128,256]{1,0:T(8,128)} %get-tuple-element.65.batch_ref, f32[2,128]{1,0:T(2,128)} %get-tuple-element.61.stat_ref, bf16[128,256]{1,0:T(8,128)(2,1)} %refs_8_.1), custom_call_target="tpu_custom_call" | custom-call | tf_op jit(solution)/shard_map/queries/pallas_call | solution.py:60
  145.9 0.9 all-to-all-done.2
  146.8 0.0 copy-start.10
  146.8 0.6 copy-done.10
  147.3 3.3 %items.1 = (f32[128,256]{1,0:T(8,128)}, f32[64,256]{1,0:T(8,128)}) custom-call(s32[3]{0:T(128)} %pad_add_fusion.refs_0_, bf16[4,336,256]{2,1,0:T(8,128)(2,1)} %copy-done.1, bf16[4,336,256]{2,1,0:T(8,128)(2,1)} %copy-done.3, bf16[2,336,256]{2,1,0:T(8,128)(2,1)} %copy-done.6, bf16[2,336,256]{2,1,0:T(8,128)(2,1)} %copy-done.5, bf16[4,336,256]{2,1,0:T(8,128)(2,1)} %copy-done.2, ...), custom_call_target="tpu_custom_call" | custom-call | tf_op jit(solution)/shard_map/items/pallas_call | solution.py:60
  (2 shorter events, 0.0 us)
Async XLA Ops:
  4.1 17.5 %collective-permute-start = (bf16[1216,256]{1,0:T(8,128)(2,1)}, bf16[1216,256]{1,0:T(8,128)(2,1)S(1)}, u32[]{:S(2)}, u32[]{:S(2)}) collective-permute-start(bf16[1216,256]{1,0:T(8,128)(2,1)} %get-tuple-element.39), channel_id=1, source_target_pairs={{0,16},{16,0},{32,48},{48,32},{64,80},{80,64},{96,112},{112,96},{1... | collective-permute-start | bytes 1867784 | tf_op jit(solution)/shard_map/ppermute | solution.py:363
  7.6 9.5 %collective-permute-start.3 = (bf16[336,256]{1,0:T(8,128)(2,1)}, bf16[336,256]{1,0:T(8,128)(2,1)S(1)}, u32[]{:S(2)}, u32[]{:S(2)}) collective-permute-start(bf16[336,256]{1,0:T(8,128)(2,1)} %get-tuple-element.40), channel_id=1, source_target_pairs={{0,3},{1,2},{2,1},{3,0},{4,7},{5,6},{6,5},{7,4},{8,11},{9,10},{10,... | collective-permute-start | bytes 516104 | tf_op jit(solution)/shard_map/ppermute | solution.py:395
  11.6 8.8 %collective-permute-start.2 = (bf16[336,256]{1,0:T(8,128)(2,1)}, bf16[336,256]{1,0:T(8,128)(2,1)S(1)}, u32[]{:S(2)}, u32[]{:S(2)}) collective-permute-start(bf16[336,256]{1,0:T(8,128)(2,1)} %get-tuple-element.40), channel_id=1, source_target_pairs={{0,2},{1,3},{2,0},{3,1},{4,6},{5,7},{6,4},{7,5},{8,10},{9,11},{10,... | collective-permute-start | bytes 516104 | tf_op jit(solution)/shard_map/ppermute | solution.py:395
  13.7 6.7 %collective-permute-start.1 = (bf16[336,256]{1,0:T(8,128)(2,1)}, bf16[336,256]{1,0:T(8,128)(2,1)S(1)}, u32[]{:S(2)}, u32[]{:S(2)}) collective-permute-start(bf16[336,256]{1,0:T(8,128)(2,1)} %get-tuple-element.40), channel_id=1, source_target_pairs={{0,1},{1,0},{2,3},{3,2},{4,5},{5,4},{6,7},{7,6},{8,9},{9,8},{10,11... | collective-permute-start | bytes 516104 | tf_op jit(solution)/shard_map/ppermute | solution.py:395
  21.5 60.0 %copy-start.1 = (bf16[4,336,256]{2,1,0:T(8,128)(2,1)}, bf16[4,336,256]{2,1,0:T(8,128)(2,1)S(1)}, u32[]{:S(2)}) copy-start(bf16[4,336,256]{2,1,0:T(8,128)(2,1)S(1)} %pad_maximum_fusion.refs_0_.refs_1_) | copy-start | bytes 2064388
  21.5 49.9 %copy-start.7 = (bf16[1216,256]{1,0:T(8,128)(2,1)}, bf16[1216,256]{1,0:T(8,128)(2,1)S(1)}, u32[]{:S(2)}) copy-start(bf16[1216,256]{1,0:T(8,128)(2,1)S(1)} %collective-permute-done.refs_3_) | copy-start | bytes 1867780
  21.5 49.9 %all-to-all-start = ((bf16[8,128,256]{2,1,0:T(8,128)(2,1)}), bf16[8,128,256]{2,1,0:T(8,128)(2,1)S(1)}, u32[]{:S(2)}, u32[]{:S(2)}) async-start(bf16[8,128,256]{2,1,0:T(8,128)(2,1)} %get-tuple-element.41), calls=%async_computation | async-start | bytes 1048576 | tf_op jit(solution)/shard_map/all_to_all | solution.py:403
  35.2 35.2 %collective-permute-start.5 = (bf16[4,336,256]{2,1,0:T(8,128)(2,1)S(1)}, bf16[4,336,256]{2,1,0:T(8,128)(2,1)S(1)}, u32[]{:S(2)}, u32[]{:S(2)}) collective-permute-start(bf16[4,336,256]{2,1,0:T(8,128)(2,1)S(1)} %pad_maximum_fusion.refs_0_.refs_1_), channel_id=1, source_target_pairs={{0,12},{1,13},{2,14},{3,15},{4,0},{5,1},{6,2},{7,3},{8,4},{9,5},{1... | collective-permute-start | bytes 2064392 | tf_op jit(solution)/shard_map/ppermute | solution.py:406
  39.6 31.8 %collective-permute-start.4 = (bf16[4,336,256]{2,1,0:T(8,128)(2,1)S(1)}, bf16[4,336,256]{2,1,0:T(8,128)(2,1)S(1)}, u32[]{:S(2)}, u32[]{:S(2)}) collective-permute-start(bf16[4,336,256]{2,1,0:T(8,128)(2,1)S(1)} %pad_maximum_fusion.refs_0_.refs_1_), channel_id=1, source_target_pairs={{0,4},{1,5},{2,6},{3,7},{4,8},{5,9},{6,10},{7,11},{8,12},{9,13},{1... | collective-permute-start | bytes 2064392 | tf_op jit(solution)/shard_map/ppermute | solution.py:406
  41.5 28.8 %collective-permute-start.7 = (bf16[1216,256]{1,0:T(8,128)(2,1)S(1)}, bf16[1216,256]{1,0:T(8,128)(2,1)S(1)}, u32[]{:S(2)}, u32[]{:S(2)}) collective-permute-start(bf16[1216,256]{1,0:T(8,128)(2,1)S(1)} %collective-permute-done.refs_3_), channel_id=1, source_target_pairs={{0,256},{16,272},{32,288},{48,304},{64,320},{80,336},{96,352},{112... | collective-permute-start | bytes 1867784 | tf_op jit(solution)/shard_map/ppermute | solution.py:363
  46.4 24.0 %collective-permute-start.6 = (bf16[1120,256]{1,0:T(8,128)(2,1)}, bf16[1120,256]{1,0:T(8,128)(2,1)S(1)}, u32[]{:S(2)}, u32[]{:S(2)}) collective-permute-start(bf16[1120,256]{1,0:T(8,128)(2,1)} %get-tuple-element.45), channel_id=1, source_target_pairs={{0,256},{16,272},{32,288},{48,304},{64,320},{80,336},{96,352},{112... | collective-permute-start | bytes 1720328 | tf_op jit(solution)/shard_map/ppermute | solution.py:363
  70.4 0.8 copy-start.9
  70.4 1.1 copy-start.8
  71.4 21.5 %copy-start.2 = (bf16[4,336,256]{2,1,0:T(8,128)(2,1)}, bf16[4,336,256]{2,1,0:T(8,128)(2,1)S(1)}, u32[]{:S(2)}) copy-start(bf16[4,336,256]{2,1,0:T(8,128)(2,1)S(1)} %collective-permute-done.5.refs_4_.refs_5_) | copy-start | bytes 2064388
  71.4 21.5 %copy-start.3 = (bf16[4,336,256]{2,1,0:T(8,128)(2,1)}, bf16[4,336,256]{2,1,0:T(8,128)(2,1)S(1)}, u32[]{:S(2)}) copy-start(bf16[4,336,256]{2,1,0:T(8,128)(2,1)S(1)} %collective-permute-done.4.refs_1_.refs_2_) | copy-start | bytes 2064388
  71.4 0.9 copy-start.4
  81.5 50.4 %all-to-all-start.1 = ((bf16[8,176,256]{2,1,0:T(8,128)(2,1)}), bf16[8,176,256]{2,1,0:T(8,128)(2,1)S(1)}, u32[]{:S(2)}, u32[]{:S(2)}) async-start(bf16[8,176,256]{2,1,0:T(8,128)(2,1)} %memory.1), calls=%async_computation.1 | async-start | bytes 1441792 | tf_op jit(solution)/shard_map/all_to_all | solution.py:420
  93.0 8.5 %collective-permute-start.9 = (bf16[2,336,256]{2,1,0:T(8,128)(2,1)S(1)}, bf16[2,336,256]{2,1,0:T(8,128)(2,1)S(1)}, u32[]{:S(2)}, u32[]{:S(2)}) collective-permute-start(bf16[2,336,256]{2,1,0:T(8,128)(2,1)S(1)} %slice.7), channel_id=1, source_target_pairs={{0,12},{1,13},{2,14},{3,15},{4,0},{5,1},{6,2},{7,3},{8,4},{9,5},{1... | collective-permute-start | bytes 1032200 | tf_op jit(solution)/shard_map/ppermute | solution.py:406
  97.3 9.5 %collective-permute-start.8 = (bf16[2,336,256]{2,1,0:T(8,128)(2,1)S(1)}, bf16[2,336,256]{2,1,0:T(8,128)(2,1)S(1)}, u32[]{:S(2)}, u32[]{:S(2)}) collective-permute-start(bf16[2,336,256]{2,1,0:T(8,128)(2,1)S(1)} %slice.6), channel_id=1, source_target_pairs={{0,4},{1,5},{2,6},{3,7},{4,8},{5,9},{6,10},{7,11},{8,12},{9,13},{1... | collective-permute-start | bytes 1032200 | tf_op jit(solution)/shard_map/ppermute | solution.py:406
  101.5 5.3 %copy-start.5 = (bf16[2,336,256]{2,1,0:T(8,128)(2,1)}, bf16[2,336,256]{2,1,0:T(8,128)(2,1)S(1)}, u32[]{:S(2)}) copy-start(bf16[2,336,256]{2,1,0:T(8,128)(2,1)S(1)} %collective-permute-done.9.refs_3_.refs_4_) | copy-start | bytes 1032196
  106.8 0.7 copy-start.6
  131.9 0.9 copy-start
  134.5 12.3 %all-to-all-start.2 = ((f32[16,1,128]{2,1,0:T(1,128)}), f32[16,1,128]{2,1,0:T(1,128)S(1)}, u32[]{:S(2)}, u32[]{:S(2)}) async-start(f32[16,1,128]{2,1,0:T(1,128)} %get-tuple-element.63), calls=%async_computation.2 | async-start | bytes 16384 | tf_op jit(solution)/shard_map/all_to_all | solution.py:452
  146.8 0.6 copy-start.10

commit v10 on v9

--- a/solution.py
+++ b/solution.py
@@ -137,7 +137,7 @@
     z_ref[0:held, :] = mem_ref[...]
     y_ref[0:held, :] = mem_ref[...]
     for c, (ref, at) in enumerate(
-        ((own_ref, 0), (z_ref, held), (y_ref, held), (z_ref, held + each + each // 2))
+        ((own_ref, 0), (z_ref, held + each + each // 2), (y_ref, held), (z_ref, held))
     ):
         some = chosen[c * each : (c + 1) * each, :]
         ref[at : at + each, :] = dot_plain(some, it_ref[...]).astype(BF16)
@@ -198,7 +198,7 @@
     total = span * 2 // 3
     each = total // pairs
     extra = 2 * each
-    sources = ((own_ref, 0), (z_ref, held), (y_ref, held), (zy_ref, held + span))
+    sources = ((own_ref, 0), (z_ref, held + span), (y_ref, held), (zy_ref, held))
     for k in range(0, pairs, 2):
         items, slots = [], []
         for ref, at in sources:
@@ -398,7 +398,7 @@
     z_rows = beside(z_sent, 0, 1)
     y_rows = beside(y_sent, 1, 0)
     copies, z_rows, pair_blocks = lax.optimization_barrier((copies, z_rows, pair_blocks))
-    zy_rows = beside(z_rows, 1, 0)
+    zy_rows = beside(z_rows[: held + span], 1, 0)
     memory_blocks = [own_items, mem, z_rows, y_rows, zy_rows]
     arrived = lax.all_to_all(copies, "zh", 0, 0, tiled=True)
 

time: 151 us -> 150 us (level)
  transfers between devices with their start and end apart: 13 -> 13, of which waited for: 7 -> 8; matrix products, arithmetic and copies ran while one was open for 1% -> 1% of each run, Pallas kernels for 6% -> 6%
where the time goes in v10:
time: 150 us; the launch traced here: 149 us
  starting transfers between devices  63.1 us (42%)
  waiting for transfers between devices  54.3 us (36%)
  Pallas kernels  25.6 us (17%)
  local copies, waits for them, and re-layouts  3.94 us (3%)
  other arithmetic  1.65 us (1%)
    pallas_call x7, Pallas kernels, call(): pl.pallas_call(kernel, out_shape=out_shape, in_specs=[scalars if operand....  25.6 us
    ppermute x3, waiting for transfers between devices, beside(): return lax.ppermute(block, column, route)  21.1 us
    all_to_all x1, waiting for transfers between devices, local(): parts_back = lax.all_to_all(parts, 'zh', 0, 0, tiled=True)  20.1 us
    all_to_all x1, starting transfers between devices, local(): arrived = lax.all_to_all(copies, 'zh', 0, 0, tiled=True)  13.7 us
    ppermute x4, starting transfers between devices, along(): lax.ppermute(blocks, 'dp', [(i, (i + near * by) % group) for i in range(g...  12.5 us
    all_to_all x1, starting transfers between devices, local(): parts_back = lax.all_to_all(parts, 'zh', 0, 0, tiled=True)  11.5 us
    ppermute x3, starting transfers between devices, beside(): return lax.ppermute(block, column, route)  10.3 us
    ppermute x3, starting transfers between devices, local(): lax.ppermute(block, 'dp', [(i, i ^ k) for i in range(group)])  8.27 us
  transfers between devices with their start and end apart: 13, of which 8 were waited for; matrix products, arithmetic and copies ran while one was open for 1% of the time, Pallas kernels for 6%

profile of v10, /device:TPU:65, one launch (start us, length us, event | category | flops | bytes accessed | tf_op | source)
XLA Modules:
  0.0 149.5 jit_solution(6780532454990819587)
XLA Ops:
  0.6 0.6 pad_add_fusion.refs_0_
  1.3 2.8 %prepare.1 = (bf16[336,256]{1,0:T(8,128)(2,1)}, bf16[8,128,256]{2,1,0:T(8,128)(2,1)}, f32[1,192]{1,0:T(1,128)}, bf16[1216,256]{1,0:T(8,128)(2,1)}, bf16[1120,256]{1,0:T(8,128)(2,1)}, /*index=5*/bf16[96,256]{1,0:T(8,128)(2,1)}) custom-call(s32[3]{0:T(128)} %pad_add_fusion.refs_0_, bf16[128,256]{1,0:T(8,128)(2,1)} %refs_7_.1, bf16[128,256]{1,0:T(8,128)(2,1)} %refs_8_.1, ...), custom_call_target="tpu_custom_call" | custom-call | tf_op jit(solution)/shard_map/prepare/pallas_call | solution.py:60
  4.0 3.5 %collective-permute-start = (bf16[1216,256]{1,0:T(8,128)(2,1)}, bf16[1216,256]{1,0:T(8,128)(2,1)S(1)}, u32[]{:S(2)}, u32[]{:S(2)}) collective-permute-start(bf16[1216,256]{1,0:T(8,128)(2,1)} %get-tuple-element.39), channel_id=1, source_target_pairs={{0,16},{16,0},{32,48},{48,32},{64,80},{80,64},{96,112},{112,96},{1... | collective-permute-start | bytes 1867784 | tf_op jit(solution)/shard_map/ppermute | solution.py:363
  7.6 4.0 %collective-permute-start.3 = (bf16[336,256]{1,0:T(8,128)(2,1)}, bf16[336,256]{1,0:T(8,128)(2,1)S(1)}, u32[]{:S(2)}, u32[]{:S(2)}) collective-permute-start(bf16[336,256]{1,0:T(8,128)(2,1)} %get-tuple-element.40), channel_id=1, source_target_pairs={{0,3},{1,2},{2,1},{3,0},{4,7},{5,6},{6,5},{7,4},{8,11},{9,10},{10,... | collective-permute-start | bytes 516104 | tf_op jit(solution)/shard_map/ppermute | solution.py:395
  11.6 2.1 %collective-permute-start.2 = (bf16[336,256]{1,0:T(8,128)(2,1)}, bf16[336,256]{1,0:T(8,128)(2,1)S(1)}, u32[]{:S(2)}, u32[]{:S(2)}) collective-permute-start(bf16[336,256]{1,0:T(8,128)(2,1)} %get-tuple-element.40), channel_id=1, source_target_pairs={{0,2},{1,3},{2,0},{3,1},{4,6},{5,7},{6,4},{7,5},{8,10},{9,11},{10,... | collective-permute-start | bytes 516104 | tf_op jit(solution)/shard_map/ppermute | solution.py:395
  13.7 2.1 %collective-permute-start.1 = (bf16[336,256]{1,0:T(8,128)(2,1)}, bf16[336,256]{1,0:T(8,128)(2,1)S(1)}, u32[]{:S(2)}, u32[]{:S(2)}) collective-permute-start(bf16[336,256]{1,0:T(8,128)(2,1)} %get-tuple-element.40), channel_id=1, source_target_pairs={{0,1},{1,0},{2,3},{3,2},{4,5},{5,4},{6,7},{7,6},{8,9},{9,8},{10,11... | collective-permute-start | bytes 516104 | tf_op jit(solution)/shard_map/ppermute | solution.py:395
  15.9 1.2 collective-permute-done.3
  17.1 3.4 %collective-permute-done.2 = bf16[336,256]{1,0:T(8,128)(2,1)S(1)} collective-permute-done((bf16[336,256]{1,0:T(8,128)(2,1)}, bf16[336,256]{1,0:T(8,128)(2,1)S(1)}, u32[]{:S(2)}, u32[]{:S(2)}) %collective-permute-start.2) | collective-permute-done | bytes 172064 | tf_op jit(solution)/shard_map/ppermute | solution.py:395
  20.5 0.0 collective-permute-done.1
  20.5 1.0 pad_maximum_fusion.refs_0_.refs_1_
  21.5 0.0 copy-start.1
  21.5 0.0 collective-permute-done.refs_3_
  21.5 0.0 copy-start.4
  21.5 13.7 %all-to-all-start = ((bf16[8,128,256]{2,1,0:T(8,128)(2,1)}), bf16[8,128,256]{2,1,0:T(8,128)(2,1)S(1)}, u32[]{:S(2)}, u32[]{:S(2)}) async-start(bf16[8,128,256]{2,1,0:T(8,128)(2,1)} %get-tuple-element.41), calls=%async_computation | async-start | bytes 1048576 | tf_op jit(solution)/shard_map/all_to_all | solution.py:403
  35.2 4.4 %collective-permute-start.5 = (bf16[4,336,256]{2,1,0:T(8,128)(2,1)S(1)}, bf16[4,336,256]{2,1,0:T(8,128)(2,1)S(1)}, u32[]{:S(2)}, u32[]{:S(2)}) collective-permute-start(bf16[4,336,256]{2,1,0:T(8,128)(2,1)S(1)} %pad_maximum_fusion.refs_0_.refs_1_), channel_id=1, source_target_pairs={{0,12},{1,13},{2,14},{3,15},{4,0},{5,1},{6,2},{7,3},{8,4},{9,5},{1... | collective-permute-start | bytes 2064392 | tf_op jit(solution)/shard_map/ppermute | solution.py:406
  39.6 1.9 %collective-permute-start.4 = (bf16[4,336,256]{2,1,0:T(8,128)(2,1)S(1)}, bf16[4,336,256]{2,1,0:T(8,128)(2,1)S(1)}, u32[]{:S(2)}, u32[]{:S(2)}) collective-permute-start(bf16[4,336,256]{2,1,0:T(8,128)(2,1)S(1)} %pad_maximum_fusion.refs_0_.refs_1_), channel_id=1, source_target_pairs={{0,4},{1,5},{2,6},{3,7},{4,8},{5,9},{6,10},{7,11},{8,12},{9,13},{1... | collective-permute-start | bytes 2064392 | tf_op jit(solution)/shard_map/ppermute | solution.py:406
  41.5 4.8 %collective-permute-start.6 = (bf16[1120,256]{1,0:T(8,128)(2,1)}, bf16[1120,256]{1,0:T(8,128)(2,1)S(1)}, u32[]{:S(2)}, u32[]{:S(2)}) collective-permute-start(bf16[1120,256]{1,0:T(8,128)(2,1)} %get-tuple-element.45), channel_id=1, source_target_pairs={{0,256},{16,272},{32,288},{48,304},{64,320},{80,336},{96,352},{112... | collective-permute-start | bytes 1720328 | tf_op jit(solution)/shard_map/ppermute | solution.py:363
  46.4 0.0 copy-done.1
  46.4 0.0 copy-done.4
  46.4 2.0 %collective-permute-start.7 = (bf16[1120,256]{1,0:T(8,128)(2,1)S(1)}, bf16[1120,256]{1,0:T(8,128)(2,1)S(1)}, u32[]{:S(2)}, u32[]{:S(2)}) collective-permute-start(bf16[1120,256]{1,0:T(8,128)(2,1)S(1)} %slice.9), channel_id=1, source_target_pairs={{0,256},{16,272},{32,288},{48,304},{64,320},{80,336},{96,352},{112... | collective-permute-start | bytes 1720328 | tf_op jit(solution)/shard_map/ppermute | solution.py:363
  48.4 8.8 %collective-permute-done.6.refs_4_ = bf16[1120,256]{1,0:T(8,128)(2,1)S(1)} collective-permute-done((bf16[1120,256]{1,0:T(8,128)(2,1)}, bf16[1120,256]{1,0:T(8,128)(2,1)S(1)}, u32[]{:S(2)}, u32[]{:S(2)}) %collective-permute-start.6) | collective-permute-done | bytes 573472 | tf_op jit(solution)/shard_map/ppermute | solution.py:363
  57.2 0.0 copy-start.8
  57.2 12.3 %collective-permute-done.7.refs_5_ = bf16[1120,256]{1,0:T(8,128)(2,1)S(1)} collective-permute-done((bf16[1120,256]{1,0:T(8,128)(2,1)S(1)}, bf16[1120,256]{1,0:T(8,128)(2,1)S(1)}, u32[]{:S(2)}, u32[]{:S(2)}) %collective-permute-start.7) | collective-permute-done | bytes 573472 | tf_op jit(solution)/shard_map/ppermute | solution.py:363
  69.5 0.0 copy-start.9
  69.5 0.0 collective-permute-done.5.refs_4_.refs_5_
  69.5 0.0 copy-done.8
  69.5 0.8 copy-done.9
  70.3 0.0 copy-start.2
  70.3 0.0 collective-permute-done.4.refs_1_.refs_2_
  70.3 0.0 copy-start.3
  70.3 0.0 all-to-all-done.refs_0_
  70.3 0.0 copy-start.5
  70.3 0.8 copy-done.5
  71.2 9.2 %memory.1 = bf16[8,176,256]{2,1,0:T(8,128)(2,1)} custom-call(bf16[8,128,256]{2,1,0:T(8,128)(2,1)} %copy-done.5, bf16[96,256]{1,0:T(8,128)(2,1)} %get-tuple-element.47.refs_1_, bf16[1024,256]{1,0:T(8,128)(2,1)} %bitcast.17, bf16[1216,256]{1,0:T(8,128)(2,1)} %copy-done.4, bf16[1120,256]{1,0:T(8,128)(2,1)} %copy-done.8, bf16[1120,256]{1,0:T(8,128)(2,1)} %copy-done.9), custom_call_target="tpu_custom_call" | custom-call | tf_op jit(solution)/shard_map/memory/pallas_call | solution.py:60
  80.3 11.5 %all-to-all-start.1 = ((bf16[8,176,256]{2,1,0:T(8,128)(2,1)}), bf16[8,176,256]{2,1,0:T(8,128)(2,1)S(1)}, u32[]{:S(2)}, u32[]{:S(2)}) async-start(bf16[8,176,256]{2,1,0:T(8,128)(2,1)} %memory.1), calls=%async_computation.1 | async-start | bytes 1441792 | tf_op jit(solution)/shard_map/all_to_all | solution.py:420
  91.8 0.0 copy-done.3
  91.8 0.0 copy-done.2
  91.9 4.3 %collective-permute-start.9 = (bf16[2,336,256]{2,1,0:T(8,128)(2,1)S(1)}, bf16[2,336,256]{2,1,0:T(8,128)(2,1)S(1)}, u32[]{:S(2)}, u32[]{:S(2)}) collective-permute-start(bf16[2,336,256]{2,1,0:T(8,128)(2,1)S(1)} %slice.11), channel_id=1, source_target_pairs={{0,12},{1,13},{2,14},{3,15},{4,0},{5,1},{6,2},{7,3},{8,4},{9,5},{1... | collective-permute-start | bytes 1032200 | tf_op jit(solution)/shard_map/ppermute | solution.py:406
  96.2 1.9 %collective-permute-start.8 = (bf16[2,336,256]{2,1,0:T(8,128)(2,1)S(1)}, bf16[2,336,256]{2,1,0:T(8,128)(2,1)S(1)}, u32[]{:S(2)}, u32[]{:S(2)}) collective-permute-start(bf16[2,336,256]{2,1,0:T(8,128)(2,1)S(1)} %slice.10), channel_id=1, source_target_pairs={{0,4},{1,5},{2,6},{3,7},{4,8},{5,9},{6,10},{7,11},{8,12},{9,13},{1... | collective-permute-start | bytes 1032200 | tf_op jit(solution)/shard_map/ppermute | solution.py:406
  98.1 2.2 %collective-permute-done.9.refs_3_.refs_4_ = bf16[2,336,256]{2,1,0:T(8,128)(2,1)S(1)} collective-permute-done((bf16[2,336,256]{2,1,0:T(8,128)(2,1)S(1)}, bf16[2,336,256]{2,1,0:T(8,128)(2,1)S(1)}, u32[]{:S(2)}, u32[]{:S(2)}) %collective-permute-start.9) | collective-permute-done | bytes 344096 | tf_op jit(solution)/shard_map/ppermute | solution.py:406
  100.3 0.0 copy-start.6
  100.3 5.3 %collective-permute-done.8.refs_2_.refs_3_ = bf16[2,336,256]{2,1,0:T(8,128)(2,1)S(1)} collective-permute-done((bf16[2,336,256]{2,1,0:T(8,128)(2,1)S(1)}, bf16[2,336,256]{2,1,0:T(8,128)(2,1)S(1)}, u32[]{:S(2)}, u32[]{:S(2)}) %collective-permute-start.8) | collective-permute-done | bytes 344096 | tf_op jit(solution)/shard_map/ppermute | solution.py:406
  105.7 0.0 copy-start.7
  105.7 0.0 copy-done.6
  105.7 0.7 copy-done.7
  106.4 4.2 %batch.1 = (f32[128,256]{1,0:T(8,128)}, f32[2,128]{1,0:T(2,128)}) custom-call(bf16[4,336,256]{2,1,0:T(8,128)(2,1)} %copy-done.1, bf16[4,336,256]{2,1,0:T(8,128)(2,1)} %copy-done.3, bf16[2,336,256]{2,1,0:T(8,128)(2,1)} %copy-done.7, bf16[2,336,256]{2,1,0:T(8,128)(2,1)} %copy-done.6, bf16[4,336,256]{2,1,0:T(8,128)(2,1)} %copy-done.2, ...), custom_call_target="tpu_custom_call" | custom-call | tf_op jit(solution)/shard_map/batch/pallas_call | solution.py:60
  110.6 20.1 %all-to-all-done.1.parts_ref.refs_1_ = bf16[8,176,256]{2,1,0:T(8,128)(2,1)S(1)} async-done(((bf16[8,176,256]{2,1,0:T(8,128)(2,1)}), bf16[8,176,256]{2,1,0:T(8,128)(2,1)S(1)}, u32[]{:S(2)}, u32[]{:S(2)}) %all-to-all-start.1) | async-done | bytes 720928 | tf_op jit(solution)/shard_map/all_to_all | solution.py:420
  130.7 0.0 copy-start
  130.7 0.9 copy-done
  131.6 1.8 %total.1 = (f32[1,128]{1,0:T(1,128)}, f32[16,1,128]{2,1,0:T(1,128)}, f32[1,128]{1,0:T(1,128)}) custom-call(bf16[8,176,256]{2,1,0:T(8,128)(2,1)} %copy-done, f32[2,128]{1,0:T(2,128)} %get-tuple-element.61.stat_ref), custom_call_target="tpu_custom_call" | custom-call | tf_op jit(solution)/shard_map/total/pallas_call | solution.py:60
  133.3 6.9 %all-to-all-start.2 = ((f32[16,1,128]{2,1,0:T(1,128)}), f32[16,1,128]{2,1,0:T(1,128)S(1)}, u32[]{:S(2)}, u32[]{:S(2)}) async-start(f32[16,1,128]{2,1,0:T(1,128)} %get-tuple-element.63), calls=%async_computation.2 | async-start | bytes 16384 | tf_op jit(solution)/shard_map/all_to_all | solution.py:452
  140.2 2.5 %update.1 = bf16[1024,256]{1,0:T(8,128)(2,1)} custom-call(s32[3]{0:T(128)} %pad_add_fusion.refs_0_, bf16[8,176,256]{2,1,0:T(8,128)(2,1)} %copy-done, bf16[1024,256]{1,0:T(8,128)(2,1)} %bitcast.18), custom_call_target="tpu_custom_call" | custom-call | tf_op jit(solution)/shard_map/update/pallas_call | solution.py:60
  142.7 2.0 %queries.1 = f32[128,256]{1,0:T(8,128)} custom-call(bf16[8,176,256]{2,1,0:T(8,128)(2,1)} %copy-done, f32[1,128]{1,0:T(1,128)} %get-tuple-element.64.lt_ref, f32[128,256]{1,0:T(8,128)} %get-tuple-element.65.batch_ref, f32[2,128]{1,0:T(2,128)} %get-tuple-element.61.stat_ref, bf16[128,256]{1,0:T(8,128)(2,1)} %refs_8_.1), custom_call_target="tpu_custom_call" | custom-call | tf_op jit(solution)/shard_map/queries/pallas_call | solution.py:60
  144.7 0.9 all-to-all-done.2
  145.6 0.0 copy-start.10
  145.6 0.6 copy-done.10
  146.2 3.2 %items.1 = (f32[128,256]{1,0:T(8,128)}, f32[64,256]{1,0:T(8,128)}) custom-call(s32[3]{0:T(128)} %pad_add_fusion.refs_0_, bf16[4,336,256]{2,1,0:T(8,128)(2,1)} %copy-done.1, bf16[4,336,256]{2,1,0:T(8,128)(2,1)} %copy-done.3, bf16[2,336,256]{2,1,0:T(8,128)(2,1)} %copy-done.7, bf16[2,336,256]{2,1,0:T(8,128)(2,1)} %copy-done.6, bf16[4,336,256]{2,1,0:T(8,128)(2,1)} %copy-done.2, ...), custom_call_target="tpu_custom_call" | custom-call | tf_op jit(solution)/shard_map/items/pallas_call | solution.py:60
  (3 shorter events, 0.1 us)
Async XLA Ops:
  4.0 17.5 %collective-permute-start = (bf16[1216,256]{1,0:T(8,128)(2,1)}, bf16[1216,256]{1,0:T(8,128)(2,1)S(1)}, u32[]{:S(2)}, u32[]{:S(2)}) collective-permute-start(bf16[1216,256]{1,0:T(8,128)(2,1)} %get-tuple-element.39), channel_id=1, source_target_pairs={{0,16},{16,0},{32,48},{48,32},{64,80},{80,64},{96,112},{112,96},{1... | collective-permute-start | bytes 1867784 | tf_op jit(solution)/shard_map/ppermute | solution.py:363
  7.6 9.5 %collective-permute-start.3 = (bf16[336,256]{1,0:T(8,128)(2,1)}, bf16[336,256]{1,0:T(8,128)(2,1)S(1)}, u32[]{:S(2)}, u32[]{:S(2)}) collective-permute-start(bf16[336,256]{1,0:T(8,128)(2,1)} %get-tuple-element.40), channel_id=1, source_target_pairs={{0,3},{1,2},{2,1},{3,0},{4,7},{5,6},{6,5},{7,4},{8,11},{9,10},{10,... | collective-permute-start | bytes 516104 | tf_op jit(solution)/shard_map/ppermute | solution.py:395
  11.6 8.8 %collective-permute-start.2 = (bf16[336,256]{1,0:T(8,128)(2,1)}, bf16[336,256]{1,0:T(8,128)(2,1)S(1)}, u32[]{:S(2)}, u32[]{:S(2)}) collective-permute-start(bf16[336,256]{1,0:T(8,128)(2,1)} %get-tuple-element.40), channel_id=1, source_target_pairs={{0,2},{1,3},{2,0},{3,1},{4,6},{5,7},{6,4},{7,5},{8,10},{9,11},{10,... | collective-permute-start | bytes 516104 | tf_op jit(solution)/shard_map/ppermute | solution.py:395
  13.7 6.7 %collective-permute-start.1 = (bf16[336,256]{1,0:T(8,128)(2,1)}, bf16[336,256]{1,0:T(8,128)(2,1)S(1)}, u32[]{:S(2)}, u32[]{:S(2)}) collective-permute-start(bf16[336,256]{1,0:T(8,128)(2,1)} %get-tuple-element.40), channel_id=1, source_target_pairs={{0,1},{1,0},{2,3},{3,2},{4,5},{5,4},{6,7},{7,6},{8,9},{9,8},{10,11... | collective-permute-start | bytes 516104 | tf_op jit(solution)/shard_map/ppermute | solution.py:395
  21.5 24.9 %copy-start.1 = (bf16[4,336,256]{2,1,0:T(8,128)(2,1)}, bf16[4,336,256]{2,1,0:T(8,128)(2,1)S(1)}, u32[]{:S(2)}) copy-start(bf16[4,336,256]{2,1,0:T(8,128)(2,1)S(1)} %pad_maximum_fusion.refs_0_.refs_1_) | copy-start | bytes 2064388
  21.5 24.9 %copy-start.4 = (bf16[1216,256]{1,0:T(8,128)(2,1)}, bf16[1216,256]{1,0:T(8,128)(2,1)S(1)}, u32[]{:S(2)}) copy-start(bf16[1216,256]{1,0:T(8,128)(2,1)S(1)} %collective-permute-done.refs_3_) | copy-start | bytes 1867780
  21.5 48.8 %all-to-all-start = ((bf16[8,128,256]{2,1,0:T(8,128)(2,1)}), bf16[8,128,256]{2,1,0:T(8,128)(2,1)S(1)}, u32[]{:S(2)}, u32[]{:S(2)}) async-start(bf16[8,128,256]{2,1,0:T(8,128)(2,1)} %get-tuple-element.41), calls=%async_computation | async-start | bytes 1048576 | tf_op jit(solution)/shard_map/all_to_all | solution.py:403
  35.2 34.3 %collective-permute-start.5 = (bf16[4,336,256]{2,1,0:T(8,128)(2,1)S(1)}, bf16[4,336,256]{2,1,0:T(8,128)(2,1)S(1)}, u32[]{:S(2)}, u32[]{:S(2)}) collective-permute-start(bf16[4,336,256]{2,1,0:T(8,128)(2,1)S(1)} %pad_maximum_fusion.refs_0_.refs_1_), channel_id=1, source_target_pairs={{0,12},{1,13},{2,14},{3,15},{4,0},{5,1},{6,2},{7,3},{8,4},{9,5},{1... | collective-permute-start | bytes 2064392 | tf_op jit(solution)/shard_map/ppermute | solution.py:406
  39.6 30.7 %collective-permute-start.4 = (bf16[4,336,256]{2,1,0:T(8,128)(2,1)S(1)}, bf16[4,336,256]{2,1,0:T(8,128)(2,1)S(1)}, u32[]{:S(2)}, u32[]{:S(2)}) collective-permute-start(bf16[4,336,256]{2,1,0:T(8,128)(2,1)S(1)} %pad_maximum_fusion.refs_0_.refs_1_), channel_id=1, source_target_pairs={{0,4},{1,5},{2,6},{3,7},{4,8},{5,9},{6,10},{7,11},{8,12},{9,13},{1... | collective-permute-start | bytes 2064392 | tf_op jit(solution)/shard_map/ppermute | solution.py:406
  41.5 15.7 %collective-permute-start.6 = (bf16[1120,256]{1,0:T(8,128)(2,1)}, bf16[1120,256]{1,0:T(8,128)(2,1)S(1)}, u32[]{:S(2)}, u32[]{:S(2)}) collective-permute-start(bf16[1120,256]{1,0:T(8,128)(2,1)} %get-tuple-element.45), channel_id=1, source_target_pairs={{0,256},{16,272},{32,288},{48,304},{64,320},{80,336},{96,352},{112... | collective-permute-start | bytes 1720328 | tf_op jit(solution)/shard_map/ppermute | solution.py:363
  46.4 23.1 %collective-permute-start.7 = (bf16[1120,256]{1,0:T(8,128)(2,1)S(1)}, bf16[1120,256]{1,0:T(8,128)(2,1)S(1)}, u32[]{:S(2)}, u32[]{:S(2)}) collective-permute-start(bf16[1120,256]{1,0:T(8,128)(2,1)S(1)} %slice.9), channel_id=1, source_target_pairs={{0,256},{16,272},{32,288},{48,304},{64,320},{80,336},{96,352},{112... | collective-permute-start | bytes 1720328 | tf_op jit(solution)/shard_map/ppermute | solution.py:363
  57.2 12.3 %copy-start.8 = (bf16[1120,256]{1,0:T(8,128)(2,1)}, bf16[1120,256]{1,0:T(8,128)(2,1)S(1)}, u32[]{:S(2)}) copy-start(bf16[1120,256]{1,0:T(8,128)(2,1)S(1)} %collective-permute-done.6.refs_4_) | copy-start | bytes 1720324
  69.5 0.8 copy-start.9
  70.3 21.5 %copy-start.2 = (bf16[4,336,256]{2,1,0:T(8,128)(2,1)}, bf16[4,336,256]{2,1,0:T(8,128)(2,1)S(1)}, u32[]{:S(2)}) copy-start(bf16[4,336,256]{2,1,0:T(8,128)(2,1)S(1)} %collective-permute-done.5.refs_4_.refs_5_) | copy-start | bytes 2064388
  70.3 21.5 %copy-start.3 = (bf16[4,336,256]{2,1,0:T(8,128)(2,1)}, bf16[4,336,256]{2,1,0:T(8,128)(2,1)S(1)}, u32[]{:S(2)}) copy-start(bf16[4,336,256]{2,1,0:T(8,128)(2,1)S(1)} %collective-permute-done.4.refs_1_.refs_2_) | copy-start | bytes 2064388
  70.3 0.9 copy-start.5
  80.3 50.4 %all-to-all-start.1 = ((bf16[8,176,256]{2,1,0:T(8,128)(2,1)}), bf16[8,176,256]{2,1,0:T(8,128)(2,1)S(1)}, u32[]{:S(2)}, u32[]{:S(2)}) async-start(bf16[8,176,256]{2,1,0:T(8,128)(2,1)} %memory.1), calls=%async_computation.1 | async-start | bytes 1441792 | tf_op jit(solution)/shard_map/all_to_all | solution.py:420
  91.9 8.5 %collective-permute-start.9 = (bf16[2,336,256]{2,1,0:T(8,128)(2,1)S(1)}, bf16[2,336,256]{2,1,0:T(8,128)(2,1)S(1)}, u32[]{:S(2)}, u32[]{:S(2)}) collective-permute-start(bf16[2,336,256]{2,1,0:T(8,128)(2,1)S(1)} %slice.11), channel_id=1, source_target_pairs={{0,12},{1,13},{2,14},{3,15},{4,0},{5,1},{6,2},{7,3},{8,4},{9,5},{1... | collective-permute-start | bytes 1032200 | tf_op jit(solution)/shard_map/ppermute | solution.py:406
  96.2 9.5 %collective-permute-start.8 = (bf16[2,336,256]{2,1,0:T(8,128)(2,1)S(1)}, bf16[2,336,256]{2,1,0:T(8,128)(2,1)S(1)}, u32[]{:S(2)}, u32[]{:S(2)}) collective-permute-start(bf16[2,336,256]{2,1,0:T(8,128)(2,1)S(1)} %slice.10), channel_id=1, source_target_pairs={{0,4},{1,5},{2,6},{3,7},{4,8},{5,9},{6,10},{7,11},{8,12},{9,13},{1... | collective-permute-start | bytes 1032200 | tf_op jit(solution)/shard_map/ppermute | solution.py:406
  100.3 5.3 %copy-start.6 = (bf16[2,336,256]{2,1,0:T(8,128)(2,1)}, bf16[2,336,256]{2,1,0:T(8,128)(2,1)S(1)}, u32[]{:S(2)}) copy-start(bf16[2,336,256]{2,1,0:T(8,128)(2,1)S(1)} %collective-permute-done.9.refs_3_.refs_4_) | copy-start | bytes 1032196
  105.7 0.7 copy-start.7
  130.7 0.9 copy-start
  133.3 12.3 %all-to-all-start.2 = ((f32[16,1,128]{2,1,0:T(1,128)}), f32[16,1,128]{2,1,0:T(1,128)S(1)}, u32[]{:S(2)}, u32[]{:S(2)}) async-start(f32[16,1,128]{2,1,0:T(1,128)} %get-tuple-element.63), calls=%async_computation.2 | async-start | bytes 16384 | tf_op jit(solution)/shard_map/all_to_all | solution.py:452
  145.6 0.6 copy-start.10
